TPU v7x, 32 devices: a whole 2x2x4 slice. The times are simulated.
32 devices in a mesh: groups: 2 (over x), dp: 16 (over z, y, core).
Axes of the slice: x: 2, y: 2, z: 4, core: 2. Of those that a mesh axis runs over, the one named last changes fastest.
Arguments:
- tokens: bfloat16 [4096, 8192], P(('groups', 'dp')), parts along dimension 0, may hold values from -6 to 6
- value_weight_matrix: bfloat16 [8192, 1024], P('dp'), may hold values from -0.0625 to 0.0625
- adapter_down_weight: bfloat16 [64, 64, 8192], P(None, None, 'dp'), may hold values from -0.0625 to 0.0625
- adapter_up_weight: bfloat16 [64, 64, 1024], P(None, None, 'dp'), may hold values from -0.75 to 0.75
- adapter_of_block: int32 [32], P('groups'), parts along dimension 0, may hold values from 0 to 63
- block_live_length: int32 [32], P(('groups', 'dp')), parts along dimension 0, may hold values from 1 to 128
Outputs:
- values: bfloat16 [4096, 1024], P(('groups', 'dp')), parts along dimension 0
There are 2 independent parts, one for each index of `groups`. A program takes and returns all parts, laid end to end along the dimension named above; an argument that names none is the same for every part. Nothing has to cross between parts.
All inputs are finite; a program needn't handle non-finite values.
Results may differ from a plain program's by a relative error of at most 0.0034.
Values may be sent and summed in bfloat16 or wider, within the bound.
No kernel may reach another device: no remote copies, remote signals or barrier semaphores. Data moves between devices by JAX's collectives and lax.ppermute only.
A program may use at most 128 MiB of HBM per device.

v0:
```python
import jax
import jax.numpy as jnp
from jax import lax
from jax.sharding import PartitionSpec as P

BLOCK = 128


ADAPTER_SCALE = 0.5


def per_device(
    tokens,
    value_weight_matrix,
    adapter_down_weight,
    adapter_up_weight,
    adapter_of_block,
    block_live_length,
):
    peer_count = lax.axis_size("dp")
    blocks_here = tokens.shape[0] // BLOCK
    lookup_index = adapter_of_block.reshape(peer_count, blocks_here).T
    up_outgoing = jnp.take(adapter_up_weight, lookup_index, axis=0)
    up_full = lax.all_to_all(up_outgoing, "dp", split_axis=1, concat_axis=3, tiled=True)
    features = lax.all_to_all(tokens, "dp", split_axis=1, concat_axis=0, tiled=True)
    feature_blocks = features.reshape(-1, BLOCK, features.shape[1])
    lookup_weights = jnp.take(adapter_down_weight, adapter_of_block, axis=0)
    narrowed_rows = lax.psum_scatter(
        jnp.einsum(
            "bnd,brd->bnr", feature_blocks, lookup_weights, preferred_element_type=jnp.float32
        ),
        "dp",
        scatter_dimension=0,
        tiled=True,
    )
    reduced_rank_output = (narrowed_rows * ADAPTER_SCALE).astype(jnp.bfloat16)
    change_rows = jnp.einsum(
        "bnr,brv->bnv", reduced_rank_output, up_full[:, 0], preferred_element_type=jnp.float32
    )
    change_rows = change_rows.reshape(tokens.shape[0], -1)
    base_out = jnp.dot(
        tokens,
        lax.all_gather(value_weight_matrix, "dp", axis=0, tiled=True),
        preferred_element_type=jnp.float32,
    )
    live_rows = jnp.arange(BLOCK, dtype=jnp.int32)[None, :] < block_live_length[:, None]
    return jnp.where(live_rows.reshape(-1, 1), base_out + change_rows, 0.0).astype(jnp.bfloat16)


def solution(mesh):
    in_specs = (
        P(("groups", "dp"), None),
        P("dp", None),
        P(None, None, "dp"),
        P(None, None, "dp"),
        P("groups"),
        P(("groups", "dp")),
    )
    out_specs = P(("groups", "dp"), None)
    return jax.shard_map(
        per_device, mesh=mesh, in_specs=in_specs, out_specs=out_specs, check_vma=False
    )
```

profile of v0, /device:TPU:0, one launch (start us, length us, event | category | flops | bytes accessed | tf_op | source)
XLA Modules:
  0.0 244.2 jit_solution(15562987998203126120)
XLA Ops:
  6.5 0.0 copy-start
  6.5 0.0 copy-start.1
  6.5 0.0 all-gather.2.cloned.1.call-start
  6.5 0.7 all-gather.2.cloned.1.call-update
  7.3 0.9 compare_select_fusion
  8.1 0.0 copy-done
  8.2 0.6 gather_fusion.1
  8.8 0.7 compare_and_fusion
  9.4 0.8 fusion.15
  10.2 1.8 reshape.72
  12.1 7.4 %all-to-all-start.1 = ((bf16[16,2,2048]{2,1,0:T(2,128)(2,1)}), bf16[16,2,2048]{2,1,0:T(2,128)(2,1)S(1)}, u32[]{:S(2)}, u32[]{:S(2)}) async-start(bf16[16,2,2048]{2,1,0:T(2,128)(2,1)} %reshape.72), calls=%async_computation.2 | async-start | bytes 262144 | tf_op jit(solution)/shard_map/all_to_all | solution.py:24
  19.4 0.0 copy-done.1
  19.5 2.4 copy.10
  21.9 4.0 %copy.11 = bf16[128,16,512]{2,0,1:T(8,128)(2,1)} copy(bf16[128,16,512]{0,2,1:T(8,128)(2,1)} %bitcast.30) | data formatting | bytes 4194304 | tf_op jit(solution)/shard_map/all_to_all | solution.py:25
  25.9 2.8 %all-to-all-done.1 = bf16[16,2,2048]{2,1,0:T(2,128)(2,1)S(1)} async-done(((bf16[16,2,2048]{2,1,0:T(2,128)(2,1)}), bf16[16,2,2048]{2,1,0:T(2,128)(2,1)S(1)}, u32[]{:S(2)}, u32[]{:S(2)}) %all-to-all-start.1) | async-done | bytes 131104 | tf_op jit(solution)/shard_map/all_to_all | solution.py:24
  28.7 4.9 %all-to-all-start = ((bf16[128,16,512]{2,0,1:T(8,128)(2,1)}), bf16[128,16,512]{2,0,1:T(8,128)(2,1)}, u32[]{:S(2)}, u32[]{:S(2)}) async-start(bf16[128,16,512]{2,0,1:T(8,128)(2,1)} %copy.11), calls=%async_computation | async-start | bytes 4194304 | tf_op jit(solution)/shard_map/all_to_all | solution.py:25
  33.6 0.0 reduce-scatter.2.cloned.1.call-start
  34.3 3.8 %gather_fusion = bf16[16,64,512]{2,1,0:T(8,128)(2,1)} fusion(bf16[64,64,512]{2,1,0:T(8,128)(2,1)} %param.8, s32[1024]{0:T(1024)S(1)} %pad_clamp_fusion), kind=kCustom, calls=%fused_computation | custom fusion | bytes 2097216 | tf_op jit(solution)/shard_map/jit(_take)/gather | solution.py:27
  38.1 0.2 reshape.73
  38.3 0.2 copy.12
  38.5 0.2 reshape.53
  38.7 58.8 %all-to-all-done = bf16[128,16,512]{2,0,1:T(8,128)(2,1)} async-done(((bf16[128,16,512]{2,0,1:T(8,128)(2,1)}), bf16[128,16,512]{2,0,1:T(8,128)(2,1)}, u32[]{:S(2)}, u32[]{:S(2)}) %all-to-all-start) | async-done | bytes 2097184 | tf_op jit(solution)/shard_map/all_to_all | solution.py:25
  97.5 3.7 %fusion.2 = f32[16,128,64]{1,2,0:T(8,128)} fusion(bf16[128,16,512]{2,0,1:T(8,128)(2,1)} %all-to-all-done, bf16[16,64,512]{2,1,0:T(8,128)(2,1)} %gather_fusion, pred[16]{0:T(512)(128)(4,1)S(1)} %compare_and_fusion), kind=kOutput, calls=%fused_computation.4 | convolution fusion | flops 134742016 | bytes 3670032 | tf_op jit(solution)/shard_map/bnd,brd->bnr/dot_general | solution.py:29
  101.3 0.0 reduce-scatter.2.cloned.1.call-update
  101.3 74.4 %all-gather.2.cloned.1.call-done = bf16[8192,1024]{1,0:T(8,128)(2,1)} async-done(((bf16[512,1024]{1,0:T(8,128)(2,1)}), bf16[8192,1024]{1,0:T(8,128)(2,1)}) %all-gather.2.cloned.1.call-update) | async-done | bytes 16777232 | tf_op jit(solution)/shard_map/all_gather | solution.py:43
  175.7 8.9 %fusion.16 = f32[128,1024]{1,0:T(8,128)} fusion(bf16[128,8192]{1,0:T(8,128)(2,1)S(1)} %copy-done.1, bf16[8192,1024]{1,0:T(8,128)(2,1)} %all-gather.2.cloned.1.call-done), kind=kOutput, calls=%fused_computation.23 | convolution fusion | flops 2147483648 | bytes 19398656 | tf_op jit(solution)/shard_map/dot_general | solution.py:41
  184.6 50.8 %reduce-scatter.2.cloned.1.call-done = f32[1,128,64]{1,2,0:T(8,128)} async-done(((f32[16,128,64]{1,2,0:T(8,128)}), f32[1,128,64]{1,2,0:T(8,128)}) %reduce-scatter.2.cloned.1.call-update) | async-done | bytes 32784 | tf_op jit(solution)/shard_map/reduce_scatter | solution.py:28
  235.4 2.0 fusion.6
  (3 shorter events, 0.0 us)
Async XLA Ops:
  6.5 1.6 copy-start
  6.5 12.9 %copy-start.1 = (bf16[128,8192]{1,0:T(8,128)(2,1)S(1)}, bf16[128,8192]{1,0:T(8,128)(2,1)}, u32[]{:S(2)}) copy-start(bf16[128,8192]{1,0:T(8,128)(2,1)} %param.6) | copy-start | bytes 6291460
  6.5 169.2 %all-gather.2.cloned.1.call-start = ((), (), s32[]{:S(2)}) async-start(), calls=%async_computation.3 | async-start | bytes 17825792 | tf_op jit(solution)/shard_map/all_gather | solution.py:43
  12.1 16.6 %all-to-all-start.1 = ((bf16[16,2,2048]{2,1,0:T(2,128)(2,1)}), bf16[16,2,2048]{2,1,0:T(2,128)(2,1)S(1)}, u32[]{:S(2)}, u32[]{:S(2)}) async-start(bf16[16,2,2048]{2,1,0:T(2,128)(2,1)} %reshape.72), calls=%async_computation.2 | async-start | bytes 262144 | tf_op jit(solution)/shard_map/all_to_all | solution.py:24
  28.7 68.8 %all-to-all-start = ((bf16[128,16,512]{2,0,1:T(8,128)(2,1)}), bf16[128,16,512]{2,0,1:T(8,128)(2,1)}, u32[]{:S(2)}, u32[]{:S(2)}) async-start(bf16[128,16,512]{2,0,1:T(8,128)(2,1)} %copy.11), calls=%async_computation | async-start | bytes 4194304 | tf_op jit(solution)/shard_map/all_to_all | solution.py:25
  33.6 201.7 %reduce-scatter.2.cloned.1.call-start = ((), (), s32[]{:S(2)}) async-start(), calls=%async_computation.4 | async-start | bytes 557056 | tf_op jit(solution)/shard_map/reduce_scatter | solution.py:28
Sparse Core Ops, SparseCore 0:
  9.5 166.1 all-gather.1
  179.2 56.0 reduce-scatter.1
where the time goes:
time: 245 us; the launch traced here: 244 us
  waiting for transfers between devices  188 us (77%)
  matrix products  14.6 us (6%)
  between operations  14.1 us (6%)
  local copies, waits for them, and re-layouts  13.2 us (5%)
  starting transfers between devices  12.4 us (5%)
    all_gather x1, waiting for transfers between devices, per_device(): lax.all_gather(value_weight_matrix, 'dp', axis=0, tiled=True)  74.4 us
    all_to_all x1, waiting for transfers between devices, per_device(): lax.all_to_all(tokens, 'dp', split_axis=1, concat_axis=0, tiled=True)  58.8 us
    reduce_scatter x1, waiting for transfers between devices, per_device(): lax.psum_scatter(jnp.einsum('bnd,brd->bnr', feature_blocks, lookup_weight...  50.8 us
    dot_general x1, matrix products, per_device(): jnp.dot(tokens, lax.all_gather(value_weight_matrix, 'dp', axis=0, tiled=T...  8.88 us
    all_to_all x1, starting transfers between devices, per_device(): lax.all_to_all(up_outgoing, 'dp', split_axis=1, concat_axis=3, tiled=True)  7.39 us
    all_to_all x1, starting transfers between devices, per_device(): lax.all_to_all(tokens, 'dp', split_axis=1, concat_axis=0, tiled=True)  4.93 us
  transfers between devices with their start and end apart: 4, of which 4 were waited for; matrix products, arithmetic and copies ran while one was open for 12% of the time, Pallas kernels for 0%

commit v1 on v0

v1 whole, which is shorter than its diff:
```python
import jax
import jax.numpy as jnp
from jax import lax
from jax.sharding import PartitionSpec as P

BLOCK = 128
SQUARE = 4
ADAPTER_SCALE = 0.5


def per_device(
    tokens,
    value_weight_matrix,
    adapter_down_weight,
    adapter_up_weight,
    adapter_of_block,
    block_live_length,
):
    group_count = lax.axis_size("groups")
    peer_count = lax.axis_size("dp")
    ring = peer_count // SQUARE
    depth, columns = value_weight_matrix.shape
    half = depth // 2
    rank = adapter_down_weight.shape[1]
    rows = tokens.shape[0]
    group, peer = lax.axis_index("groups"), lax.axis_index("dp")
    side = lax.rem(group, 2)
    place, member = peer // SQUARE, lax.rem(peer, SQUARE)

    across = [(g, g ^ 1) for g in range(group_count)]
    onward = [
        (p, (p // SQUARE + 1) % ring * SQUARE + p % SQUARE) for p in range(peer_count)
    ]

    def within(step):
        return [(p, p ^ step) for p in range(peer_count)]

    held = lax.dynamic_slice_in_dim(value_weight_matrix, side * half, half, 0)
    other = lax.dynamic_slice_in_dim(value_weight_matrix, (1 - side) * half, half, 0)
    weights = [(held, other)]
    for _ in range(ring - 1):
        held = lax.ppermute(held, "dp", onward)
        weights.append((held, lax.ppermute(held, "groups", across)))

    pieces = tokens.reshape(rows, ring, SQUARE, 2, half)
    order = lax.rem(place - jnp.arange(ring) + ring, ring)
    shares = []
    for step in range(SQUARE):
        share = lax.dynamic_index_in_dim(pieces, member ^ step, 2, keepdims=False)
        share = jnp.take(share, order, axis=1)
        share = jnp.take(share, jnp.stack([side, 1 - side]), axis=2)
        share = share.reshape(rows, ring, 2 * half)
        shares.append(share if step == 0 else lax.ppermute(share, "dp", within(step)))
    features = jnp.stack(shares)

    chosen = jnp.concatenate(
        [
            jnp.take(adapter_down_weight, adapter_of_block, axis=0),
            jnp.take(adapter_up_weight, adapter_of_block, axis=0),
        ],
        axis=2,
    )
    chosen = lax.all_to_all(chosen, "dp", 0, 0, tiled=True)
    shrunk = jnp.einsum(
        "nif,irf->nr",
        tokens.reshape(rows, peer_count, depth),
        chosen[:, :, :depth],
        preferred_element_type=jnp.float32,
    )
    low_rank = (shrunk * ADAPTER_SCALE).astype(jnp.bfloat16)
    up = jnp.swapaxes(chosen[:, :, depth:], 0, 1).reshape(rank, columns)
    change = jnp.dot(low_rank, up, preferred_element_type=jnp.float32)

    partial = jnp.zeros((SQUARE, rows, columns), jnp.float32)
    for step, pair in enumerate(weights):
        partial = partial + jnp.einsum(
            "bnf,fv->bnv",
            features[:, :, step],
            jnp.concatenate(pair),
            preferred_element_type=jnp.float32,
        )
    outgoing = jnp.stack([partial[1], partial[3]])
    incoming = lax.ppermute(outgoing, "dp", within(1))
    there = partial[2] + incoming[1]
    here = partial[0] + incoming[0]
    base = here + lax.ppermute(there, "dp", within(2))

    live_rows = jnp.arange(BLOCK, dtype=jnp.int32)[None, :] < block_live_length[:, None]
    return jnp.where(live_rows.reshape(-1, 1), base + change, 0.0).astype(jnp.bfloat16)


def solution(mesh):
    in_specs = (
        P(("groups", "dp"), None),
        P("dp", None),
        P(None, None, "dp"),
        P(None, None, "dp"),
        P("groups"),
        P(("groups", "dp")),
    )
    out_specs = P(("groups", "dp"), None)
    return jax.shard_map(
        per_device, mesh=mesh, in_specs=in_specs, out_specs=out_specs, check_vma=False
    )
```

time: 245 us -> 107 us (0.44)
  waiting for transfers between devices: 188 us -> 36.4 us
  local copies, waits for them, and re-layouts: 13.2 us -> 30.4 us
  between operations: 14.1 us -> 0.94 us
  starting transfers between devices: 12.4 us -> 19.3 us
  other arithmetic: 2.35 us -> 9.14 us
  matrix products: 14.6 us -> 10.1 us
    all_gather x1 -> x0, waiting for transfers between devices: 74.4 us -> none  [per_device(): lax.all_gather(value_weight_matrix, 'dp', axis=0, tiled=True)]
    all_to_all x2 -> x1, waiting for transfers between devices: 61.6 us -> 0.01 us  [per_device(): chosen = lax.all_to_all(chosen, 'dp', 0, 0, tiled=True)]
    reduce_scatter x1 -> x0, waiting for transfers between devices: 50.8 us -> none  [per_device(): lax.psum_scatter(jnp.einsum('bnd,brd->bnr', feature_blocks, lookup_weight...]
    ppermute x0 -> x11, waiting for transfers between devices: none -> 36.4 us  [the longest x3 14.6 us: per_device(): weights.append((held, lax.ppermute(held, 'groups', across)))]
    ppermute x0 -> x11, starting transfers between devices: none -> 13.1 us  [the longest x3 4.66 us: per_device(): held = lax.ppermute(held, 'dp', onward)]
    gather x2 -> x10, local copies, waits for them, and re-layouts: 4.37 us -> 13.1 us  [the longest x4 6.31 us: per_device(): share = jnp.take(share, jnp.stack([side, 1 - side]), axis=2)]
    dynamic_slice x0 -> x2, local copies, waits for them, and re-layouts: none -> 6.33 us  [the longest x1 3.95 us: per_device(): share = lax.dynamic_index_in_dim(pieces, member ^ step, 2, keepdims=False)]
    all_to_all x2 -> x1, starting transfers between devices: 12.3 us -> 6.2 us  [per_device(): chosen = lax.all_to_all(chosen, 'dp', 0, 0, tiled=True)]
  transfers between devices with their start and end apart: 4 -> 12, of which waited for: 4 -> 6; matrix products, arithmetic and copies ran while one was open for 12% -> 41% of each run, Pallas kernels for 0% -> 0%
where the time goes in v1:
time: 107 us; the launch traced here: 106 us
  waiting for transfers between devices  36.4 us (34%)
  local copies, waits for them, and re-layouts  30.4 us (28%)
  starting transfers between devices  19.3 us (18%)
  matrix products  10.1 us (9%)
  other arithmetic  9.14 us (9%)
    ppermute x3, waiting for transfers between devices, per_device(): weights.append((held, lax.ppermute(held, 'groups', across)))  14.6 us
    ppermute x3, waiting for transfers between devices, per_device(): held = lax.ppermute(held, 'dp', onward)  12.5 us
    ppermute x1, waiting for transfers between devices, per_device(): base = here + lax.ppermute(there, 'dp', within(2))  7.36 us
    gather x4, local copies, waits for them, and re-layouts, per_device(): share = jnp.take(share, jnp.stack([side, 1 - side]), axis=2)  6.31 us
    all_to_all x1, starting transfers between devices, per_device(): chosen = lax.all_to_all(chosen, 'dp', 0, 0, tiled=True)  6.2 us
    dot_general x4, matrix products, per_device(): jnp.einsum('bnf,fv->bnv', features[:, :, step], jnp.concatenate(pair), pr...  6.16 us
    ppermute x3, starting transfers between devices, per_device(): held = lax.ppermute(held, 'dp', onward)  4.66 us
    ppermute x3, starting transfers between devices, per_device(): weights.append((held, lax.ppermute(held, 'groups', across)))  4.62 us
  transfers between devices with their start and end apart: 12, of which 6 were waited for; matrix products, arithmetic and copies ran while one was open for 41% of the time, Pallas kernels for 0%

profile of v1, /device:TPU:0, one launch (start us, length us, event | category | flops | bytes accessed | tf_op | source)
XLA Modules:
  0.0 106.3 jit_solution(2623740507743485818)
XLA Ops:
  0.0 2.4 %constant_dynamic-slice_fusion = (bf16[256,1024]{1,0:T(8,128)(2,1)}, bf16[256,1024]{1,0:T(8,128)(2,1)}) fusion(bf16[512,1024]{1,0:T(8,128)(2,1)} %param.11, s32[]{:T(128)S(6)} %select_n.63, s32[]{:T(128)S(6)} %select_n.62), kind=kLoop, calls=%fused_computation.76 | loop fusion | bytes 2097160 | tf_op jit(solution)/shard_map/dynamic_slice | solution.py:39
  2.4 3.0 %collective-permute-start.3 = (bf16[256,1024]{1,0:T(8,128)(2,1)}, bf16[256,1024]{1,0:T(8,128)(2,1)}, u32[]{:S(2)}, u32[]{:S(2)}) collective-permute-start(bf16[256,1024]{1,0:T(8,128)(2,1)} %get-tuple-element.16), channel_id=1, source_target_pairs={{0,4},{1,5},{2,6},{3,7},{4,8},{5,9},{6,10},{7,11},{8,12},{9,13},{1... | collective-permute-start | bytes 1572872 | tf_op jit(solution)/shard_map/ppermute | solution.py:42
  5.4 2.8 %reshape.45 = bf16[128,4,4,2,256]{4,3,2,1,0:T(2,128)(2,1)} reshape(bf16[128,8192]{1,0:T(8,128)(2,1)S(1)} %copy-done.1) | data formatting | bytes 4194304 | tf_op jit(solution)/shard_map/reshape | solution.py:45
  8.2 4.0 %constant_dynamic-slice_fusion.5 = (bf16[128,4,1,2,256]{4,3,2,1,0:T(2,128)(2,1)S(1)}, bf16[128,4,1,2,256]{4,3,2,1,0:T(2,128)(2,1)}, bf16[128,4,1,2,256]{4,3,2,1,0:T(2,128)(2,1)S(1)}, bf16[128,4,1,2,256]{4,3,2,1,0:T(2,128)(2,1)}) fusion(bf16[128,4,4,2,256]{4,3,2,1,0:T(2,128)(2,1)} %reshape.45, s32[]{:T(128)S(6)} %select_n.57, s32[]{:T(128)S(6)} %select_n.60, ...), kind=kLoop, calls=%fused_computation.81 | loop fusion | bytes 4194320 | tf_op jit(solution)/shard_map/jit(dynamic_index_in_dim)/dynamic_slice | solution.py:49
  13.6 2.2 %copy_bitcast_fusion = (bf16[128,4,2,256]{3,0,2,1:T(8,128)(2,1)}, bf16[128,4,2,256]{3,0,2,1:T(8,128)(2,1)S(1)}) fusion(bf16[128,4,1,2,256]{4,3,2,1,0:T(2,128)(2,1)} %get-tuple-element.14, bf16[128,4,1,2,256]{4,3,2,1,0:T(2,128)(2,1)} %get-tuple-element.12), kind=kLoop, calls=%fused_computation.50 | loop fusion | bytes 2097152 | tf_op jit(solution)/shard_map/jit(dynamic_index_in_dim)/squeeze | solution.py:49
  16.4 1.6 %gather_fusion.8 = bf16[4,128,2,256]{3,1,2,0:T(8,128)(2,1)S(1)} fusion(bf16[128,4,2,256]{3,0,2,1:T(8,128)(2,1)} %get-tuple-element.25, s32[1024]{0:T(1024)S(1)} %pad_clamp_fusion.2), kind=kCustom, calls=%fused_computation.4.clone | custom fusion | bytes 1048592 | tf_op jit(solution)/shard_map/jit(_take)/gather | solution.py:50
  18.1 1.4 %select_bitcast_fusion.7 = (bf16[128,4,2,256]{3,0,2,1:T(8,128)(2,1)}, bf16[128,4,2,256]{3,0,2,1:T(8,128)(2,1)}, bf16[128,4,2,256]{3,0,2,1:T(8,128)(2,1)}, bf16[128,4,2,256]{3,0,2,1:T(8,128)(2,1)}) fusion(bf16[4,128,2,256]{3,1,2,0:T(8,128)(2,1)S(1)} %gather_fusion.2, pred[4]{0:T(512)(128)(4,1)S(1)} %compare_and_fusion.1, ...), kind=kLoop, calls=%fused_computation.61 | loop fusion | flops 1048576 | bytes 4194308 | tf_op jit(solution)/shard_map/jit(_take)/select_n | solution.py:50
  19.6 1.7 %gather_fusion.5 = bf16[2,128,4,256]{3,1,2,0:T(8,128)(2,1)S(1)} fusion(bf16[128,4,2,256]{3,0,2,1:T(8,128)(2,1)} %get-tuple-element.22, s32[1024]{0:T(1024)S(1)} %pad_clamp_fusion.1), kind=kCustom, calls=%fused_computation.5.clone | custom fusion | bytes 1048584 | tf_op jit(solution)/shard_map/jit(_take)/gather | solution.py:51
  21.2 1.6 %gather_fusion.7 = bf16[2,128,4,256]{3,1,2,0:T(8,128)(2,1)S(1)} fusion(bf16[128,4,2,256]{3,0,2,1:T(8,128)(2,1)} %get-tuple-element.23, s32[1024]{0:T(1024)S(1)} %pad_clamp_fusion.1), kind=kCustom, calls=%fused_computation.6.clone | custom fusion | bytes 1048584 | tf_op jit(solution)/shard_map/jit(_take)/gather | solution.py:51
  22.9 1.6 %gather_fusion.9 = bf16[2,128,4,256]{3,1,2,0:T(8,128)(2,1)S(1)} fusion(bf16[128,4,2,256]{3,0,2,1:T(8,128)(2,1)} %get-tuple-element.24, s32[1024]{0:T(1024)S(1)} %pad_clamp_fusion.1), kind=kCustom, calls=%fused_computation.7.clone | custom fusion | bytes 1048584 | tf_op jit(solution)/shard_map/jit(_take)/gather | solution.py:51
  24.5 1.4 %gather_fusion.3 = bf16[2,128,4,256]{3,1,2,0:T(8,128)(2,1)} fusion(bf16[128,4,2,256]{3,0,2,1:T(8,128)(2,1)S(1)} %copy-done.2, s32[1024]{0:T(1024)S(1)} %pad_clamp_fusion.1), kind=kCustom, calls=%fused_computation.1.clone | custom fusion | bytes 1048584 | tf_op jit(solution)/shard_map/jit(_take)/gather | solution.py:51
  25.9 1.3 %select_bitcast_fusion.6 = (bf16[128,4,2,256]{3,0,1,2:T(8,128)(2,1)S(1)}, bf16[2,4,16,8,256]{4,3,2,1,0:T(8,128)(2,1)S(1)}, bf16[2,4,16,8,256]{4,3,2,1,0:T(8,128)(2,1)S(1)}, bf16[2,4,16,8,256]{4,3,2,1,0:T(8,128)(2,1)S(1)}) fusion(bf16[2,128,4,256]{3,1,2,0:T(8,128)(2,1)} %gather_fusion.3, pred[2]{0:T(512)(128)(4,1)S(1)} %get-tuple-element.6, ...), kind=kLoop, calls=%fused_computation.60 | loop fusion | flops 1048576 | bytes 4194306 | tf_op jit(solution)/shard_map/jit(_take)/select_n | solution.py:51
  28.1 1.5 %collective-permute-start.1 = (bf16[128,4,512]{2,0,1:T(8,128)(2,1)}, bf16[128,4,512]{2,0,1:T(8,128)(2,1)}, u32[]{:S(2)}, u32[]{:S(2)}) collective-permute-start(bf16[128,4,512]{2,0,1:T(8,128)(2,1)} %bitcast.35), channel_id=1, source_target_pairs={{0,2},{1,3},{2,0},{3,1},{4,6},{5,7},{6,4},{7,5},{8,10},{9,11},{10,... | collective-permute-start | bytes 1572872 | tf_op jit(solution)/shard_map/ppermute | solution.py:53
  31.9 1.6 %collective-permute-start.5 = (bf16[256,1024]{1,0:T(8,128)(2,1)}, bf16[256,1024]{1,0:T(8,128)(2,1)S(1)}, u32[]{:S(2)}, u32[]{:S(2)}) collective-permute-start(bf16[256,1024]{1,0:T(8,128)(2,1)} %collective-permute-done.3), channel_id=1, source_target_pairs={{0,4},{1,5},{2,6},{3,7},{4,8},{5,9},{6,10},{7,11},{8,12},{9,13},{1... | collective-permute-start | bytes 1572872 | tf_op jit(solution)/shard_map/ppermute | solution.py:42
  34.2 2.8 %gather_fusion = bf16[16,64,512]{2,1,0:T(8,128)(2,1)S(1)} fusion(bf16[64,64,512]{2,1,0:T(8,128)(2,1)} %param.12, s32[1024]{0:T(1024)S(1)} %pad_clamp_fusion), kind=kCustom, calls=%fused_computation.8 | custom fusion | bytes 2097216 | tf_op jit(solution)/shard_map/jit(_take)/gather | solution.py:58
  37.2 1.6 %collective-permute-start.4 = (bf16[256,1024]{1,0:T(8,128)(2,1)}, bf16[256,1024]{1,0:T(8,128)(2,1)}, u32[]{:S(2)}, u32[]{:S(2)}) collective-permute-start(bf16[256,1024]{1,0:T(8,128)(2,1)} %collective-permute-done.3), channel_id=1, source_target_pairs={{0,16},{16,0},{1,17},{17,1},{2,18},{18,2},{3,19},{19,3},{4,20},{20... | collective-permute-start | bytes 1572872 | tf_op jit(solution)/shard_map/ppermute | solution.py:43
  38.8 9.0 %collective-permute-done.5 = bf16[256,1024]{1,0:T(8,128)(2,1)S(1)} collective-permute-done((bf16[256,1024]{1,0:T(8,128)(2,1)}, bf16[256,1024]{1,0:T(8,128)(2,1)S(1)}, u32[]{:S(2)}, u32[]{:S(2)}) %collective-permute-start.5) | collective-permute-done | bytes 524320 | tf_op jit(solution)/shard_map/ppermute | solution.py:42
  49.0 6.2 %all-to-all-start = ((bf16[16,64,576]{2,1,0:T(8,128)(2,1)}), bf16[16,64,576]{2,1,0:T(8,128)(2,1)}, u32[]{:S(2)}, u32[]{:S(2)}) async-start(bf16[16,64,576]{2,1,0:T(8,128)(2,1)} %pad_maximum_fusion.1), calls=%async_computation | async-start | bytes 2621440 | tf_op jit(solution)/shard_map/all_to_all | solution.py:63
  56.1 1.7 %pad_maximum_fusion = bf16[4,128,4,512]{3,1,0,2:T(8,128)(2,1)S(1)} fusion(bf16[1,128,4,512]{3,1,0,2:T(8,128)(2,1)} %bitcast.17, bf16[1,128,4,512]{3,1,0,2:T(8,128)(2,1)} %bitcast.13, bf16[1,128,4,512]{3,1,0,2:T(8,128)(2,1)} %bitcast.9, bf16[1,128,4,512]{3,1,0,2:T(8,128)(2,1)S(1)} %stack_reshape.3), kind=kLoop, calls=%fused_computation.13 | loop fusion | flops 3145728 | bytes 4194304 | tf_op jit(solution)/shard_map/stack | solution.py:54
  57.8 1.6 %collective-permute-start.6 = (bf16[256,1024]{1,0:T(8,128)(2,1)S(1)}, bf16[256,1024]{1,0:T(8,128)(2,1)S(1)}, u32[]{:S(2)}, u32[]{:S(2)}) collective-permute-start(bf16[256,1024]{1,0:T(8,128)(2,1)S(1)} %collective-permute-done.5), channel_id=1, source_target_pairs={{0,16},{16,0},{1,17},{17,1},{2,18},{18,2},{3,19},{19,3},{4,20},{20... | collective-permute-start | bytes 1572872 | tf_op jit(solution)/shard_map/ppermute | solution.py:43
  59.4 1.8 %fusion.17 = f32[4,128,1024]{2,1,0:T(8,128)S(1)} fusion(bf16[256,1024]{1,0:T(8,128)(2,1)S(1)} %copy-done.3, bf16[256,1024]{1,0:T(8,128)(2,1)} %get-tuple-element.16, bf16[4,128,4,512]{3,1,0,2:T(8,128)(2,1)S(1)} %pad_maximum_fusion), kind=kOutput, calls=%fused_computation.22 | convolution fusion | flops 538968064 | bytes 3670016 | tf_op jit(solution)/shard_map/bnf,fv->bnv/dot_general | solution.py:76
  61.1 3.4 %collective-permute-done.7 = bf16[256,1024]{1,0:T(8,128)(2,1)S(1)} collective-permute-done((bf16[256,1024]{1,0:T(8,128)(2,1)S(1)}, bf16[256,1024]{1,0:T(8,128)(2,1)S(1)}, u32[]{:S(2)}, u32[]{:S(2)}) %collective-permute-start.7) | collective-permute-done | bytes 524320 | tf_op jit(solution)/shard_map/ppermute | solution.py:42
  64.6 1.5 %collective-permute-start.8 = (bf16[256,1024]{1,0:T(8,128)(2,1)S(1)}, bf16[256,1024]{1,0:T(8,128)(2,1)S(1)}, u32[]{:S(2)}, u32[]{:S(2)}) collective-permute-start(bf16[256,1024]{1,0:T(8,128)(2,1)S(1)} %collective-permute-done.7), channel_id=1, source_target_pairs={{0,16},{16,0},{1,17},{17,1},{2,18},{18,2},{3,19},{19,3},{4,20},{20... | collective-permute-start | bytes 1572872 | tf_op jit(solution)/shard_map/ppermute | solution.py:43
  66.1 1.9 %fusion.20 = f32[4,128,1024]{2,1,0:T(8,128)S(1)} fusion(bf16[256,1024]{1,0:T(8,128)(2,1)} %collective-permute-done.4, bf16[256,1024]{1,0:T(8,128)(2,1)} %collective-permute-done.3, bf16[4,128,4,512]{3,1,0,2:T(8,128)(2,1)S(1)} %pad_maximum_fusion), kind=kOutput, calls=%fused_computation.26 | convolution fusion | flops 538968064 | bytes 3670016 | tf_op jit(solution)/shard_map/bnf,fv->bnv/dot_general | solution.py:76
  68.0 4.6 %collective-permute-done.6 = bf16[256,1024]{1,0:T(8,128)(2,1)S(1)} collective-permute-done((bf16[256,1024]{1,0:T(8,128)(2,1)S(1)}, bf16[256,1024]{1,0:T(8,128)(2,1)S(1)}, u32[]{:S(2)}, u32[]{:S(2)}) %collective-permute-start.6) | collective-permute-done | bytes 524320 | tf_op jit(solution)/shard_map/ppermute | solution.py:43
  73.4 9.9 %collective-permute-done.8 = bf16[256,1024]{1,0:T(8,128)(2,1)S(1)} collective-permute-done((bf16[256,1024]{1,0:T(8,128)(2,1)S(1)}, bf16[256,1024]{1,0:T(8,128)(2,1)S(1)}, u32[]{:S(2)}, u32[]{:S(2)}) %collective-permute-start.8) | collective-permute-done | bytes 524320 | tf_op jit(solution)/shard_map/ppermute | solution.py:43
  83.3 1.8 %add_add_fusion = f32[4,128,1024]{2,1,0:T(8,128)S(1)} fusion(f32[4,128,1024]{2,1,0:T(8,128)S(1)} %fusion.23, f32[4,128,1024]{2,1,0:T(8,128)S(1)} %fusion.17, f32[4,128,1024]{2,1,0:T(8,128)S(1)} %fusion.20, bf16[256,1024]{1,0:T(8,128)(2,1)S(1)} %collective-permute-done.8, bf16[256,1024]{1,0:T(8,128)(2,1)} %copy-done.5, ...), kind=kOutput, calls=%fused_computation.14 | convolution fusion | flops 540540928 | bytes 9961472 | tf_op jit(solution)/shard_map/bnf,fv->bnv/dot_general | solution.py:76
  86.0 2.0 %collective-permute-done.9 = f32[2,128,1024]{2,1,0:T(8,128)S(1)} collective-permute-done((f32[2,128,1024]{2,1,0:T(8,128)S(1)}, f32[2,128,1024]{2,1,0:T(8,128)S(1)}, u32[]{:S(2)}, u32[]{:S(2)}) %collective-permute-start.9) | collective-permute-done | bytes 1048608 | tf_op jit(solution)/shard_map/ppermute | solution.py:83
  89.9 1.7 %collective-permute-start.10 = (f32[128,1024]{1,0:T(8,128)}, f32[128,1024]{1,0:T(8,128)}, u32[]{:S(2)}, u32[]{:S(2)}) collective-permute-start(f32[128,1024]{1,0:T(8,128)} %fusion.28), channel_id=1, source_target_pairs={{0,2},{1,3},{2,0},{3,1},{4,6},{5,7},{6,4},{7,5},{8,10},{9,11},{10,... | collective-permute-start | bytes 1572872 | tf_op jit(solution)/shard_map/ppermute | solution.py:86
  92.9 3.9 %fusion.13 = f32[128,1024]{1,0:T(8,128)} fusion(bf16[64,1024]{1,0:T(8,128)(2,1)S(1)} %reshape.50, bf16[16,16,8,512]{3,2,1,0:T(8,128)(2,1)} %bitcast.98, bf16[16,64,576]{2,1,0:T(8,128)(2,1)} %all-to-all-done), kind=kOutput, calls=%fused_computation.19 | convolution fusion | flops 151011328 | bytes 3801088 | tf_op jit(solution)/shard_map/dot_general | solution.py:72
  96.8 7.4 %collective-permute-done.10 = f32[128,1024]{1,0:T(8,128)} collective-permute-done((f32[128,1024]{1,0:T(8,128)}, f32[128,1024]{1,0:T(8,128)}, u32[]{:S(2)}, u32[]{:S(2)}) %collective-permute-start.10) | collective-permute-done | bytes 524320 | tf_op jit(solution)/shard_map/ppermute | solution.py:86
  104.1 2.2 %fusion.33 = bf16[128,1024]{1,0:T(8,128)(2,1)} fusion(f32[128,1024]{1,0:T(8,128)} %fusion.13, f32[128,1024]{1,0:T(8,128)} %collective-permute-done.10, f32[2,128,1024]{2,1,0:T(8,128)} %copy-done.4, f32[4,128,1024]{2,1,0:T(8,128)S(1)} %add_add_fusion, pred[128]{0:T(512)(128)(4,1)S(1)} %iota_compare_fusion), kind=kLoop, calls=%fused_computation.45 | loop fusion | flops 655360 | bytes 2359424 | tf_op jit(solution)/shard_map/convert_element_type | solution.py:89
  (53 shorter events, 12.3 us)
Async XLA Ops:
  0.0 33.5 %copy-start = (bf16[64,64,64]{2,1,0:T(8,128)(2,1)S(1)}, bf16[64,64,64]{2,1,0:T(8,128)(2,1)}, u32[]{:S(2)}) copy-start(bf16[64,64,64]{2,1,0:T(8,128)(2,1)} %param.13) | copy-start | bytes 1572868
  0.0 5.4 %copy-start.1 = (bf16[128,8192]{1,0:T(8,128)(2,1)S(1)}, bf16[128,8192]{1,0:T(8,128)(2,1)}, u32[]{:S(2)}) copy-start(bf16[128,8192]{1,0:T(8,128)(2,1)} %param.10) | copy-start | bytes 6291460
  2.4 29.5 %collective-permute-start.3 = (bf16[256,1024]{1,0:T(8,128)(2,1)}, bf16[256,1024]{1,0:T(8,128)(2,1)}, u32[]{:S(2)}, u32[]{:S(2)}) collective-permute-start(bf16[256,1024]{1,0:T(8,128)(2,1)} %get-tuple-element.16), channel_id=1, source_target_pairs={{0,4},{1,5},{2,6},{3,7},{4,8},{5,9},{6,10},{7,11},{8,12},{9,13},{1... | collective-permute-start | bytes 1572872 | tf_op jit(solution)/shard_map/ppermute | solution.py:42
  19.6 4.9 %copy-start.2 = (bf16[128,4,2,256]{3,0,2,1:T(8,128)(2,1)S(1)}, bf16[128,4,2,256]{3,0,2,1:T(8,128)(2,1)}, u32[]{:S(2)}) copy-start(bf16[128,4,2,256]{3,0,2,1:T(8,128)(2,1)} %get-tuple-element.21) | copy-start | bytes 1572868
  27.2 4.7 %copy-start.6 = (s32[16]{0:T(128)S(1)}, s32[16]{0:T(128)}, u32[]{:S(2)}) copy-start(s32[16]{0:T(128)} %param.14) | copy-start | bytes 196
  28.1 28.0 %collective-permute-start.1 = (bf16[128,4,512]{2,0,1:T(8,128)(2,1)}, bf16[128,4,512]{2,0,1:T(8,128)(2,1)}, u32[]{:S(2)}, u32[]{:S(2)}) collective-permute-start(bf16[128,4,512]{2,0,1:T(8,128)(2,1)} %bitcast.35), channel_id=1, source_target_pairs={{0,2},{1,3},{2,0},{3,1},{4,6},{5,7},{6,4},{7,5},{8,10},{9,11},{10,... | collective-permute-start | bytes 1572872 | tf_op jit(solution)/shard_map/ppermute | solution.py:53
  30.4 25.7 %collective-permute-start.2 = (bf16[128,4,512]{2,0,1:T(8,128)(2,1)}, bf16[128,4,512]{2,0,1:T(8,128)(2,1)}, u32[]{:S(2)}, u32[]{:S(2)}) collective-permute-start(bf16[128,4,512]{2,0,1:T(8,128)(2,1)} %bitcast.37), channel_id=1, source_target_pairs={{0,3},{1,2},{2,1},{3,0},{4,7},{5,6},{6,5},{7,4},{8,11},{9,10},{10,... | collective-permute-start | bytes 1572872 | tf_op jit(solution)/shard_map/ppermute | solution.py:53
  31.2 24.9 %collective-permute-start = (bf16[128,4,512]{2,0,1:T(8,128)(2,1)}, bf16[128,4,512]{2,0,1:T(8,128)(2,1)}, u32[]{:S(2)}, u32[]{:S(2)}) collective-permute-start(bf16[128,4,512]{2,0,1:T(8,128)(2,1)} %bitcast.33), channel_id=1, source_target_pairs={{0,1},{1,0},{2,3},{3,2},{4,5},{5,4},{6,7},{7,6},{8,9},{9,8},{10,11... | collective-permute-start | bytes 1572872 | tf_op jit(solution)/shard_map/ppermute | solution.py:53
  31.9 15.9 %collective-permute-start.5 = (bf16[256,1024]{1,0:T(8,128)(2,1)}, bf16[256,1024]{1,0:T(8,128)(2,1)S(1)}, u32[]{:S(2)}, u32[]{:S(2)}) collective-permute-start(bf16[256,1024]{1,0:T(8,128)(2,1)} %collective-permute-done.3), channel_id=1, source_target_pairs={{0,4},{1,5},{2,6},{3,7},{4,8},{5,9},{6,10},{7,11},{8,12},{9,13},{1... | collective-permute-start | bytes 1572872 | tf_op jit(solution)/shard_map/ppermute | solution.py:42
  37.2 28.9 %collective-permute-start.4 = (bf16[256,1024]{1,0:T(8,128)(2,1)}, bf16[256,1024]{1,0:T(8,128)(2,1)}, u32[]{:S(2)}, u32[]{:S(2)}) collective-permute-start(bf16[256,1024]{1,0:T(8,128)(2,1)} %collective-permute-done.3), channel_id=1, source_target_pairs={{0,16},{16,0},{1,17},{17,1},{2,18},{18,2},{3,19},{19,3},{4,20},{20... | collective-permute-start | bytes 1572872 | tf_op jit(solution)/shard_map/ppermute | solution.py:43
  47.8 16.8 %collective-permute-start.7 = (bf16[256,1024]{1,0:T(8,128)(2,1)S(1)}, bf16[256,1024]{1,0:T(8,128)(2,1)S(1)}, u32[]{:S(2)}, u32[]{:S(2)}) collective-permute-start(bf16[256,1024]{1,0:T(8,128)(2,1)S(1)} %collective-permute-done.5), channel_id=1, source_target_pairs={{0,4},{1,5},{2,6},{3,7},{4,8},{5,9},{6,10},{7,11},{8,12},{9,13},{1... | collective-permute-start | bytes 1572872 | tf_op jit(solution)/shard_map/ppermute | solution.py:42
  49.0 42.5 %all-to-all-start = ((bf16[16,64,576]{2,1,0:T(8,128)(2,1)}), bf16[16,64,576]{2,1,0:T(8,128)(2,1)}, u32[]{:S(2)}, u32[]{:S(2)}) async-start(bf16[16,64,576]{2,1,0:T(8,128)(2,1)} %pad_maximum_fusion.1), calls=%async_computation | async-start | bytes 2621440 | tf_op jit(solution)/shard_map/all_to_all | solution.py:63
  56.1 3.3 %copy-start.3 = (bf16[256,1024]{1,0:T(8,128)(2,1)S(1)}, bf16[256,1024]{1,0:T(8,128)(2,1)}, u32[]{:S(2)}) copy-start(bf16[256,1024]{1,0:T(8,128)(2,1)} %get-tuple-element.15) | copy-start | bytes 1572868
  57.8 14.8 %collective-permute-start.6 = (bf16[256,1024]{1,0:T(8,128)(2,1)S(1)}, bf16[256,1024]{1,0:T(8,128)(2,1)S(1)}, u32[]{:S(2)}, u32[]{:S(2)}) collective-permute-start(bf16[256,1024]{1,0:T(8,128)(2,1)S(1)} %collective-permute-done.5), channel_id=1, source_target_pairs={{0,16},{16,0},{1,17},{17,1},{2,18},{18,2},{3,19},{19,3},{4,20},{20... | collective-permute-start | bytes 1572872 | tf_op jit(solution)/shard_map/ppermute | solution.py:43
  64.6 8.8 %copy-start.5 = (bf16[256,1024]{1,0:T(8,128)(2,1)}, bf16[256,1024]{1,0:T(8,128)(2,1)S(1)}, u32[]{:S(2)}) copy-start(bf16[256,1024]{1,0:T(8,128)(2,1)S(1)} %collective-permute-done.7) | copy-start | bytes 1572868
  64.6 18.7 %collective-permute-start.8 = (bf16[256,1024]{1,0:T(8,128)(2,1)S(1)}, bf16[256,1024]{1,0:T(8,128)(2,1)S(1)}, u32[]{:S(2)}, u32[]{:S(2)}) collective-permute-start(bf16[256,1024]{1,0:T(8,128)(2,1)S(1)} %collective-permute-done.7), channel_id=1, source_target_pairs={{0,16},{16,0},{1,17},{17,1},{2,18},{18,2},{3,19},{19,3},{4,20},{20... | collective-permute-start | bytes 1572872 | tf_op jit(solution)/shard_map/ppermute | solution.py:43
  85.3 2.7 %collective-permute-start.9 = (f32[2,128,1024]{2,1,0:T(8,128)S(1)}, f32[2,128,1024]{2,1,0:T(8,128)S(1)}, u32[]{:S(2)}, u32[]{:S(2)}) collective-permute-start(f32[2,128,1024]{2,1,0:T(8,128)S(1)} %pad_maximum_fusion.2), channel_id=1, source_target_pairs={{0,1},{1,0},{2,3},{3,2},{4,5},{5,4},{6,7},{7,6},{8,9},{9,8},{10,11... | collective-permute-start | bytes 3145736 | tf_op jit(solution)/shard_map/ppermute | solution.py:83
  88.0 1.0 copy-start.4
  89.9 14.3 %collective-permute-start.10 = (f32[128,1024]{1,0:T(8,128)}, f32[128,1024]{1,0:T(8,128)}, u32[]{:S(2)}, u32[]{:S(2)}) collective-permute-start(f32[128,1024]{1,0:T(8,128)} %fusion.28), channel_id=1, source_target_pairs={{0,2},{1,3},{2,0},{3,1},{4,6},{5,7},{6,4},{7,5},{8,10},{9,11},{10,... | collective-permute-start | bytes 1572872 | tf_op jit(solution)/shard_map/ppermute | solution.py:86

commit v2 on v0

v2 whole, which is shorter than its diff:
```python
import functools

import jax
import jax.numpy as jnp
from jax import lax
from jax.experimental import pallas as pl
from jax.experimental.pallas import tpu as pltpu
from jax.sharding import PartitionSpec as P

BLOCK = 128
SQUARE = 4
CHUNKS = 2
LANES = 128
ADAPTER_SCALE = 0.5
VMEM_BYTES = 40 * 2**20

VMEM = pl.BlockSpec(memory_space=pltpu.VMEM)
SMEM = pl.BlockSpec(memory_space=pltpu.SMEM)
ANY = pl.BlockSpec(memory_space=pl.ANY)


def params():
    return pltpu.CompilerParams(vmem_limit_bytes=VMEM_BYTES)


def cost(flops, touched):
    return pl.CostEstimate(flops=flops, bytes_accessed=touched, transcendentals=0)


def share_kernel(ring, depth, where_ref, tokens_ref, *share_refs):
    place, member, side = where_ref[0], where_ref[1], where_ref[2]
    step = 2 * side - 1
    order = [0]
    for hop in range(1, ring // 2):
        order += [step * hop, -step * hop]
    order.append(ring // 2)
    for turn, ahead in enumerate(order):
        source = lax.rem(place + ahead + ring, ring)
        for mate, share_ref in enumerate(share_refs):
            start = pl.multiple_of((source * SQUARE + (member ^ mate)) * depth, depth)
            share_ref[:, turn * depth : (turn + 1) * depth] = tokens_ref[:, pl.ds(start, depth)]


def shares_of(where, tokens, ring, depth):
    rows, features = tokens.shape
    step = 32
    width = ring * depth
    return pl.pallas_call(
        functools.partial(share_kernel, ring, depth),
        grid=(rows // step,),
        in_specs=[SMEM, pl.BlockSpec((step, features), lambda i: (i, 0))],
        out_specs=[pl.BlockSpec((step, width), lambda i: (i, 0))] * SQUARE,
        out_shape=[jax.ShapeDtypeStruct((rows, width), tokens.dtype)] * SQUARE,
        compiler_params=params(),
        cost_estimate=cost(0, 4 * rows * features),
    )(where, tokens)


def packet_sizes(depth, rank, width):
    folds = min(LANES // width, rank // 16)
    return depth // LANES, folds, rank // folds


def packet_kernel(chosen_ref, down_ref, up_ref, packet_ref, down_held, up_held, sems):
    blocks, rank, depth = down_held.shape
    width = up_held.shape[2]
    groups, folds, high = packet_sizes(depth, rank, width)

    def copies(k):
        a = chosen_ref[k]
        return (
            pltpu.make_async_copy(down_ref.at[a], down_held.at[k], sems.at[0, k]),
            pltpu.make_async_copy(up_ref.at[a], up_held.at[k], sems.at[1, k]),
        )

    for k in range(blocks):
        for copy in copies(k):
            copy.start()
    for k in range(blocks):
        for copy in copies(k):
            copy.wait()
        for g in range(groups):
            packet_ref[k, g * rank : (g + 1) * rank, :] = down_held[
                k, :, g * LANES : (g + 1) * LANES
            ]
        parts = [up_held[k, f * high : (f + 1) * high, :] for f in range(folds)]
        if folds * width < LANES:
            parts.append(jnp.zeros((high, LANES - folds * width), packet_ref.dtype))
        packet_ref[k, groups * rank :, :] = jnp.concatenate(parts, axis=1)


def packets_of(adapter_of_block, down, up):
    blocks = adapter_of_block.shape[0]
    rank, depth, width = down.shape[1], down.shape[2], up.shape[2]
    groups, _, high = packet_sizes(depth, rank, width)
    tall = groups * rank + high
    return pl.pallas_call(
        packet_kernel,
        in_specs=[SMEM, ANY, ANY],
        out_specs=VMEM,
        out_shape=jax.ShapeDtypeStruct((blocks, tall, LANES), down.dtype),
        scratch_shapes=[
            pltpu.VMEM((blocks, rank, depth), down.dtype),
            pltpu.VMEM((blocks, rank, width), up.dtype),
            pltpu.SemaphoreType.DMA((2, blocks)),
        ],
        compiler_params=params(),
        cost_estimate=cost(0, 4 * blocks * tall * LANES),
    )(adapter_of_block, down, up)


def change_kernel(rank, depth, width, tokens_ref, packet_ref, change_ref, down_held, up_held):
    peers = packet_ref.shape[0]
    groups, folds, high = packet_sizes(depth, rank, width)
    for p in range(peers):
        for g in range(groups):
            start = p * depth + g * LANES
            down_held[:, start : start + LANES] = packet_ref[p, g * rank : (g + 1) * rank, :]
        for f in range(folds):
            up_held[f * high : (f + 1) * high, p * width : (p + 1) * width] = packet_ref[
                p, groups * rank :, f * width : (f + 1) * width
            ]
    shrunk = lax.dot_general(
        tokens_ref[...],
        down_held[...],
        (((1,), (1,)), ((), ())),
        preferred_element_type=jnp.float32,
    )
    low_rank = (shrunk * ADAPTER_SCALE).astype(jnp.bfloat16)
    change_ref[...] = jnp.dot(low_rank, up_held[...], preferred_element_type=jnp.float32)


def change_of(tokens, packets, rank, depth, width):
    rows, features = tokens.shape
    columns = packets.shape[0] * width
    return pl.pallas_call(
        functools.partial(change_kernel, rank, depth, width),
        in_specs=[VMEM, VMEM],
        out_specs=VMEM,
        out_shape=jax.ShapeDtypeStruct((rows, columns), jnp.float32),
        scratch_shapes=[
            pltpu.VMEM((rank, features), tokens.dtype),
            pltpu.VMEM((rank, columns), tokens.dtype),
        ],
        compiler_params=params(),
        cost_estimate=cost(2 * rows * rank * (features + columns), 2 * rows * features),
    )(tokens, packets)


def stacked(share_refs, turn, depth):
    return jnp.concatenate(
        [share[:, turn * depth : (turn + 1) * depth] for share in share_refs], axis=0
    )


def near_kernel(depth, *refs):
    shares, weights, total_ref = refs[:SQUARE], refs[SQUARE:-1], refs[-1]
    total = None
    for turn, weight in enumerate(weights):
        term = jnp.dot(
            stacked(shares, turn, depth), weight[...], preferred_element_type=jnp.float32
        )
        total = term if total is None else total + term
    total_ref[...] = total


def near_of(shares, own, chunk, pieces):
    depth = own.shape[0]
    rows = shares[0].shape[0] * SQUARE
    columns = own.shape[1] // CHUNKS
    return pl.pallas_call(
        functools.partial(near_kernel, depth),
        grid=(1,),
        in_specs=[pl.BlockSpec(shares[0].shape, lambda i: (0, 0))] * SQUARE
        + [pl.BlockSpec((depth, columns), lambda i: (0, chunk))]
        + [pl.BlockSpec((depth, columns), lambda i: (0, 0))] * len(pieces),
        out_specs=pl.BlockSpec((rows, columns), lambda i: (0, 0)),
        out_shape=jax.ShapeDtypeStruct((rows, columns), jnp.float32),
        compiler_params=params(),
        cost_estimate=cost(2 * rows * depth * columns * (1 + len(pieces)), 2**22),
    )(*shares, own, *pieces)


def far_kernel(
    depth, where_ref, s0, s1, s2, s3, total_ref, held_ref, other_ref, out_ref, keep_ref, weight
):
    half = depth // 2
    side = where_ref[2]
    weight[pl.ds(pl.multiple_of(side * half, half), half), :] = held_ref[...]
    weight[pl.ds(pl.multiple_of((1 - side) * half, half), half), :] = other_ref[...]
    turn = s0.shape[1] // depth - 1
    rows = s0.shape[0]
    total = total_ref[...] + jnp.dot(
        stacked((s0, s1, s2, s3), turn, depth), weight[...], preferred_element_type=jnp.float32
    )
    keep_ref[0] = total[:rows]
    out_ref[0] = total[rows : 2 * rows]
    keep_ref[1] = total[2 * rows : 3 * rows]
    out_ref[1] = total[3 * rows :]


def far_of(where, shares, total, held, other):
    half, columns = held.shape
    rows = shares[0].shape[0]
    result = jax.ShapeDtypeStruct((2, rows, columns), jnp.float32)
    return pl.pallas_call(
        functools.partial(far_kernel, 2 * half),
        in_specs=[SMEM] + [VMEM] * (SQUARE + 3),
        out_specs=[VMEM] * 2,
        out_shape=[result] * 2,
        scratch_shapes=[pltpu.VMEM((2 * half, columns), held.dtype)],
        compiler_params=params(),
        cost_estimate=cost(2 * SQUARE * rows * 2 * half * columns, 2**22),
    )(where, *shares, total, held, other)


def half_kernel(where_ref, whole_ref, half_ref):
    half = half_ref.shape[0]
    start = pl.multiple_of(where_ref[2] * half, half)
    half_ref[...] = whole_ref[pl.ds(start, half), :]


def half_of(where, whole):
    depth, columns = whole.shape
    return pl.pallas_call(
        half_kernel,
        in_specs=[SMEM, VMEM],
        out_specs=VMEM,
        out_shape=jax.ShapeDtypeStruct((depth // 2, columns), whole.dtype),
        compiler_params=params(),
        cost_estimate=cost(0, 3 * depth * columns),
    )(where, whole)


def per_device(
    tokens,
    value_weight_matrix,
    adapter_down_weight,
    adapter_up_weight,
    adapter_of_block,
    block_live_length,
):
    group_count = lax.axis_size("groups")
    peer_count = lax.axis_size("dp")
    ring = peer_count // SQUARE
    depth, columns = value_weight_matrix.shape
    rank, width = adapter_up_weight.shape[1:]
    group, peer = lax.axis_index("groups"), lax.axis_index("dp")
    where = jnp.stack([peer // SQUARE, lax.rem(peer, SQUARE), lax.rem(group, 2)])

    onward = []
    for g in range(group_count):
        for p in range(peer_count):
            place = (p // SQUARE + (1 if g % 2 == 0 else ring - 1)) % ring
            onward.append((g * peer_count + p, g * peer_count + place * SQUARE + p % SQUARE))

    def along(x):
        return lax.ppermute(x, ("groups", "dp"), onward)

    def across(x):
        return lax.ppermute(x, "groups", [(g, g ^ 1) for g in range(group_count)])

    def within(x, step):
        return lax.ppermute(x, "dp", [(p, p ^ step) for p in range(peer_count)])

    wide = columns // CHUNKS
    held = [value_weight_matrix[:, c * wide : (c + 1) * wide] for c in range(CHUNKS)]
    pieces = [[] for _ in range(CHUNKS)]
    for _ in range(ring // 2 - 1):
        for c in range(CHUNKS):
            held[c] = along(held[c])
            pieces[c] += [held[c], across(held[c])]
    far = []
    for c in range(CHUNKS):
        mine = along(half_of(where, held[c]))
        far.append((mine, across(mine)))

    shares = shares_of(where, tokens, ring, depth)
    shares = [shares[0]] + [within(shares[m], m) for m in range(1, SQUARE)]

    packets = packets_of(adapter_of_block, adapter_down_weight, adapter_up_weight)
    packets = lax.all_to_all(packets, "dp", 0, 0, tiled=True)
    change = change_of(tokens, packets, rank, depth, width)

    base = []
    for c in range(CHUNKS):
        total = near_of(shares, value_weight_matrix, c, pieces[c])
        outgoing, keep = far_of(where, shares, total, *far[c])
        incoming = within(outgoing, 1)
        there = within(keep[1] + incoming[1], 2)
        base.append(keep[0] + incoming[0] + there)
    base = jnp.concatenate(base, axis=1)

    live_rows = jnp.arange(BLOCK, dtype=jnp.int32)[None, :] < block_live_length[:, None]
    return jnp.where(live_rows.reshape(-1, 1), base + change, 0.0).astype(jnp.bfloat16)


def solution(mesh):
    in_specs = (
        P(("groups", "dp"), None),
        P("dp", None),
        P(None, None, "dp"),
        P(None, None, "dp"),
        P("groups"),
        P(("groups", "dp")),
    )
    out_specs = P(("groups", "dp"), None)
    return jax.shard_map(
        per_device, mesh=mesh, in_specs=in_specs, out_specs=out_specs, check_vma=False
    )
```

time: 245 us -> 103 us (0.42)
  the two profiles are of different devices: /device:TPU:0 before, /device:TPU:8 now
where the time goes in v2:
time: 103 us; the launch traced here: 102 us
  waiting for transfers between devices  48.8 us (47%)
  starting transfers between devices  24.4 us (24%)
  Pallas kernels  19.6 us (19%)
  local copies, waits for them, and re-layouts  7.44 us (7%)
  other arithmetic  1.07 us (1%)
    ppermute x4, waiting for transfers between devices, along(): return lax.ppermute(x, ('groups', 'dp'), onward)  37.4 us
    ppermute x7, waiting for transfers between devices, within(): return lax.ppermute(x, 'dp', [(p, p ^ step) for p in range(peer_count)])  11.4 us
    all_to_all x1, starting transfers between devices, per_device(): packets = lax.all_to_all(packets, 'dp', 0, 0, tiled=True)  8.23 us
    ppermute x4, starting transfers between devices, along(): return lax.ppermute(x, ('groups', 'dp'), onward)  6.19 us
    ppermute x4, starting transfers between devices, across(): return lax.ppermute(x, 'groups', [(g, g ^ 1) for g in range(group_count)])  5.37 us
    pallas_call x2, Pallas kernels, near_of(): pl.pallas_call(functools.partial(near_kernel, depth), grid=(1,), in_specs...  5.21 us
    unnamed x18, local copies, waits for them, and re-layouts  5.04 us
    ppermute x7, starting transfers between devices, within(): return lax.ppermute(x, 'dp', [(p, p ^ step) for p in range(peer_count)])  4.62 us
  transfers between devices with their start and end apart: 16, of which 5 were waited for; matrix products, arithmetic and copies ran while one was open for 0% of the time, Pallas kernels for 17%

profile of v2, /device:TPU:8, one launch (start us, length us, event | category | flops | bytes accessed | tf_op | source)
XLA Modules:
  0.0 102.2 jit_solution(3992666189199086103)
XLA Ops:
  0.0 2.4 %fusion.8 = (bf16[512,512]{1,0:T(8,128)(2,1)}, bf16[512,512]{1,0:T(8,128)(2,1)}) fusion(bf16[512,1024]{1,0:T(8,128)(2,1)} %refs_4_.3), kind=kLoop, calls=%fused_computation.15 | loop fusion | bytes 2097152 | tf_op jit(solution)/shard_map/slice | solution.py:267
  2.4 1.6 %collective-permute-start.3 = (bf16[512,512]{1,0:T(8,128)(2,1)}, bf16[512,512]{1,0:T(8,128)(2,1)}, u32[]{:S(2)}, u32[]{:S(2)}) collective-permute-start(bf16[512,512]{1,0:T(8,128)(2,1)} %get-tuple-element.21), channel_id=1, source_target_pairs={{0,4},{1,5},{2,6},{3,7},{4,8},{5,9},{6,10},{7,11},{8,12},{9,13},{1... | collective-permute-start | bytes 1572872 | tf_op jit(solution)/shard_map/ppermute | solution.py:258
  4.1 2.3 %shard_map.64 = (bf16[128,2048]{1,0:T(8,128)(2,1)S(1)}, bf16[128,2048]{1,0:T(8,128)(2,1)}, bf16[128,2048]{1,0:T(8,128)(2,1)}, bf16[128,2048]{1,0:T(8,128)(2,1)}) custom-call(s32[3]{0:T(128)S(1)} %pad_add_fusion.where_ref, bf16[128,8192]{1,0:T(8,128)(2,1)S(1)} %copy-done.1), custom_call_target="tpu_custom_call" | custom-call | bytes 4194304 | tf_op jit(solution)/shard_map/pallas_call | solution.py:48
  6.4 0.8 copy-done.2
  7.2 1.6 %collective-permute-start.9 = (bf16[512,512]{1,0:T(8,128)(2,1)}, bf16[512,512]{1,0:T(8,128)(2,1)}, u32[]{:S(2)}, u32[]{:S(2)}) collective-permute-start(bf16[512,512]{1,0:T(8,128)(2,1)} %get-tuple-element.22), channel_id=1, source_target_pairs={{0,4},{1,5},{2,6},{3,7},{4,8},{5,9},{6,10},{7,11},{8,12},{9,13},{1... | collective-permute-start | bytes 1572872 | tf_op jit(solution)/shard_map/ppermute | solution.py:258
  8.7 1.5 %collective-permute-start.1 = (bf16[128,2048]{1,0:T(8,128)(2,1)}, bf16[128,2048]{1,0:T(8,128)(2,1)}, u32[]{:S(2)}, u32[]{:S(2)}) collective-permute-start(bf16[128,2048]{1,0:T(8,128)(2,1)} %get-tuple-element.15), channel_id=1, source_target_pairs={{0,2},{1,3},{2,0},{3,1},{4,6},{5,7},{6,4},{7,5},{8,10},{9,11},{10,... | collective-permute-start | bytes 1572872 | tf_op jit(solution)/shard_map/ppermute | solution.py:264
  10.3 7.2 %collective-permute-done.3.refs_5_.whole_ref = bf16[512,512]{1,0:T(8,128)(2,1)} collective-permute-done((bf16[512,512]{1,0:T(8,128)(2,1)}, bf16[512,512]{1,0:T(8,128)(2,1)}, u32[]{:S(2)}, u32[]{:S(2)}) %collective-permute-start.3) | collective-permute-done | bytes 524320 | tf_op jit(solution)/shard_map/ppermute | solution.py:258
  17.5 1.5 %collective-permute-start.4 = (bf16[512,512]{1,0:T(8,128)(2,1)}, bf16[512,512]{1,0:T(8,128)(2,1)}, u32[]{:S(2)}, u32[]{:S(2)}) collective-permute-start(bf16[512,512]{1,0:T(8,128)(2,1)} %collective-permute-done.3.refs_5_.whole_ref), channel_id=1, source_target_pairs={{0,16},{16,0},{1,17},{17,1},{2,18},{18,2},{3,19},{19,3},{4,20},{20... | collective-permute-start | bytes 1572872 | tf_op jit(solution)/shard_map/ppermute | solution.py:261
  19.0 2.2 %copy-done.6 = bf16[64,64,512]{2,1,0:T(8,128)(2,1)S(1)} copy-done((bf16[64,64,512]{2,1,0:T(8,128)(2,1)S(1)}, bf16[64,64,512]{2,1,0:T(8,128)(2,1)}, u32[]{:S(2)}) %copy-start.6) | copy-done | bytes 4194328
  21.2 3.9 %shard_map.71 = bf16[16,288,128]{2,1,0:T(8,128)(2,1)S(1)} custom-call(s32[16]{0:T(128)S(1)} %copy-done.8, bf16[64,64,512]{2,1,0:T(8,128)(2,1)S(1)} %copy-done.6, bf16[64,64,64]{2,1,0:T(8,128)(2,1)S(1)} %copy-done.7), custom_call_target="tpu_custom_call" | custom-call | bytes 2359296 | tf_op jit(solution)/shard_map/pallas_call | solution.py:97
  25.2 1.0 copy-done.5
  26.2 8.2 %all-to-all-start = ((bf16[16,288,128]{2,1,0:T(8,128)(2,1)}), bf16[16,288,128]{2,1,0:T(8,128)(2,1)}, u32[]{:S(2)}, u32[]{:S(2)}) async-start(bf16[16,288,128]{2,1,0:T(8,128)(2,1)} %copy-done.5), calls=%async_computation | async-start | bytes 2359296 | tf_op jit(solution)/shard_map/all_to_all | solution.py:282
  34.4 1.1 %shard_map.66 = bf16[256,512]{1,0:T(8,128)(2,1)S(1)} custom-call(s32[3]{0:T(128)S(1)} %pad_add_fusion.where_ref, bf16[512,512]{1,0:T(8,128)(2,1)} %collective-permute-done.3.refs_5_.whole_ref), custom_call_target="tpu_custom_call" | custom-call | bytes 786432 | tf_op jit(solution)/shard_map/pallas_call | solution.py:225
  35.5 1.5 %collective-permute-start.5 = (bf16[256,512]{1,0:T(8,128)(2,1)S(1)}, bf16[256,512]{1,0:T(8,128)(2,1)S(1)}, u32[]{:S(2)}, u32[]{:S(2)}) collective-permute-start(bf16[256,512]{1,0:T(8,128)(2,1)S(1)} %shard_map.66), channel_id=1, source_target_pairs={{0,4},{1,5},{2,6},{3,7},{4,8},{5,9},{6,10},{7,11},{8,12},{9,13},{1... | collective-permute-start | bytes 786440 | tf_op jit(solution)/shard_map/ppermute | solution.py:258
  37.0 1.1 %shard_map.69 = bf16[256,512]{1,0:T(8,128)(2,1)S(1)} custom-call(s32[3]{0:T(128)S(1)} %pad_add_fusion.where_ref, bf16[512,512]{1,0:T(8,128)(2,1)} %collective-permute-done.9.refs_5_.whole_ref), custom_call_target="tpu_custom_call" | custom-call | bytes 786432 | tf_op jit(solution)/shard_map/pallas_call | solution.py:225
  38.2 1.5 %collective-permute-start.11 = (bf16[256,512]{1,0:T(8,128)(2,1)S(1)}, bf16[256,512]{1,0:T(8,128)(2,1)S(1)}, u32[]{:S(2)}, u32[]{:S(2)}) collective-permute-start(bf16[256,512]{1,0:T(8,128)(2,1)S(1)} %shard_map.69), channel_id=1, source_target_pairs={{0,4},{1,5},{2,6},{3,7},{4,8},{5,9},{6,10},{7,11},{8,12},{9,13},{1... | collective-permute-start | bytes 786440 | tf_op jit(solution)/shard_map/ppermute | solution.py:258
  39.7 27.0 %collective-permute-done.5.held_ref = bf16[256,512]{1,0:T(8,128)(2,1)S(1)} collective-permute-done((bf16[256,512]{1,0:T(8,128)(2,1)S(1)}, bf16[256,512]{1,0:T(8,128)(2,1)S(1)}, u32[]{:S(2)}, u32[]{:S(2)}) %collective-permute-start.5) | collective-permute-done | bytes 262176 | tf_op jit(solution)/shard_map/ppermute | solution.py:258
  66.7 1.9 %collective-permute-start.6 = (bf16[256,512]{1,0:T(8,128)(2,1)S(1)}, bf16[256,512]{1,0:T(8,128)(2,1)S(1)}, u32[]{:S(2)}, u32[]{:S(2)}) collective-permute-start(bf16[256,512]{1,0:T(8,128)(2,1)S(1)} %collective-permute-done.5.held_ref), channel_id=1, source_target_pairs={{0,16},{16,0},{1,17},{17,1},{2,18},{18,2},{3,19},{19,3},{4,20},{20... | collective-permute-start | bytes 786440 | tf_op jit(solution)/shard_map/ppermute | solution.py:261
  68.6 3.2 %collective-permute-done.11.held_ref = bf16[256,512]{1,0:T(8,128)(2,1)S(1)} collective-permute-done((bf16[256,512]{1,0:T(8,128)(2,1)S(1)}, bf16[256,512]{1,0:T(8,128)(2,1)S(1)}, u32[]{:S(2)}, u32[]{:S(2)}) %collective-permute-start.11) | collective-permute-done | bytes 262176 | tf_op jit(solution)/shard_map/ppermute | solution.py:258
  71.8 1.9 %collective-permute-start.12 = (bf16[256,512]{1,0:T(8,128)(2,1)S(1)}, bf16[256,512]{1,0:T(8,128)(2,1)S(1)}, u32[]{:S(2)}, u32[]{:S(2)}) collective-permute-start(bf16[256,512]{1,0:T(8,128)(2,1)S(1)} %collective-permute-done.11.held_ref), channel_id=1, source_target_pairs={{0,16},{16,0},{1,17},{17,1},{2,18},{18,2},{3,19},{19,3},{4,20},{20... | collective-permute-start | bytes 786440 | tf_op jit(solution)/shard_map/ppermute | solution.py:261
  73.8 1.0 %copy-done.3 = bf16[128,2048]{1,0:T(8,128)(2,1)S(1)} copy-done((bf16[128,2048]{1,0:T(8,128)(2,1)S(1)}, bf16[128,2048]{1,0:T(8,128)(2,1)}, u32[]{:S(2)}) %copy-start.3) | copy-done | bytes 524312
  74.8 2.7 %shard_map.65.total_ref = f32[512,512]{1,0:T(8,128)S(1)} custom-call(bf16[128,2048]{1,0:T(8,128)(2,1)S(1)} %copy-done.3, bf16[128,2048]{1,0:T(8,128)(2,1)} %collective-permute-done.refs_1_.s1, bf16[128,2048]{1,0:T(8,128)(2,1)} %collective-permute-done.1.refs_2_.s2, bf16[128,2048]{1,0:T(8,128)(2,1)} %collective-permute-done.2.refs_3_.s3, ...), custom_call_target="tpu_custom_call" | custom-call | flops 805306368 | bytes 4194304 | tf_op jit(solution)/shard_map/pallas_call | solution.py:171
  77.5 1.8 %shard_map.67 = (f32[2,128,512]{2,1,0:T(8,128)S(1)}, f32[2,128,512]{2,1,0:T(8,128)S(1)}) custom-call(s32[3]{0:T(128)S(1)} %pad_add_fusion.where_ref, bf16[128,2048]{1,0:T(8,128)(2,1)S(1)} %copy-done.4, bf16[128,2048]{1,0:T(8,128)(2,1)} %collective-permute-done.refs_1_.s1, bf16[128,2048]{1,0:T(8,128)(2,1)} %collective-permute-done.1.refs_2_.s2, ...), custom_call_target="tpu_custom_call" | custom-call | flops 268435456 | bytes 4194304 | tf_op jit(solution)/shard_map/pallas_call | solution.py:206
  79.5 2.5 %shard_map.68.total_ref = f32[512,512]{1,0:T(8,128)S(1)} custom-call(bf16[128,2048]{1,0:T(8,128)(2,1)S(1)} %copy-done.4, bf16[128,2048]{1,0:T(8,128)(2,1)} %collective-permute-done.refs_1_.s1, bf16[128,2048]{1,0:T(8,128)(2,1)} %collective-permute-done.1.refs_2_.s2, bf16[128,2048]{1,0:T(8,128)(2,1)} %collective-permute-done.2.refs_3_.s3, ...), custom_call_target="tpu_custom_call" | custom-call | flops 805306368 | bytes 4194304 | tf_op jit(solution)/shard_map/pallas_call | solution.py:171
  82.0 1.8 %shard_map.70 = (f32[2,128,512]{2,1,0:T(8,128)S(1)}, f32[2,128,512]{2,1,0:T(8,128)S(1)}) custom-call(s32[3]{0:T(128)S(1)} %pad_add_fusion.where_ref, bf16[128,2048]{1,0:T(8,128)(2,1)S(1)} %copy-done.4, bf16[128,2048]{1,0:T(8,128)(2,1)} %collective-permute-done.refs_1_.s1, bf16[128,2048]{1,0:T(8,128)(2,1)} %collective-permute-done.1.refs_2_.s2, ...), custom_call_target="tpu_custom_call" | custom-call | flops 268435456 | bytes 4194304 | tf_op jit(solution)/shard_map/pallas_call | solution.py:206
  83.8 0.5 collective-permute-start.13
  85.1 1.6 %collective-permute-start.8 = (f32[128,512]{1,0:T(8,128)S(1)}, f32[128,512]{1,0:T(8,128)S(1)}, u32[]{:S(2)}, u32[]{:S(2)}) collective-permute-start(f32[128,512]{1,0:T(8,128)S(1)} %fusion.5), channel_id=1, source_target_pairs={{0,2},{1,3},{2,0},{3,1},{4,6},{5,7},{6,4},{7,5},{8,10},{9,11},{10,... | collective-permute-start | bytes 786440 | tf_op jit(solution)/shard_map/ppermute | solution.py:264
  86.7 0.8 collective-permute-start.14
  87.6 6.8 %collective-permute-done.8 = f32[128,512]{1,0:T(8,128)S(1)} collective-permute-done((f32[128,512]{1,0:T(8,128)S(1)}, f32[128,512]{1,0:T(8,128)S(1)}, u32[]{:S(2)}, u32[]{:S(2)}) %collective-permute-start.8) | collective-permute-done | bytes 262176 | tf_op jit(solution)/shard_map/ppermute | solution.py:264
  94.4 4.6 %collective-permute-done.14 = f32[128,512]{1,0:T(8,128)S(1)} collective-permute-done((f32[128,512]{1,0:T(8,128)S(1)}, f32[128,512]{1,0:T(8,128)S(1)}, u32[]{:S(2)}, u32[]{:S(2)}) %collective-permute-start.14) | collective-permute-done | bytes 262176 | tf_op jit(solution)/shard_map/ppermute | solution.py:264
  99.1 2.3 %shard_map.72 = f32[128,1024]{1,0:T(8,128)S(1)} custom-call(bf16[128,8192]{1,0:T(8,128)(2,1)S(1)} %copy-done.1, bf16[16,288,128]{2,1,0:T(8,128)(2,1)} %all-to-all-done.packet_ref), custom_call_target="tpu_custom_call" | custom-call | flops 150994944 | bytes 2097152 | tf_op jit(solution)/shard_map/pallas_call | solution.py:136
  101.4 0.8 fusion.1
  (35 shorter events, 0.5 us)
Async XLA Ops:
  0.0 4.1 %copy-start.1 = (bf16[128,8192]{1,0:T(8,128)(2,1)S(1)}, bf16[128,8192]{1,0:T(8,128)(2,1)}, u32[]{:S(2)}) copy-start(bf16[128,8192]{1,0:T(8,128)(2,1)} %tokens_ref.3) | copy-start | bytes 6291460
  0.0 19.0 %copy-start.8 = (s32[16]{0:T(128)S(1)}, s32[16]{0:T(128)}, u32[]{:S(2)}) copy-start(s32[16]{0:T(128)} %chosen_ref.1) | copy-start | bytes 196
  0.0 19.0 %copy-start.7 = (bf16[64,64,64]{2,1,0:T(8,128)(2,1)S(1)}, bf16[64,64,64]{2,1,0:T(8,128)(2,1)}, u32[]{:S(2)}) copy-start(bf16[64,64,64]{2,1,0:T(8,128)(2,1)} %up_ref.1) | copy-start | bytes 1572868
  2.4 15.1 %collective-permute-start.3 = (bf16[512,512]{1,0:T(8,128)(2,1)}, bf16[512,512]{1,0:T(8,128)(2,1)}, u32[]{:S(2)}, u32[]{:S(2)}) collective-permute-start(bf16[512,512]{1,0:T(8,128)(2,1)} %get-tuple-element.21), channel_id=1, source_target_pairs={{0,4},{1,5},{2,6},{3,7},{4,8},{5,9},{6,10},{7,11},{8,12},{9,13},{1... | collective-permute-start | bytes 1572872 | tf_op jit(solution)/shard_map/ppermute | solution.py:258
  6.4 0.8 copy-start.2
  7.2 28.3 %collective-permute-start = (bf16[128,2048]{1,0:T(8,128)(2,1)}, bf16[128,2048]{1,0:T(8,128)(2,1)}, u32[]{:S(2)}, u32[]{:S(2)}) collective-permute-start(bf16[128,2048]{1,0:T(8,128)(2,1)} %get-tuple-element.14), channel_id=1, source_target_pairs={{0,1},{1,0},{2,3},{3,2},{4,5},{5,4},{6,7},{7,6},{8,9},{9,8},{10,11... | collective-permute-start | bytes 1572872 | tf_op jit(solution)/shard_map/ppermute | solution.py:264
  7.2 29.9 %collective-permute-start.9 = (bf16[512,512]{1,0:T(8,128)(2,1)}, bf16[512,512]{1,0:T(8,128)(2,1)}, u32[]{:S(2)}, u32[]{:S(2)}) collective-permute-start(bf16[512,512]{1,0:T(8,128)(2,1)} %get-tuple-element.22), channel_id=1, source_target_pairs={{0,4},{1,5},{2,6},{3,7},{4,8},{5,9},{6,10},{7,11},{8,12},{9,13},{1... | collective-permute-start | bytes 1572872 | tf_op jit(solution)/shard_map/ppermute | solution.py:258
  8.7 29.4 %collective-permute-start.1 = (bf16[128,2048]{1,0:T(8,128)(2,1)}, bf16[128,2048]{1,0:T(8,128)(2,1)}, u32[]{:S(2)}, u32[]{:S(2)}) collective-permute-start(bf16[128,2048]{1,0:T(8,128)(2,1)} %get-tuple-element.15), channel_id=1, source_target_pairs={{0,2},{1,3},{2,0},{3,1},{4,6},{5,7},{6,4},{7,5},{8,10},{9,11},{10,... | collective-permute-start | bytes 1572872 | tf_op jit(solution)/shard_map/ppermute | solution.py:264
  10.3 63.5 %collective-permute-start.2 = (bf16[128,2048]{1,0:T(8,128)(2,1)}, bf16[128,2048]{1,0:T(8,128)(2,1)}, u32[]{:S(2)}, u32[]{:S(2)}) collective-permute-start(bf16[128,2048]{1,0:T(8,128)(2,1)} %get-tuple-element.16), channel_id=1, source_target_pairs={{0,3},{1,2},{2,1},{3,0},{4,7},{5,6},{6,5},{7,4},{8,11},{9,10},{10,... | collective-permute-start | bytes 1572872 | tf_op jit(solution)/shard_map/ppermute | solution.py:264
  17.5 56.2 %collective-permute-start.4 = (bf16[512,512]{1,0:T(8,128)(2,1)}, bf16[512,512]{1,0:T(8,128)(2,1)}, u32[]{:S(2)}, u32[]{:S(2)}) collective-permute-start(bf16[512,512]{1,0:T(8,128)(2,1)} %collective-permute-done.3.refs_5_.whole_ref), channel_id=1, source_target_pairs={{0,16},{16,0},{1,17},{17,1},{2,18},{18,2},{3,19},{19,3},{4,20},{20... | collective-permute-start | bytes 1572872 | tf_op jit(solution)/shard_map/ppermute | solution.py:261
  19.0 2.2 %copy-start.6 = (bf16[64,64,512]{2,1,0:T(8,128)(2,1)S(1)}, bf16[64,64,512]{2,1,0:T(8,128)(2,1)}, u32[]{:S(2)}) copy-start(bf16[64,64,512]{2,1,0:T(8,128)(2,1)} %down_ref.1) | copy-start | bytes 12582916
  25.2 1.0 copy-start.5
  26.2 47.6 %copy-start = (bf16[512,1024]{1,0:T(8,128)(2,1)S(1)}, bf16[512,1024]{1,0:T(8,128)(2,1)}, u32[]{:S(2)}) copy-start(bf16[512,1024]{1,0:T(8,128)(2,1)} %refs_4_.3) | copy-start | bytes 3145732
  26.2 72.9 %all-to-all-start = ((bf16[16,288,128]{2,1,0:T(8,128)(2,1)}), bf16[16,288,128]{2,1,0:T(8,128)(2,1)}, u32[]{:S(2)}, u32[]{:S(2)}) async-start(bf16[16,288,128]{2,1,0:T(8,128)(2,1)} %copy-done.5), calls=%async_computation | async-start | bytes 2359296 | tf_op jit(solution)/shard_map/all_to_all | solution.py:282
  35.5 31.1 %collective-permute-start.5 = (bf16[256,512]{1,0:T(8,128)(2,1)S(1)}, bf16[256,512]{1,0:T(8,128)(2,1)S(1)}, u32[]{:S(2)}, u32[]{:S(2)}) collective-permute-start(bf16[256,512]{1,0:T(8,128)(2,1)S(1)} %shard_map.66), channel_id=1, source_target_pairs={{0,4},{1,5},{2,6},{3,7},{4,8},{5,9},{6,10},{7,11},{8,12},{9,13},{1... | collective-permute-start | bytes 786440 | tf_op jit(solution)/shard_map/ppermute | solution.py:258
  37.0 42.4 %collective-permute-start.10 = (bf16[512,512]{1,0:T(8,128)(2,1)}, bf16[512,512]{1,0:T(8,128)(2,1)S(1)}, u32[]{:S(2)}, u32[]{:S(2)}) collective-permute-start(bf16[512,512]{1,0:T(8,128)(2,1)} %collective-permute-done.9.refs_5_.whole_ref), channel_id=1, source_target_pairs={{0,16},{16,0},{1,17},{17,1},{2,18},{18,2},{3,19},{19,3},{4,20},{20... | collective-permute-start | bytes 1572872 | tf_op jit(solution)/shard_map/ppermute | solution.py:261
  38.2 33.6 %collective-permute-start.11 = (bf16[256,512]{1,0:T(8,128)(2,1)S(1)}, bf16[256,512]{1,0:T(8,128)(2,1)S(1)}, u32[]{:S(2)}, u32[]{:S(2)}) collective-permute-start(bf16[256,512]{1,0:T(8,128)(2,1)S(1)} %shard_map.69), channel_id=1, source_target_pairs={{0,4},{1,5},{2,6},{3,7},{4,8},{5,9},{6,10},{7,11},{8,12},{9,13},{1... | collective-permute-start | bytes 786440 | tf_op jit(solution)/shard_map/ppermute | solution.py:258
  66.7 10.9 %collective-permute-start.6 = (bf16[256,512]{1,0:T(8,128)(2,1)S(1)}, bf16[256,512]{1,0:T(8,128)(2,1)S(1)}, u32[]{:S(2)}, u32[]{:S(2)}) collective-permute-start(bf16[256,512]{1,0:T(8,128)(2,1)S(1)} %collective-permute-done.5.held_ref), channel_id=1, source_target_pairs={{0,16},{16,0},{1,17},{17,1},{2,18},{18,2},{3,19},{19,3},{4,20},{20... | collective-permute-start | bytes 786440 | tf_op jit(solution)/shard_map/ppermute | solution.py:261
  71.8 10.2 %collective-permute-start.12 = (bf16[256,512]{1,0:T(8,128)(2,1)S(1)}, bf16[256,512]{1,0:T(8,128)(2,1)S(1)}, u32[]{:S(2)}, u32[]{:S(2)}) collective-permute-start(bf16[256,512]{1,0:T(8,128)(2,1)S(1)} %collective-permute-done.11.held_ref), channel_id=1, source_target_pairs={{0,16},{16,0},{1,17},{17,1},{2,18},{18,2},{3,19},{19,3},{4,20},{20... | collective-permute-start | bytes 786440 | tf_op jit(solution)/shard_map/ppermute | solution.py:261
  73.8 1.0 %copy-start.3 = (bf16[128,2048]{1,0:T(8,128)(2,1)S(1)}, bf16[128,2048]{1,0:T(8,128)(2,1)}, u32[]{:S(2)}) copy-start(bf16[128,2048]{1,0:T(8,128)(2,1)} %copy-done.2) | copy-start | bytes 1572868
  74.8 2.7 %copy-start.4 = (bf16[128,2048]{1,0:T(8,128)(2,1)S(1)}, bf16[128,2048]{1,0:T(8,128)(2,1)}, u32[]{:S(2)}) copy-start(bf16[128,2048]{1,0:T(8,128)(2,1)} %copy-done.2) | copy-start | bytes 1572868
  79.4 5.7 %collective-permute-start.7 = (f32[2,128,512]{2,1,0:T(8,128)S(1)}, f32[2,128,512]{2,1,0:T(8,128)S(1)}, u32[]{:S(2)}, u32[]{:S(2)}) collective-permute-start(f32[2,128,512]{2,1,0:T(8,128)S(1)} %get-tuple-element.18), channel_id=1, source_target_pairs={{0,1},{1,0},{2,3},{3,2},{4,5},{5,4},{6,7},{7,6},{8,9},{9,8},{10,11... | collective-permute-start | bytes 1572872 | tf_op jit(solution)/shard_map/ppermute | solution.py:264
  83.8 2.8 %collective-permute-start.13 = (f32[2,128,512]{2,1,0:T(8,128)S(1)}, f32[2,128,512]{2,1,0:T(8,128)S(1)}, u32[]{:S(2)}, u32[]{:S(2)}) collective-permute-start(f32[2,128,512]{2,1,0:T(8,128)S(1)} %get-tuple-element.20), channel_id=1, source_target_pairs={{0,1},{1,0},{2,3},{3,2},{4,5},{5,4},{6,7},{7,6},{8,9},{9,8},{10,11... | collective-permute-start | bytes 1572872 | tf_op jit(solution)/shard_map/ppermute | solution.py:264
  85.1 9.2 %collective-permute-start.8 = (f32[128,512]{1,0:T(8,128)S(1)}, f32[128,512]{1,0:T(8,128)S(1)}, u32[]{:S(2)}, u32[]{:S(2)}) collective-permute-start(f32[128,512]{1,0:T(8,128)S(1)} %fusion.5), channel_id=1, source_target_pairs={{0,2},{1,3},{2,0},{3,1},{4,6},{5,7},{6,4},{7,5},{8,10},{9,11},{10,... | collective-permute-start | bytes 786440 | tf_op jit(solution)/shard_map/ppermute | solution.py:264
  86.7 12.3 %collective-permute-start.14 = (f32[128,512]{1,0:T(8,128)S(1)}, f32[128,512]{1,0:T(8,128)S(1)}, u32[]{:S(2)}, u32[]{:S(2)}) collective-permute-start(f32[128,512]{1,0:T(8,128)S(1)} %fusion.2), channel_id=1, source_target_pairs={{0,2},{1,3},{2,0},{3,1},{4,6},{5,7},{6,4},{7,5},{8,10},{9,11},{10,... | collective-permute-start | bytes 786440 | tf_op jit(solution)/shard_map/ppermute | solution.py:264

commit v3 on v2

--- a/solution.py
+++ b/solution.py
@@ -12,15 +12,20 @@
 CHUNKS = 2
 LANES = 128
 ADAPTER_SCALE = 0.5
-VMEM_BYTES = 40 * 2**20
+VMEM_BYTES = 16 * 2**20
+TABLE_VMEM_BYTES = 58 * 2**20
 
 VMEM = pl.BlockSpec(memory_space=pltpu.VMEM)
 SMEM = pl.BlockSpec(memory_space=pltpu.SMEM)
-ANY = pl.BlockSpec(memory_space=pl.ANY)
-
-
-def params():
-    return pltpu.CompilerParams(vmem_limit_bytes=VMEM_BYTES)
+HBM = pl.BlockSpec(memory_space=pltpu.HBM)
+
+
+def params(vmem_bytes=VMEM_BYTES):
+    return pltpu.CompilerParams(vmem_limit_bytes=vmem_bytes)
+
+
+def after(*values):
+    return lax.optimization_barrier(values)
 
 
 def cost(flops, touched):
@@ -43,14 +48,12 @@
 
 def shares_of(where, tokens, ring, depth):
     rows, features = tokens.shape
-    step = 32
-    width = ring * depth
+    share = jax.ShapeDtypeStruct((rows, ring * depth), tokens.dtype)
     return pl.pallas_call(
         functools.partial(share_kernel, ring, depth),
-        grid=(rows // step,),
-        in_specs=[SMEM, pl.BlockSpec((step, features), lambda i: (i, 0))],
-        out_specs=[pl.BlockSpec((step, width), lambda i: (i, 0))] * SQUARE,
-        out_shape=[jax.ShapeDtypeStruct((rows, width), tokens.dtype)] * SQUARE,
+        in_specs=[SMEM, VMEM],
+        out_specs=[VMEM] * SQUARE,
+        out_shape=[share] * SQUARE,
         compiler_params=params(),
         cost_estimate=cost(0, 4 * rows * features),
     )(where, tokens)
@@ -61,7 +64,9 @@
     return depth // LANES, folds, rank // folds
 
 
-def packet_kernel(chosen_ref, down_ref, up_ref, packet_ref, down_held, up_held, sems):
+def packet_kernel(
+    chosen_ref, down_ref, up_ref, packet_ref, down_held, up_held, packed, sems
+):
     blocks, rank, depth = down_held.shape
     width = up_held.shape[2]
     groups, folds, high = packet_sizes(depth, rank, width)
@@ -76,17 +81,23 @@
     for k in range(blocks):
         for copy in copies(k):
             copy.start()
+    def packet(k):
+        return pltpu.make_async_copy(packed.at[k], packet_ref.at[k], sems.at[2, k])
+
     for k in range(blocks):
         for copy in copies(k):
             copy.wait()
         for g in range(groups):
-            packet_ref[k, g * rank : (g + 1) * rank, :] = down_held[
+            packed[k, g * rank : (g + 1) * rank, :] = down_held[
                 k, :, g * LANES : (g + 1) * LANES
             ]
         parts = [up_held[k, f * high : (f + 1) * high, :] for f in range(folds)]
         if folds * width < LANES:
             parts.append(jnp.zeros((high, LANES - folds * width), packet_ref.dtype))
-        packet_ref[k, groups * rank :, :] = jnp.concatenate(parts, axis=1)
+        packed[k, groups * rank :, :] = jnp.concatenate(parts, axis=1)
+        packet(k).start()
+    for k in range(blocks):
+        packet(k).wait()
 
 
 def packets_of(adapter_of_block, down, up):
@@ -96,15 +107,16 @@
     tall = groups * rank + high
     return pl.pallas_call(
         packet_kernel,
-        in_specs=[SMEM, ANY, ANY],
-        out_specs=VMEM,
+        in_specs=[SMEM, HBM, HBM],
+        out_specs=HBM,
         out_shape=jax.ShapeDtypeStruct((blocks, tall, LANES), down.dtype),
         scratch_shapes=[
             pltpu.VMEM((blocks, rank, depth), down.dtype),
             pltpu.VMEM((blocks, rank, width), up.dtype),
-            pltpu.SemaphoreType.DMA((2, blocks)),
+            pltpu.VMEM((blocks, tall, LANES), down.dtype),
+            pltpu.SemaphoreType.DMA((3, blocks)),
         ],
-        compiler_params=params(),
+        compiler_params=params(TABLE_VMEM_BYTES),
         cost_estimate=cost(0, 4 * blocks * tall * LANES),
     )(adapter_of_block, down, up)
 
@@ -147,51 +159,79 @@
     )(tokens, packets)
 
 
+def half_kernel(turn, where_ref, whole_ref, half_ref):
+    half = half_ref.shape[0]
+    start = pl.multiple_of((where_ref[2] ^ turn) * half, half)
+    half_ref[...] = whole_ref[pl.ds(start, half), :]
+
+
+def half_of(where, whole, turn):
+    depth, columns = whole.shape
+    return pl.pallas_call(
+        functools.partial(half_kernel, turn),
+        in_specs=[SMEM, VMEM],
+        out_specs=VMEM,
+        out_shape=jax.ShapeDtypeStruct((depth // 2, columns), whole.dtype),
+        compiler_params=params(),
+        cost_estimate=cost(0, 2 * depth * columns),
+    )(where, whole)
+
+
 def stacked(share_refs, turn, depth):
     return jnp.concatenate(
         [share[:, turn * depth : (turn + 1) * depth] for share in share_refs], axis=0
     )
 
 
-def near_kernel(depth, *refs):
-    shares, weights, total_ref = refs[:SQUARE], refs[SQUARE:-1], refs[-1]
-    total = None
-    for turn, weight in enumerate(weights):
-        term = jnp.dot(
-            stacked(shares, turn, depth), weight[...], preferred_element_type=jnp.float32
+def place_half(weight, side, half_ref):
+    half = half_ref.shape[0]
+    weight[pl.ds(pl.multiple_of(side * half, half), half), :] = half_ref[...]
+
+
+def near_kernel(where_ref, s0, s1, s2, s3, own_ref, *refs):
+    pieces, total_ref, weight = refs[:-2], refs[-2], refs[-1]
+    depth = own_ref.shape[0]
+    shares = (s0, s1, s2, s3)
+    side = where_ref[2]
+    total_ref[...] = jnp.dot(
+        stacked(shares, 0, depth), own_ref[...], preferred_element_type=jnp.float32
+    )
+    for turn in range(len(pieces) // 2):
+        first = lax.rem(side + turn, 2)
+        place_half(weight, first, pieces[2 * turn])
+        place_half(weight, 1 - first, pieces[2 * turn + 1])
+        total_ref[...] += jnp.dot(
+            stacked(shares, turn + 1, depth), weight[...], preferred_element_type=jnp.float32
         )
-        total = term if total is None else total + term
-    total_ref[...] = total
-
-
-def near_of(shares, own, chunk, pieces):
-    depth = own.shape[0]
+
+
+def near_of(where, shares, own, pieces):
+    depth, columns = own.shape
     rows = shares[0].shape[0] * SQUARE
-    columns = own.shape[1] // CHUNKS
-    return pl.pallas_call(
-        functools.partial(near_kernel, depth),
-        grid=(1,),
-        in_specs=[pl.BlockSpec(shares[0].shape, lambda i: (0, 0))] * SQUARE
-        + [pl.BlockSpec((depth, columns), lambda i: (0, chunk))]
-        + [pl.BlockSpec((depth, columns), lambda i: (0, 0))] * len(pieces),
-        out_specs=pl.BlockSpec((rows, columns), lambda i: (0, 0)),
+    turns = 1 + len(pieces) // 2
+    return pl.pallas_call(
+        near_kernel,
+        in_specs=[SMEM] + [VMEM] * (SQUARE + 1 + len(pieces)),
+        out_specs=VMEM,
         out_shape=jax.ShapeDtypeStruct((rows, columns), jnp.float32),
-        compiler_params=params(),
-        cost_estimate=cost(2 * rows * depth * columns * (1 + len(pieces)), 2**22),
-    )(*shares, own, *pieces)
+        scratch_shapes=[pltpu.VMEM((depth, columns), own.dtype)],
+        compiler_params=params(),
+        cost_estimate=cost(2 * rows * depth * columns * turns, 2 * depth * columns * turns),
+    )(where, *shares, own, *pieces)
 
 
 def far_kernel(
-    depth, where_ref, s0, s1, s2, s3, total_ref, held_ref, other_ref, out_ref, keep_ref, weight
+    chunk, where_ref, s0, s1, s2, s3, total_ref, mine_ref, other_ref, out_ref, keep_ref, weight
 ):
-    half = depth // 2
+    half, wide = mine_ref.shape
+    columns = slice(chunk * wide, (chunk + 1) * wide)
     side = where_ref[2]
-    weight[pl.ds(pl.multiple_of(side * half, half), half), :] = held_ref[...]
-    weight[pl.ds(pl.multiple_of((1 - side) * half, half), half), :] = other_ref[...]
-    turn = s0.shape[1] // depth - 1
+    place_half(weight, side, mine_ref)
+    place_half(weight, 1 - side, other_ref)
+    turn = s0.shape[1] // (2 * half) - 1
     rows = s0.shape[0]
-    total = total_ref[...] + jnp.dot(
-        stacked((s0, s1, s2, s3), turn, depth), weight[...], preferred_element_type=jnp.float32
+    total = total_ref[:, columns] + jnp.dot(
+        stacked((s0, s1, s2, s3), turn, 2 * half), weight[...], preferred_element_type=jnp.float32
     )
     keep_ref[0] = total[:rows]
     out_ref[0] = total[rows : 2 * rows]
@@ -199,37 +239,19 @@
     out_ref[1] = total[3 * rows :]
 
 
-def far_of(where, shares, total, held, other):
-    half, columns = held.shape
+def far_of(where, shares, total, mine, other, chunk):
+    half, wide = mine.shape
     rows = shares[0].shape[0]
-    result = jax.ShapeDtypeStruct((2, rows, columns), jnp.float32)
-    return pl.pallas_call(
-        functools.partial(far_kernel, 2 * half),
+    result = jax.ShapeDtypeStruct((2, rows, wide), jnp.float32)
+    return pl.pallas_call(
+        functools.partial(far_kernel, chunk),
         in_specs=[SMEM] + [VMEM] * (SQUARE + 3),
         out_specs=[VMEM] * 2,
         out_shape=[result] * 2,
-        scratch_shapes=[pltpu.VMEM((2 * half, columns), held.dtype)],
-        compiler_params=params(),
-        cost_estimate=cost(2 * SQUARE * rows * 2 * half * columns, 2**22),
-    )(where, *shares, total, held, other)
-
-
-def half_kernel(where_ref, whole_ref, half_ref):
-    half = half_ref.shape[0]
-    start = pl.multiple_of(where_ref[2] * half, half)
-    half_ref[...] = whole_ref[pl.ds(start, half), :]
-
-
-def half_of(where, whole):
-    depth, columns = whole.shape
-    return pl.pallas_call(
-        half_kernel,
-        in_specs=[SMEM, VMEM],
-        out_specs=VMEM,
-        out_shape=jax.ShapeDtypeStruct((depth // 2, columns), whole.dtype),
-        compiler_params=params(),
-        cost_estimate=cost(0, 3 * depth * columns),
-    )(where, whole)
+        scratch_shapes=[pltpu.VMEM((2 * half, wide), mine.dtype)],
+        compiler_params=params(),
+        cost_estimate=cost(2 * SQUARE * rows * 2 * half * wide, 2**22),
+    )(where, *shares, total, mine, other)
 
 
 def per_device(
@@ -263,29 +285,34 @@
     def within(x, step):
         return lax.ppermute(x, "dp", [(p, p ^ step) for p in range(peer_count)])
 
-    wide = columns // CHUNKS
-    held = [value_weight_matrix[:, c * wide : (c + 1) * wide] for c in range(CHUNKS)]
-    pieces = [[] for _ in range(CHUNKS)]
-    for _ in range(ring // 2 - 1):
-        for c in range(CHUNKS):
-            held[c] = along(held[c])
-            pieces[c] += [held[c], across(held[c])]
-    far = []
-    for c in range(CHUNKS):
-        mine = along(half_of(where, held[c]))
-        far.append((mine, across(mine)))
-
-    shares = shares_of(where, tokens, ring, depth)
-    shares = [shares[0]] + [within(shares[m], m) for m in range(1, SQUARE)]
-
+    held = [half_of(where, value_weight_matrix, turn) for turn in range(2)]
+    shares = list(shares_of(where, tokens, ring, depth))
     packets = packets_of(adapter_of_block, adapter_down_weight, adapter_up_weight)
+    shares[1], packets = after(shares[1], packets)
+    for m in range(1, SQUARE - 1):
+        shares[m] = within(shares[m], m)
+
+    pieces = []
+    for hop in range(ring // 2 - 1):
+        held = [along(piece) for piece in held]
+        if hop == 0:
+            held[0], shares[1] = after(held[0], shares[1])
+            held[1], shares[-1] = after(held[1], shares[-1])
+        pieces += held + [across(piece) for piece in held]
+    mine = along(held[0])
+    shares[-1] = within(shares[-1], SQUARE - 1)
+
+    if pieces:
+        packets, pieces[-3] = after(packets, pieces[-3])
     packets = lax.all_to_all(packets, "dp", 0, 0, tiled=True)
     change = change_of(tokens, packets, rank, depth, width)
 
+    total = near_of(where, shares, value_weight_matrix, pieces)
+    wide = columns // CHUNKS
     base = []
     for c in range(CHUNKS):
-        total = near_of(shares, value_weight_matrix, c, pieces[c])
-        outgoing, keep = far_of(where, shares, total, *far[c])
+        part = mine[:, c * wide : (c + 1) * wide]
+        outgoing, keep = far_of(where, shares, total, part, across(part), c)
         incoming = within(outgoing, 1)
         there = within(keep[1] + incoming[1], 2)
         base.append(keep[0] + incoming[0] + there)

time: 103 us -> 78.9 us (0.77)
  the two profiles are of different devices: /device:TPU:8 before, /device:TPU:0 now
where the time goes in v3:
time: 78.9 us; the launch traced here: 78.5 us
  waiting for transfers between devices  33.8 us (43%)
  starting transfers between devices  23.3 us (30%)
  Pallas kernels  14.8 us (19%)
  local copies, waits for them, and re-layouts  3.89 us (5%)
  other arithmetic  1.77 us (2%)
  between operations  0.93 us (1%)
    ppermute x7, waiting for transfers between devices, within(): return lax.ppermute(x, 'dp', [(p, p ^ step) for p in range(peer_count)])  15.9 us
    ppermute x3, waiting for transfers between devices, along(): return lax.ppermute(x, ('groups', 'dp'), onward)  12.5 us
    ppermute x4, starting transfers between devices, across(): return lax.ppermute(x, 'groups', [(g, g ^ 1) for g in range(group_count)])  8.15 us
    all_to_all x1, starting transfers between devices, per_device(): packets = lax.all_to_all(packets, 'dp', 0, 0, tiled=True)  6.72 us
    ppermute x4, waiting for transfers between devices, across(): return lax.ppermute(x, 'groups', [(g, g ^ 1) for g in range(group_count)])  5.41 us
    ppermute x3, starting transfers between devices, along(): return lax.ppermute(x, ('groups', 'dp'), onward)  4.71 us
    pallas_call x1, Pallas kernels, packets_of(): pl.pallas_call(packet_kernel, in_specs=[SMEM, HBM, HBM], out_specs=HBM, o...  3.9 us
    ppermute x7, starting transfers between devices, within(): return lax.ppermute(x, 'dp', [(p, p ^ step) for p in range(peer_count)])  3.68 us
  transfers between devices with their start and end apart: 15, of which 10 were waited for; matrix products, arithmetic and copies ran while one was open for 2% of the time, Pallas kernels for 17%

profile of v3, /device:TPU:0, one launch (start us, length us, event | category | flops | bytes accessed | tf_op | source)
XLA Modules:
  0.0 78.5 jit_solution(10454832551472364982)
XLA Ops:
  0.1 1.2 %copy-done = bf16[512,1024]{1,0:T(8,128)(2,1)S(1)} copy-done((bf16[512,1024]{1,0:T(8,128)(2,1)S(1)}, bf16[512,1024]{1,0:T(8,128)(2,1)}, u32[]{:S(2)}) %copy-start) | copy-done | bytes 1048600
  1.3 0.6 shard_map.65
  1.9 3.1 %collective-permute-start = (bf16[256,1024]{1,0:T(8,128)(2,1)S(1)}, bf16[256,1024]{1,0:T(8,128)(2,1)}, u32[]{:S(2)}, u32[]{:S(2)}) collective-permute-start(bf16[256,1024]{1,0:T(8,128)(2,1)S(1)} %shard_map.65), channel_id=1, source_target_pairs={{0,4},{1,5},{2,6},{3,7},{4,8},{5,9},{6,10},{7,11},{8,12},{9,13},{1... | collective-permute-start | bytes 1572872 | tf_op jit(solution)/shard_map/ppermute | solution.py:280
  5.0 1.6 %copy-done.2 = bf16[128,8192]{1,0:T(8,128)(2,1)S(1)} copy-done((bf16[128,8192]{1,0:T(8,128)(2,1)S(1)}, bf16[128,8192]{1,0:T(8,128)(2,1)}, u32[]{:S(2)}) %copy-start.2) | copy-done | bytes 2097176
  6.6 1.7 %shard_map.64 = (bf16[128,2048]{1,0:T(8,128)(2,1)S(1)}, bf16[128,2048]{1,0:T(8,128)(2,1)S(1)}, bf16[128,2048]{1,0:T(8,128)(2,1)}, bf16[128,2048]{1,0:T(8,128)(2,1)}) custom-call(s32[3]{0:T(128)S(1)} %pad_add_fusion.where_ref, bf16[128,8192]{1,0:T(8,128)(2,1)S(1)} %copy-done.2), custom_call_target="tpu_custom_call" | custom-call | bytes 4194304 | tf_op jit(solution)/shard_map/pallas_call | solution.py:52
  8.3 3.9 %shard_map.66 = bf16[16,288,128]{2,1,0:T(8,128)(2,1)} custom-call(s32[16]{0:T(128)} %chosen_ref.1, bf16[64,64,512]{2,1,0:T(8,128)(2,1)} %down_ref.1, bf16[64,64,64]{2,1,0:T(8,128)(2,1)} %up_ref.1), custom_call_target="tpu_custom_call" | custom-call | bytes 2359296 | tf_op jit(solution)/shard_map/pallas_call | solution.py:108
  12.3 0.6 shard_map.67
  12.8 1.6 %collective-permute-start.3 = (bf16[256,1024]{1,0:T(8,128)(2,1)S(1)}, bf16[256,1024]{1,0:T(8,128)(2,1)}, u32[]{:S(2)}, u32[]{:S(2)}) collective-permute-start(bf16[256,1024]{1,0:T(8,128)(2,1)S(1)} %shard_map.67), channel_id=1, source_target_pairs={{0,4},{1,5},{2,6},{3,7},{4,8},{5,9},{6,10},{7,11},{8,12},{9,13},{1... | collective-permute-start | bytes 1572872 | tf_op jit(solution)/shard_map/ppermute | solution.py:280
  14.5 5.4 %collective-permute-done.refs_0_ = bf16[256,1024]{1,0:T(8,128)(2,1)} collective-permute-done((bf16[256,1024]{1,0:T(8,128)(2,1)S(1)}, bf16[256,1024]{1,0:T(8,128)(2,1)}, u32[]{:S(2)}, u32[]{:S(2)}) %collective-permute-start) | collective-permute-done | bytes 524320 | tf_op jit(solution)/shard_map/ppermute | solution.py:280
  19.9 1.8 %collective-permute-start.2 = (bf16[128,2048]{1,0:T(8,128)(2,1)}, bf16[128,2048]{1,0:T(8,128)(2,1)}, u32[]{:S(2)}, u32[]{:S(2)}) collective-permute-start(bf16[128,2048]{1,0:T(8,128)(2,1)} %get-tuple-element.25), channel_id=1, source_target_pairs={{0,2},{1,3},{2,0},{3,1},{4,6},{5,7},{6,4},{7,5},{8,10},{9,11},{10,... | collective-permute-start | bytes 1572872 | tf_op jit(solution)/shard_map/ppermute | solution.py:286
  21.6 5.1 %collective-permute-start.5 = (bf16[256,1024]{1,0:T(8,128)(2,1)}, bf16[256,1024]{1,0:T(8,128)(2,1)}, u32[]{:S(2)}, u32[]{:S(2)}) collective-permute-start(bf16[256,1024]{1,0:T(8,128)(2,1)} %collective-permute-done.refs_0_), channel_id=1, source_target_pairs={{0,16},{16,0},{1,17},{17,1},{2,18},{18,2},{3,19},{19,3},{4,20},{20... | collective-permute-start | bytes 1572872 | tf_op jit(solution)/shard_map/ppermute | solution.py:283
  26.7 4.4 %collective-permute-done.3.refs_1_ = bf16[256,1024]{1,0:T(8,128)(2,1)} collective-permute-done((bf16[256,1024]{1,0:T(8,128)(2,1)S(1)}, bf16[256,1024]{1,0:T(8,128)(2,1)}, u32[]{:S(2)}, u32[]{:S(2)}) %collective-permute-start.3) | collective-permute-done | bytes 524320 | tf_op jit(solution)/shard_map/ppermute | solution.py:280
  31.1 1.0 %collective-permute-start.6 = (bf16[256,1024]{1,0:T(8,128)(2,1)}, bf16[256,1024]{1,0:T(8,128)(2,1)}, u32[]{:S(2)}, u32[]{:S(2)}) collective-permute-start(bf16[256,1024]{1,0:T(8,128)(2,1)} %collective-permute-done.3.refs_1_), channel_id=1, source_target_pairs={{0,16},{16,0},{1,17},{17,1},{2,18},{18,2},{3,19},{19,3},{4,20},{20... | collective-permute-start | bytes 1572872 | tf_op jit(solution)/shard_map/ppermute | solution.py:283
  32.1 6.7 %all-to-all-start = ((bf16[16,288,128]{2,1,0:T(8,128)(2,1)}), bf16[16,288,128]{2,1,0:T(8,128)(2,1)S(1)}, u32[]{:S(2)}, u32[]{:S(2)}) async-start(bf16[16,288,128]{2,1,0:T(8,128)(2,1)} %shard_map.66), calls=%async_computation | async-start | bytes 2359296 | tf_op jit(solution)/shard_map/all_to_all | solution.py:307
  38.8 2.7 %collective-permute-done.7 = bf16[256,1024]{1,0:T(8,128)(2,1)} collective-permute-done((bf16[256,1024]{1,0:T(8,128)(2,1)}, bf16[256,1024]{1,0:T(8,128)(2,1)}, u32[]{:S(2)}, u32[]{:S(2)}) %collective-permute-start.7) | collective-permute-done | bytes 524320 | tf_op jit(solution)/shard_map/ppermute | solution.py:280
  41.5 1.1 %fusion.8 = (bf16[256,512]{1,0:T(8,128)(2,1)S(1)}, bf16[256,512]{1,0:T(8,128)(2,1)S(1)}) fusion(bf16[256,1024]{1,0:T(8,128)(2,1)} %collective-permute-done.7), kind=kLoop, calls=%fused_computation.15 | loop fusion | bytes 1048576 | tf_op jit(solution)/shard_map/slice | solution.py:314
  42.6 2.0 %collective-permute-start.11 = (bf16[256,512]{1,0:T(8,128)(2,1)S(1)}, bf16[256,512]{1,0:T(8,128)(2,1)S(1)}, u32[]{:S(2)}, u32[]{:S(2)}) collective-permute-start(bf16[256,512]{1,0:T(8,128)(2,1)S(1)} %get-tuple-element.38.mine_ref), channel_id=1, source_target_pairs={{0,16},{16,0},{1,17},{17,1},{2,18},{18,2},{3,19},{19,3},{4,20},{20... | collective-permute-start | bytes 786440 | tf_op jit(solution)/shard_map/ppermute | solution.py:283
  44.7 3.2 %collective-permute-done.4.s3 = bf16[128,2048]{1,0:T(8,128)(2,1)} collective-permute-done((bf16[128,2048]{1,0:T(8,128)(2,1)}, bf16[128,2048]{1,0:T(8,128)(2,1)}, u32[]{:S(2)}, u32[]{:S(2)}) %collective-permute-start.4) | collective-permute-done | bytes 524320 | tf_op jit(solution)/shard_map/ppermute | solution.py:286
  47.9 0.5 collective-permute-done.6.refs_3_
  48.3 3.7 %shard_map.68.total_ref = f32[512,1024]{1,0:T(8,128)S(1)} custom-call(s32[3]{0:T(128)S(1)} %pad_add_fusion.where_ref, bf16[128,2048]{1,0:T(8,128)(2,1)S(1)} %get-tuple-element.21.s0, bf16[128,2048]{1,0:T(8,128)(2,1)S(1)} %collective-permute-done.1.s1, bf16[128,2048]{1,0:T(8,128)(2,1)} %collective-permute-done.2.s2, ...), custom_call_target="tpu_custom_call" | custom-call | flops 1610612736 | bytes 3145728 | tf_op jit(solution)/shard_map/pallas_call | solution.py:212
  52.0 1.8 %collective-permute-done.11.other_ref = bf16[256,512]{1,0:T(8,128)(2,1)S(1)} collective-permute-done((bf16[256,512]{1,0:T(8,128)(2,1)S(1)}, bf16[256,512]{1,0:T(8,128)(2,1)S(1)}, u32[]{:S(2)}, u32[]{:S(2)}) %collective-permute-start.11) | collective-permute-done | bytes 262176 | tf_op jit(solution)/shard_map/ppermute | solution.py:283
  53.9 1.7 %shard_map.70 = (f32[2,128,512]{2,1,0:T(8,128)S(1)}, f32[2,128,512]{2,1,0:T(8,128)S(1)}) custom-call(s32[3]{0:T(128)S(1)} %pad_add_fusion.where_ref, bf16[128,2048]{1,0:T(8,128)(2,1)S(1)} %get-tuple-element.21.s0, bf16[128,2048]{1,0:T(8,128)(2,1)S(1)} %collective-permute-done.1.s1, bf16[128,2048]{1,0:T(8,128)(2,1)} %collective-permute-done.2.s2, ...), custom_call_target="tpu_custom_call" | custom-call | flops 268435456 | bytes 4194304 | tf_op jit(solution)/shard_map/pallas_call | solution.py:246
  55.6 3.1 %collective-permute-done.8.other_ref = bf16[256,512]{1,0:T(8,128)(2,1)S(1)} collective-permute-done((bf16[256,512]{1,0:T(8,128)(2,1)S(1)}, bf16[256,512]{1,0:T(8,128)(2,1)S(1)}, u32[]{:S(2)}, u32[]{:S(2)}) %collective-permute-start.8) | collective-permute-done | bytes 262176 | tf_op jit(solution)/shard_map/ppermute | solution.py:283
  58.7 1.7 %shard_map.69 = (f32[2,128,512]{2,1,0:T(8,128)S(1)}, f32[2,128,512]{2,1,0:T(8,128)S(1)}) custom-call(s32[3]{0:T(128)S(1)} %pad_add_fusion.where_ref, bf16[128,2048]{1,0:T(8,128)(2,1)S(1)} %get-tuple-element.21.s0, bf16[128,2048]{1,0:T(8,128)(2,1)S(1)} %collective-permute-done.1.s1, bf16[128,2048]{1,0:T(8,128)(2,1)} %collective-permute-done.2.s2, ...), custom_call_target="tpu_custom_call" | custom-call | flops 268435456 | bytes 4194304 | tf_op jit(solution)/shard_map/pallas_call | solution.py:246
  61.4 0.6 collective-permute-start.13
  62.0 0.5 collective-permute-done.9
  62.5 1.1 %collective-permute-start.10 = (f32[128,512]{1,0:T(8,128)S(1)}, f32[128,512]{1,0:T(8,128)S(1)}, u32[]{:S(2)}, u32[]{:S(2)}) collective-permute-start(f32[128,512]{1,0:T(8,128)S(1)} %fusion.5), channel_id=1, source_target_pairs={{0,2},{1,3},{2,0},{3,1},{4,6},{5,7},{6,4},{7,5},{8,10},{9,11},{10,... | collective-permute-start | bytes 786440 | tf_op jit(solution)/shard_map/ppermute | solution.py:286
  63.6 7.0 %collective-permute-done.13 = f32[128,512]{1,0:T(8,128)S(1)} collective-permute-done((f32[128,512]{1,0:T(8,128)S(1)}, f32[128,512]{1,0:T(8,128)S(1)}, u32[]{:S(2)}, u32[]{:S(2)}) %collective-permute-start.13) | collective-permute-done | bytes 262176 | tf_op jit(solution)/shard_map/ppermute | solution.py:286
  70.6 5.2 %collective-permute-done.10 = f32[128,512]{1,0:T(8,128)S(1)} collective-permute-done((f32[128,512]{1,0:T(8,128)S(1)}, f32[128,512]{1,0:T(8,128)S(1)}, u32[]{:S(2)}, u32[]{:S(2)}) %collective-permute-start.10) | collective-permute-done | bytes 262176 | tf_op jit(solution)/shard_map/ppermute | solution.py:286
  75.9 0.8 fusion.7
  76.6 1.0 %shard_map.71 = f32[128,1024]{1,0:T(8,128)S(1)} custom-call(bf16[128,8192]{1,0:T(8,128)(2,1)S(1)} %copy-done.3, bf16[16,288,128]{2,1,0:T(8,128)(2,1)S(1)} %all-to-all-done.packet_ref), custom_call_target="tpu_custom_call" | custom-call | flops 150994944 | bytes 2097152 | tf_op jit(solution)/shard_map/pallas_call | solution.py:148
  77.7 0.8 %fusion.1 = bf16[128,1024]{1,0:T(8,128)(2,1)} fusion(f32[128,1024]{1,0:T(8,128)S(1)} %shard_map.71, f32[128,512]{1,0:T(8,128)S(1)} %fusion.4, f32[128,512]{1,0:T(8,128)S(1)} %copy-done.4, pred[128]{0:T(512)(128)(4,1)S(1)} %iota_compare_fusion), kind=kLoop, calls=%fused_computation.2 | loop fusion | flops 524288 | bytes 1310848 | tf_op jit(solution)/shard_map/convert_element_type | solution.py:322
  (24 shorter events, 0.6 us)
Async XLA Ops:
  0.1 1.2 %copy-start = (bf16[512,1024]{1,0:T(8,128)(2,1)S(1)}, bf16[512,1024]{1,0:T(8,128)(2,1)}, u32[]{:S(2)}) copy-start(bf16[512,1024]{1,0:T(8,128)(2,1)} %own_ref.1) | copy-start | bytes 3145732
  1.9 18.0 %collective-permute-start = (bf16[256,1024]{1,0:T(8,128)(2,1)S(1)}, bf16[256,1024]{1,0:T(8,128)(2,1)}, u32[]{:S(2)}, u32[]{:S(2)}) collective-permute-start(bf16[256,1024]{1,0:T(8,128)(2,1)S(1)} %shard_map.65), channel_id=1, source_target_pairs={{0,4},{1,5},{2,6},{3,7},{4,8},{5,9},{6,10},{7,11},{8,12},{9,13},{1... | collective-permute-start | bytes 1572872 | tf_op jit(solution)/shard_map/ppermute | solution.py:280
  5.0 1.6 %copy-start.2 = (bf16[128,8192]{1,0:T(8,128)(2,1)S(1)}, bf16[128,8192]{1,0:T(8,128)(2,1)}, u32[]{:S(2)}) copy-start(bf16[128,8192]{1,0:T(8,128)(2,1)} %tokens_ref.3) | copy-start | bytes 6291460
  8.3 4.0 %copy-start.1 = (bf16[512,1024]{1,0:T(8,128)(2,1)S(1)}, bf16[512,1024]{1,0:T(8,128)(2,1)}, u32[]{:S(2)}) copy-start(bf16[512,1024]{1,0:T(8,128)(2,1)} %own_ref.1) | copy-start | bytes 3145732
  12.2 7.7 %collective-permute-start.1 = (bf16[128,2048]{1,0:T(8,128)(2,1)S(1)}, bf16[128,2048]{1,0:T(8,128)(2,1)S(1)}, u32[]{:S(2)}, u32[]{:S(2)}) collective-permute-start(bf16[128,2048]{1,0:T(8,128)(2,1)S(1)} %get-tuple-element.23), channel_id=1, source_target_pairs={{0,1},{1,0},{2,3},{3,2},{4,5},{5,4},{6,7},{7,6},{8,9},{9,8},{10,11... | collective-permute-start | bytes 1572872 | tf_op jit(solution)/shard_map/ppermute | solution.py:286
  12.8 18.2 %collective-permute-start.3 = (bf16[256,1024]{1,0:T(8,128)(2,1)S(1)}, bf16[256,1024]{1,0:T(8,128)(2,1)}, u32[]{:S(2)}, u32[]{:S(2)}) collective-permute-start(bf16[256,1024]{1,0:T(8,128)(2,1)S(1)} %shard_map.67), channel_id=1, source_target_pairs={{0,4},{1,5},{2,6},{3,7},{4,8},{5,9},{6,10},{7,11},{8,12},{9,13},{1... | collective-permute-start | bytes 1572872 | tf_op jit(solution)/shard_map/ppermute | solution.py:280
  19.9 21.6 %collective-permute-start.7 = (bf16[256,1024]{1,0:T(8,128)(2,1)}, bf16[256,1024]{1,0:T(8,128)(2,1)}, u32[]{:S(2)}, u32[]{:S(2)}) collective-permute-start(bf16[256,1024]{1,0:T(8,128)(2,1)} %collective-permute-done.refs_0_), channel_id=1, source_target_pairs={{0,4},{1,5},{2,6},{3,7},{4,8},{5,9},{6,10},{7,11},{8,12},{9,13},{1... | collective-permute-start | bytes 1572872 | tf_op jit(solution)/shard_map/ppermute | solution.py:280
  19.9 24.7 %collective-permute-start.2 = (bf16[128,2048]{1,0:T(8,128)(2,1)}, bf16[128,2048]{1,0:T(8,128)(2,1)}, u32[]{:S(2)}, u32[]{:S(2)}) collective-permute-start(bf16[128,2048]{1,0:T(8,128)(2,1)} %get-tuple-element.25), channel_id=1, source_target_pairs={{0,2},{1,3},{2,0},{3,1},{4,6},{5,7},{6,4},{7,5},{8,10},{9,11},{10,... | collective-permute-start | bytes 1572872 | tf_op jit(solution)/shard_map/ppermute | solution.py:286
  21.6 26.3 %collective-permute-start.5 = (bf16[256,1024]{1,0:T(8,128)(2,1)}, bf16[256,1024]{1,0:T(8,128)(2,1)}, u32[]{:S(2)}, u32[]{:S(2)}) collective-permute-start(bf16[256,1024]{1,0:T(8,128)(2,1)} %collective-permute-done.refs_0_), channel_id=1, source_target_pairs={{0,16},{16,0},{1,17},{17,1},{2,18},{18,2},{3,19},{19,3},{4,20},{20... | collective-permute-start | bytes 1572872 | tf_op jit(solution)/shard_map/ppermute | solution.py:283
  31.1 16.8 %collective-permute-start.4 = (bf16[128,2048]{1,0:T(8,128)(2,1)}, bf16[128,2048]{1,0:T(8,128)(2,1)}, u32[]{:S(2)}, u32[]{:S(2)}) collective-permute-start(bf16[128,2048]{1,0:T(8,128)(2,1)} %get-tuple-element.27), channel_id=1, source_target_pairs={{0,3},{1,2},{2,1},{3,0},{4,7},{5,6},{6,5},{7,4},{8,11},{9,10},{10,... | collective-permute-start | bytes 1572872 | tf_op jit(solution)/shard_map/ppermute | solution.py:286
  31.1 17.3 %collective-permute-start.6 = (bf16[256,1024]{1,0:T(8,128)(2,1)}, bf16[256,1024]{1,0:T(8,128)(2,1)}, u32[]{:S(2)}, u32[]{:S(2)}) collective-permute-start(bf16[256,1024]{1,0:T(8,128)(2,1)} %collective-permute-done.3.refs_1_), channel_id=1, source_target_pairs={{0,16},{16,0},{1,17},{17,1},{2,18},{18,2},{3,19},{19,3},{4,20},{20... | collective-permute-start | bytes 1572872 | tf_op jit(solution)/shard_map/ppermute | solution.py:283
  32.1 44.6 %all-to-all-start = ((bf16[16,288,128]{2,1,0:T(8,128)(2,1)}), bf16[16,288,128]{2,1,0:T(8,128)(2,1)S(1)}, u32[]{:S(2)}, u32[]{:S(2)}) async-start(bf16[16,288,128]{2,1,0:T(8,128)(2,1)} %shard_map.66), calls=%async_computation | async-start | bytes 2359296 | tf_op jit(solution)/shard_map/all_to_all | solution.py:307
  42.6 11.3 %collective-permute-start.11 = (bf16[256,512]{1,0:T(8,128)(2,1)S(1)}, bf16[256,512]{1,0:T(8,128)(2,1)S(1)}, u32[]{:S(2)}, u32[]{:S(2)}) collective-permute-start(bf16[256,512]{1,0:T(8,128)(2,1)S(1)} %get-tuple-element.38.mine_ref), channel_id=1, source_target_pairs={{0,16},{16,0},{1,17},{17,1},{2,18},{18,2},{3,19},{19,3},{4,20},{20... | collective-permute-start | bytes 786440 | tf_op jit(solution)/shard_map/ppermute | solution.py:283
  44.5 14.2 %collective-permute-start.8 = (bf16[256,512]{1,0:T(8,128)(2,1)S(1)}, bf16[256,512]{1,0:T(8,128)(2,1)S(1)}, u32[]{:S(2)}, u32[]{:S(2)}) collective-permute-start(bf16[256,512]{1,0:T(8,128)(2,1)S(1)} %get-tuple-element.37.mine_ref), channel_id=1, source_target_pairs={{0,16},{16,0},{1,17},{17,1},{2,18},{18,2},{3,19},{19,3},{4,20},{20... | collective-permute-start | bytes 786440 | tf_op jit(solution)/shard_map/ppermute | solution.py:283
  55.5 5.8 %collective-permute-start.12 = (f32[2,128,512]{2,1,0:T(8,128)S(1)}, f32[2,128,512]{2,1,0:T(8,128)S(1)}, u32[]{:S(2)}, u32[]{:S(2)}) collective-permute-start(f32[2,128,512]{2,1,0:T(8,128)S(1)} %get-tuple-element.35), channel_id=1, source_target_pairs={{0,1},{1,0},{2,3},{3,2},{4,5},{5,4},{6,7},{7,6},{8,9},{9,8},{10,11... | collective-permute-start | bytes 1572872 | tf_op jit(solution)/shard_map/ppermute | solution.py:286
  60.4 16.2 %copy-start.3 = (bf16[128,8192]{1,0:T(8,128)(2,1)S(1)}, bf16[128,8192]{1,0:T(8,128)(2,1)}, u32[]{:S(2)}) copy-start(bf16[128,8192]{1,0:T(8,128)(2,1)} %tokens_ref.3) | copy-start | bytes 6291460
  60.5 2.0 %collective-permute-start.9 = (f32[2,128,512]{2,1,0:T(8,128)S(1)}, f32[2,128,512]{2,1,0:T(8,128)S(1)}, u32[]{:S(2)}, u32[]{:S(2)}) collective-permute-start(f32[2,128,512]{2,1,0:T(8,128)S(1)} %get-tuple-element.33), channel_id=1, source_target_pairs={{0,1},{1,0},{2,3},{3,2},{4,5},{5,4},{6,7},{7,6},{8,9},{9,8},{10,11... | collective-permute-start | bytes 1572872 | tf_op jit(solution)/shard_map/ppermute | solution.py:286
  61.4 9.2 %collective-permute-start.13 = (f32[128,512]{1,0:T(8,128)S(1)}, f32[128,512]{1,0:T(8,128)S(1)}, u32[]{:S(2)}, u32[]{:S(2)}) collective-permute-start(f32[128,512]{1,0:T(8,128)S(1)} %fusion.2), channel_id=1, source_target_pairs={{0,2},{1,3},{2,0},{3,1},{4,6},{5,7},{6,4},{7,5},{8,10},{9,11},{10,... | collective-permute-start | bytes 786440 | tf_op jit(solution)/shard_map/ppermute | solution.py:286
  62.5 13.4 %collective-permute-start.10 = (f32[128,512]{1,0:T(8,128)S(1)}, f32[128,512]{1,0:T(8,128)S(1)}, u32[]{:S(2)}, u32[]{:S(2)}) collective-permute-start(f32[128,512]{1,0:T(8,128)S(1)} %fusion.5), channel_id=1, source_target_pairs={{0,2},{1,3},{2,0},{3,1},{4,6},{5,7},{6,4},{7,5},{8,10},{9,11},{10,... | collective-permute-start | bytes 786440 | tf_op jit(solution)/shard_map/ppermute | solution.py:286
  76.6 1.0 %copy-start.4 = (f32[128,512]{1,0:T(8,128)S(1)}, f32[128,512]{1,0:T(8,128)}, u32[]{:S(2)}) copy-start(f32[128,512]{1,0:T(8,128)} %fusion.7) | copy-start | bytes 786436

commit v4 on v3

--- a/solution.py
+++ b/solution.py
@@ -9,7 +9,6 @@
 
 BLOCK = 128
 SQUARE = 4
-CHUNKS = 2
 LANES = 128
 ADAPTER_SCALE = 0.5
 VMEM_BYTES = 16 * 2**20
@@ -155,7 +154,7 @@
             pltpu.VMEM((rank, columns), tokens.dtype),
         ],
         compiler_params=params(),
-        cost_estimate=cost(2 * rows * rank * (features + columns), 2 * rows * features),
+        cost_estimate=cost(2 * rows * rank * (features + columns), 4 * rows * features),
     )(tokens, packets)
 
 
@@ -188,50 +187,52 @@
     weight[pl.ds(pl.multiple_of(side * half, half), half), :] = half_ref[...]
 
 
-def near_kernel(where_ref, s0, s1, s2, s3, own_ref, *refs):
-    pieces, total_ref, weight = refs[:-2], refs[-2], refs[-1]
-    depth = own_ref.shape[0]
+def near_kernel(where_ref, s0, s1, s2, s3, own_ref, mine_ref, *refs):
+    pieces, (total_ref, left_ref, weight) = refs[:-3], refs[-3:]
+    depth = weight.shape[0]
+    half = depth // 2
     shares = (s0, s1, s2, s3)
     side = where_ref[2]
     total_ref[...] = jnp.dot(
         stacked(shares, 0, depth), own_ref[...], preferred_element_type=jnp.float32
     )
-    for turn in range(len(pieces) // 2):
+    turns = len(pieces) // 2
+    for turn in range(turns):
         first = lax.rem(side + turn, 2)
         place_half(weight, first, pieces[2 * turn])
         place_half(weight, 1 - first, pieces[2 * turn + 1])
         total_ref[...] += jnp.dot(
             stacked(shares, turn + 1, depth), weight[...], preferred_element_type=jnp.float32
         )
-
-
-def near_of(where, shares, own, pieces):
+    far = stacked(shares, turns + 1, depth)
+    low, high = far[:, :half], far[:, half:]
+    total_ref[...] += jnp.dot(
+        jnp.where(side == 0, low, high), mine_ref[...], preferred_element_type=jnp.float32
+    )
+    left_ref[...] = jnp.where(side == 0, high, low)
+
+
+def near_of(where, shares, own, mine, pieces):
     depth, columns = own.shape
     rows = shares[0].shape[0] * SQUARE
-    turns = 1 + len(pieces) // 2
     return pl.pallas_call(
         near_kernel,
-        in_specs=[SMEM] + [VMEM] * (SQUARE + 1 + len(pieces)),
-        out_specs=VMEM,
-        out_shape=jax.ShapeDtypeStruct((rows, columns), jnp.float32),
+        in_specs=[SMEM] + [VMEM] * (SQUARE + 2 + len(pieces)),
+        out_specs=[VMEM] * 2,
+        out_shape=[
+            jax.ShapeDtypeStruct((rows, columns), jnp.float32),
+            jax.ShapeDtypeStruct((rows, depth // 2), own.dtype),
+        ],
         scratch_shapes=[pltpu.VMEM((depth, columns), own.dtype)],
         compiler_params=params(),
-        cost_estimate=cost(2 * rows * depth * columns * turns, 2 * depth * columns * turns),
-    )(where, *shares, own, *pieces)
-
-
-def far_kernel(
-    chunk, where_ref, s0, s1, s2, s3, total_ref, mine_ref, other_ref, out_ref, keep_ref, weight
-):
-    half, wide = mine_ref.shape
-    columns = slice(chunk * wide, (chunk + 1) * wide)
-    side = where_ref[2]
-    place_half(weight, side, mine_ref)
-    place_half(weight, 1 - side, other_ref)
-    turn = s0.shape[1] // (2 * half) - 1
-    rows = s0.shape[0]
-    total = total_ref[:, columns] + jnp.dot(
-        stacked((s0, s1, s2, s3), turn, 2 * half), weight[...], preferred_element_type=jnp.float32
+        cost_estimate=cost(2 * rows * depth * columns * (1 + len(pieces) // 2), 8 * rows * columns),
+    )(where, *shares, own, mine, *pieces)
+
+
+def far_kernel(total_ref, left_ref, other_ref, out_ref, keep_ref):
+    rows = out_ref.shape[1]
+    total = total_ref[...] + jnp.dot(
+        left_ref[...], other_ref[...], preferred_element_type=jnp.float32
     )
     keep_ref[0] = total[:rows]
     out_ref[0] = total[rows : 2 * rows]
@@ -239,19 +240,17 @@
     out_ref[1] = total[3 * rows :]
 
 
-def far_of(where, shares, total, mine, other, chunk):
-    half, wide = mine.shape
-    rows = shares[0].shape[0]
-    result = jax.ShapeDtypeStruct((2, rows, wide), jnp.float32)
-    return pl.pallas_call(
-        functools.partial(far_kernel, chunk),
-        in_specs=[SMEM] + [VMEM] * (SQUARE + 3),
+def far_of(total, left, other):
+    rows, columns = total.shape[0] // SQUARE, other.shape[1]
+    result = jax.ShapeDtypeStruct((2, rows, columns), jnp.float32)
+    return pl.pallas_call(
+        far_kernel,
+        in_specs=[VMEM] * 3,
         out_specs=[VMEM] * 2,
         out_shape=[result] * 2,
-        scratch_shapes=[pltpu.VMEM((2 * half, wide), mine.dtype)],
-        compiler_params=params(),
-        cost_estimate=cost(2 * SQUARE * rows * 2 * half * wide, 2**22),
-    )(where, *shares, total, mine, other)
+        compiler_params=params(),
+        cost_estimate=cost(8 * rows * left.shape[1] * columns, 32 * rows * columns),
+    )(total, left, other)
 
 
 def per_device(
@@ -286,38 +285,30 @@
         return lax.ppermute(x, "dp", [(p, p ^ step) for p in range(peer_count)])
 
     held = [half_of(where, value_weight_matrix, turn) for turn in range(2)]
-    shares = list(shares_of(where, tokens, ring, depth))
+    shares = shares_of(where, tokens, ring, depth)
     packets = packets_of(adapter_of_block, adapter_down_weight, adapter_up_weight)
-    shares[1], packets = after(shares[1], packets)
-    for m in range(1, SQUARE - 1):
-        shares[m] = within(shares[m], m)
-
+
+    swapped, packets = after(shares[1], packets)
+    swapped, crossed, slanted = within(swapped, 1), within(shares[2], 2), shares[3]
     pieces = []
     for hop in range(ring // 2 - 1):
         held = [along(piece) for piece in held]
         if hop == 0:
-            held[0], shares[1] = after(held[0], shares[1])
-            held[1], shares[-1] = after(held[1], shares[-1])
+            held[0], swapped = after(held[0], swapped)
+            held[1], slanted = after(held[1], slanted)
+            held[1], packets = after(held[1], packets)
         pieces += held + [across(piece) for piece in held]
     mine = along(held[0])
-    shares[-1] = within(shares[-1], SQUARE - 1)
-
-    if pieces:
-        packets, pieces[-3] = after(packets, pieces[-3])
+    shares = [shares[0], swapped, crossed, within(slanted, 3)]
     packets = lax.all_to_all(packets, "dp", 0, 0, tiled=True)
+
+    total, left = near_of(where, shares, value_weight_matrix, mine, pieces)
+    outgoing, keep = far_of(total, left, across(mine))
+    incoming = within(outgoing, 1)
+    there = (keep[1] + incoming[1]).astype(jnp.bfloat16)
+    base = keep[0] + incoming[0] + within(there, 2).astype(jnp.float32)
+
     change = change_of(tokens, packets, rank, depth, width)
-
-    total = near_of(where, shares, value_weight_matrix, pieces)
-    wide = columns // CHUNKS
-    base = []
-    for c in range(CHUNKS):
-        part = mine[:, c * wide : (c + 1) * wide]
-        outgoing, keep = far_of(where, shares, total, part, across(part), c)
-        incoming = within(outgoing, 1)
-        there = within(keep[1] + incoming[1], 2)
-        base.append(keep[0] + incoming[0] + there)
-    base = jnp.concatenate(base, axis=1)
-
     live_rows = jnp.arange(BLOCK, dtype=jnp.int32)[None, :] < block_live_length[:, None]
     return jnp.where(live_rows.reshape(-1, 1), base + change, 0.0).astype(jnp.bfloat16)
 

time: 78.9 us -> 73.5 us (0.932)
  waiting for transfers between devices: 33.8 us -> 28.7 us
  Pallas kernels: 14.8 us -> 12.1 us
  local copies, waits for them, and re-layouts: 3.89 us -> 6.51 us
    unnamed x10 -> x24, local copies, waits for them, and re-layouts: 2.83 us -> 6.51 us
    ppermute x7 -> x5, waiting for transfers between devices: 15.9 us -> 13.3 us  [within(): return lax.ppermute(x, 'dp', [(p, p ^ step) for p in range(peer_count)])]
    pallas_call x3 -> x2, Pallas kernels: 7.04 us -> 4.38 us  [the longest x1 3.94 us: near_of(): pl.pallas_call(near_kernel, in_specs=[SMEM] + [VMEM] * (SQUARE + 2 + len(...]
    ppermute x3, waiting for transfers between devices: 12.5 us -> 9.8 us  [along(): return lax.ppermute(x, ('groups', 'dp'), onward)]
    slice x1 -> x0, local copies, waits for them, and re-layouts: 1.06 us -> none  [per_device(): part = mine[:, c * wide:(c + 1) * wide]]
    add x4 -> x0, other arithmetic: 0.89 us -> none  [the longest x2 0.81 us: per_device(): base.append(keep[0] + incoming[0] + there)]
    ppermute x7 -> x5, starting transfers between devices: 3.68 us -> 2.81 us  [within(): return lax.ppermute(x, 'dp', [(p, p ^ step) for p in range(peer_count)])]
    convert_element_type x0 -> x1, other arithmetic: none -> 0.86 us  [per_device(): there = (keep[1] + incoming[1]).astype(jnp.bfloat16)]
  transfers between devices with their start and end apart: 15 -> 12, of which waited for: 10 -> 8; matrix products, arithmetic and copies ran while one was open for 2% -> 1% of each run, Pallas kernels for 17% -> 16%
where the time goes in v4:
time: 73.5 us; the launch traced here: 72.7 us
  waiting for transfers between devices  28.7 us (39%)
  starting transfers between devices  22.8 us (31%)
  Pallas kernels  12.1 us (16%)
  local copies, waits for them, and re-layouts  6.51 us (9%)
  other arithmetic  1.75 us (2%)
  between operations  0.81 us (1%)
    ppermute x5, waiting for transfers between devices, within(): return lax.ppermute(x, 'dp', [(p, p ^ step) for p in range(peer_count)])  13.3 us
    ppermute x3, waiting for transfers between devices, along(): return lax.ppermute(x, ('groups', 'dp'), onward)  9.8 us
    ppermute x3, starting transfers between devices, across(): return lax.ppermute(x, 'groups', [(g, g ^ 1) for g in range(group_count)])  8.99 us
    unnamed x24, local copies, waits for them, and re-layouts  6.51 us
    all_to_all x1, starting transfers between devices, per_device(): packets = lax.all_to_all(packets, 'dp', 0, 0, tiled=True)  6.28 us
    ppermute x3, waiting for transfers between devices, across(): return lax.ppermute(x, 'groups', [(g, g ^ 1) for g in range(group_count)])  5.6 us
    ppermute x3, starting transfers between devices, along(): return lax.ppermute(x, ('groups', 'dp'), onward)  4.71 us
    pallas_call x1, Pallas kernels, near_of(): pl.pallas_call(near_kernel, in_specs=[SMEM] + [VMEM] * (SQUARE + 2 + len(...  3.94 us
  transfers between devices with their start and end apart: 12, of which 8 were waited for; matrix products, arithmetic and copies ran while one was open for 1% of the time, Pallas kernels for 16%

profile of v4, /device:TPU:0, one launch (start us, length us, event | category | flops | bytes accessed | tf_op | source)
XLA Modules:
  0.0 72.7 jit_solution(2791084895045711022)
XLA Ops:
  0.1 1.2 %copy-done.2 = bf16[512,1024]{1,0:T(8,128)(2,1)S(1)} copy-done((bf16[512,1024]{1,0:T(8,128)(2,1)S(1)}, bf16[512,1024]{1,0:T(8,128)(2,1)}, u32[]{:S(2)}) %copy-start.2) | copy-done | bytes 1048600
  1.3 0.6 shard_map.65
  1.9 3.1 %collective-permute-start = (bf16[256,1024]{1,0:T(8,128)(2,1)S(1)}, bf16[256,1024]{1,0:T(8,128)(2,1)S(1)}, u32[]{:S(2)}, u32[]{:S(2)}) collective-permute-start(bf16[256,1024]{1,0:T(8,128)(2,1)S(1)} %shard_map.65), channel_id=1, source_target_pairs={{0,4},{1,5},{2,6},{3,7},{4,8},{5,9},{6,10},{7,11},{8,12},{9,13},{1... | collective-permute-start | bytes 1572872 | tf_op jit(solution)/shard_map/ppermute | solution.py:279
  5.0 1.6 %copy-done = bf16[128,8192]{1,0:T(8,128)(2,1)S(1)} copy-done((bf16[128,8192]{1,0:T(8,128)(2,1)S(1)}, bf16[128,8192]{1,0:T(8,128)(2,1)}, u32[]{:S(2)}) %copy-start) | copy-done | bytes 2097176
  6.6 1.7 %shard_map.64 = (bf16[128,2048]{1,0:T(8,128)(2,1)S(1)}, bf16[128,2048]{1,0:T(8,128)(2,1)S(1)}, bf16[128,2048]{1,0:T(8,128)(2,1)}, bf16[128,2048]{1,0:T(8,128)(2,1)}) custom-call(s32[3]{0:T(128)S(1)} %pad_add_fusion.where_ref, bf16[128,8192]{1,0:T(8,128)(2,1)S(1)} %copy-done), custom_call_target="tpu_custom_call" | custom-call | bytes 4194304 | tf_op jit(solution)/shard_map/pallas_call | solution.py:51
  8.3 0.8 %copy-done.6 = bf16[128,2048]{1,0:T(8,128)(2,1)} copy-done((bf16[128,2048]{1,0:T(8,128)(2,1)}, bf16[128,2048]{1,0:T(8,128)(2,1)S(1)}, u32[]{:S(2)}) %copy-start.6) | copy-done | bytes 524312
  9.1 3.9 %shard_map.66 = bf16[16,288,128]{2,1,0:T(8,128)(2,1)} custom-call(s32[16]{0:T(128)} %chosen_ref.1, bf16[64,64,512]{2,1,0:T(8,128)(2,1)} %down_ref.1, bf16[64,64,64]{2,1,0:T(8,128)(2,1)} %up_ref.1), custom_call_target="tpu_custom_call" | custom-call | bytes 2359296 | tf_op jit(solution)/shard_map/pallas_call | solution.py:107
  13.0 0.6 shard_map.67
  13.6 1.6 %collective-permute-start.3 = (bf16[256,1024]{1,0:T(8,128)(2,1)S(1)}, bf16[256,1024]{1,0:T(8,128)(2,1)}, u32[]{:S(2)}, u32[]{:S(2)}) collective-permute-start(bf16[256,1024]{1,0:T(8,128)(2,1)S(1)} %shard_map.67), channel_id=1, source_target_pairs={{0,4},{1,5},{2,6},{3,7},{4,8},{5,9},{6,10},{7,11},{8,12},{9,13},{1... | collective-permute-start | bytes 1572872 | tf_op jit(solution)/shard_map/ppermute | solution.py:279
  15.2 4.0 %collective-permute-done.refs_0_ = bf16[256,1024]{1,0:T(8,128)(2,1)S(1)} collective-permute-done((bf16[256,1024]{1,0:T(8,128)(2,1)S(1)}, bf16[256,1024]{1,0:T(8,128)(2,1)S(1)}, u32[]{:S(2)}, u32[]{:S(2)}) %collective-permute-start) | collective-permute-done | bytes 524320 | tf_op jit(solution)/shard_map/ppermute | solution.py:279
  19.2 0.8 %copy-done.8 = bf16[128,2048]{1,0:T(8,128)(2,1)} copy-done((bf16[128,2048]{1,0:T(8,128)(2,1)}, bf16[128,2048]{1,0:T(8,128)(2,1)S(1)}, u32[]{:S(2)}) %copy-start.8) | copy-done | bytes 524312
  20.0 1.5 %collective-permute-start.2 = (bf16[128,2048]{1,0:T(8,128)(2,1)}, bf16[128,2048]{1,0:T(8,128)(2,1)}, u32[]{:S(2)}, u32[]{:S(2)}) collective-permute-start(bf16[128,2048]{1,0:T(8,128)(2,1)} %get-tuple-element.25), channel_id=1, source_target_pairs={{0,2},{1,3},{2,0},{3,1},{4,6},{5,7},{6,4},{7,5},{8,10},{9,11},{10,... | collective-permute-start | bytes 1572872 | tf_op jit(solution)/shard_map/ppermute | solution.py:285
  21.5 5.9 %collective-permute-start.6 = (bf16[256,1024]{1,0:T(8,128)(2,1)S(1)}, bf16[256,1024]{1,0:T(8,128)(2,1)}, u32[]{:S(2)}, u32[]{:S(2)}) collective-permute-start(bf16[256,1024]{1,0:T(8,128)(2,1)S(1)} %collective-permute-done.refs_0_), channel_id=1, source_target_pairs={{0,16},{16,0},{1,17},{17,1},{2,18},{18,2},{3,19},{19,3},{4,20},{20... | collective-permute-start | bytes 1572872 | tf_op jit(solution)/shard_map/ppermute | solution.py:282
  27.4 3.1 %collective-permute-done.3.refs_1_ = bf16[256,1024]{1,0:T(8,128)(2,1)} collective-permute-done((bf16[256,1024]{1,0:T(8,128)(2,1)S(1)}, bf16[256,1024]{1,0:T(8,128)(2,1)}, u32[]{:S(2)}, u32[]{:S(2)}) %collective-permute-start.3) | collective-permute-done | bytes 524320 | tf_op jit(solution)/shard_map/ppermute | solution.py:279
  30.6 0.6 collective-permute-start.4
  31.2 1.3 %collective-permute-start.7 = (bf16[256,1024]{1,0:T(8,128)(2,1)}, bf16[256,1024]{1,0:T(8,128)(2,1)}, u32[]{:S(2)}, u32[]{:S(2)}) collective-permute-start(bf16[256,1024]{1,0:T(8,128)(2,1)} %collective-permute-done.3.refs_1_), channel_id=1, source_target_pairs={{0,16},{16,0},{1,17},{17,1},{2,18},{18,2},{3,19},{19,3},{4,20},{20... | collective-permute-start | bytes 1572872 | tf_op jit(solution)/shard_map/ppermute | solution.py:282
  32.5 6.3 %all-to-all-start = ((bf16[16,288,128]{2,1,0:T(8,128)(2,1)}), bf16[16,288,128]{2,1,0:T(8,128)(2,1)S(1)}, u32[]{:S(2)}, u32[]{:S(2)}) async-start(bf16[16,288,128]{2,1,0:T(8,128)(2,1)} %shard_map.66), calls=%async_computation | async-start | bytes 2359296 | tf_op jit(solution)/shard_map/all_to_all | solution.py:303
  38.8 2.7 %collective-permute-done.5.mine_ref = bf16[256,1024]{1,0:T(8,128)(2,1)} collective-permute-done((bf16[256,1024]{1,0:T(8,128)(2,1)S(1)}, bf16[256,1024]{1,0:T(8,128)(2,1)}, u32[]{:S(2)}, u32[]{:S(2)}) %collective-permute-start.5) | collective-permute-done | bytes 524320 | tf_op jit(solution)/shard_map/ppermute | solution.py:279
  41.5 1.8 %collective-permute-start.8 = (bf16[256,1024]{1,0:T(8,128)(2,1)}, bf16[256,1024]{1,0:T(8,128)(2,1)S(1)}, u32[]{:S(2)}, u32[]{:S(2)}) collective-permute-start(bf16[256,1024]{1,0:T(8,128)(2,1)} %collective-permute-done.5.mine_ref), channel_id=1, source_target_pairs={{0,16},{16,0},{1,17},{17,1},{2,18},{18,2},{3,19},{19,3},{4,20},{20... | collective-permute-start | bytes 1572872 | tf_op jit(solution)/shard_map/ppermute | solution.py:282
  43.3 4.3 %collective-permute-done.4.s3 = bf16[128,2048]{1,0:T(8,128)(2,1)} collective-permute-done((bf16[128,2048]{1,0:T(8,128)(2,1)}, bf16[128,2048]{1,0:T(8,128)(2,1)}, u32[]{:S(2)}, u32[]{:S(2)}) %collective-permute-start.4) | collective-permute-done | bytes 524320 | tf_op jit(solution)/shard_map/ppermute | solution.py:285
  47.6 2.2 %collective-permute-done.7.refs_3_ = bf16[256,1024]{1,0:T(8,128)(2,1)} collective-permute-done((bf16[256,1024]{1,0:T(8,128)(2,1)}, bf16[256,1024]{1,0:T(8,128)(2,1)}, u32[]{:S(2)}, u32[]{:S(2)}) %collective-permute-start.7) | collective-permute-done | bytes 524320 | tf_op jit(solution)/shard_map/ppermute | solution.py:282
  49.8 1.0 %copy-done.7 = bf16[128,2048]{1,0:T(8,128)(2,1)S(1)} copy-done((bf16[128,2048]{1,0:T(8,128)(2,1)S(1)}, bf16[128,2048]{1,0:T(8,128)(2,1)}, u32[]{:S(2)}) %copy-start.7) | copy-done | bytes 524312
  50.8 1.0 %copy-done.9 = bf16[128,2048]{1,0:T(8,128)(2,1)S(1)} copy-done((bf16[128,2048]{1,0:T(8,128)(2,1)S(1)}, bf16[128,2048]{1,0:T(8,128)(2,1)}, u32[]{:S(2)}) %copy-start.9) | copy-done | bytes 524312
  51.9 3.9 %shard_map.68 = (f32[512,1024]{1,0:T(8,128)S(1)}, bf16[512,256]{1,0:T(8,128)(2,1)S(1)}) custom-call(s32[3]{0:T(128)S(1)} %pad_add_fusion.where_ref, bf16[128,2048]{1,0:T(8,128)(2,1)S(1)} %copy-done.7, bf16[128,2048]{1,0:T(8,128)(2,1)S(1)} %copy-done.9, bf16[128,2048]{1,0:T(8,128)(2,1)} %collective-permute-done.2.s2, ...), custom_call_target="tpu_custom_call" | custom-call | flops 1610612736 | bytes 4194304 | tf_op jit(solution)/shard_map/pallas_call | solution.py:218
  55.8 3.4 %collective-permute-done.8.other_ref = bf16[256,1024]{1,0:T(8,128)(2,1)S(1)} collective-permute-done((bf16[256,1024]{1,0:T(8,128)(2,1)}, bf16[256,1024]{1,0:T(8,128)(2,1)S(1)}, u32[]{:S(2)}, u32[]{:S(2)}) %collective-permute-start.8) | collective-permute-done | bytes 524320 | tf_op jit(solution)/shard_map/ppermute | solution.py:282
  59.2 0.4 shard_map.69
  59.8 2.6 %collective-permute-done.9 = f32[2,128,1024]{2,1,0:T(8,128)S(1)} collective-permute-done((f32[2,128,1024]{2,1,0:T(8,128)S(1)}, f32[2,128,1024]{2,1,0:T(8,128)S(1)}, u32[]{:S(2)}, u32[]{:S(2)}) %collective-permute-start.9) | collective-permute-done | bytes 1048608 | tf_op jit(solution)/shard_map/ppermute | solution.py:285
  62.4 0.9 %fusion.6 = bf16[128,1024]{1,0:T(8,128)(2,1)} fusion(f32[2,128,1024]{2,1,0:T(8,128)S(1)} %collective-permute-done.9, f32[2,128,1024]{2,1,0:T(8,128)S(1)} %get-tuple-element.34), kind=kLoop, calls=%fused_computation.8 | loop fusion | flops 262144 | bytes 1310720 | tf_op jit(solution)/shard_map/convert_element_type | solution.py:308
  63.3 0.5 collective-permute-start.10
  64.5 1.0 %shard_map.70 = f32[128,1024]{1,0:T(8,128)S(1)} custom-call(bf16[128,8192]{1,0:T(8,128)(2,1)S(1)} %copy-done.1, bf16[16,288,128]{2,1,0:T(8,128)(2,1)S(1)} %all-to-all-done.packet_ref), custom_call_target="tpu_custom_call" | custom-call | flops 150994944 | bytes 4194304 | tf_op jit(solution)/shard_map/pallas_call | solution.py:147
  65.5 6.3 %collective-permute-done.10 = bf16[128,1024]{1,0:T(8,128)(2,1)S(1)} collective-permute-done((bf16[128,1024]{1,0:T(8,128)(2,1)}, bf16[128,1024]{1,0:T(8,128)(2,1)S(1)}, u32[]{:S(2)}, u32[]{:S(2)}) %collective-permute-start.10) | collective-permute-done | bytes 262176 | tf_op jit(solution)/shard_map/ppermute | solution.py:285
  71.8 0.8 %fusion.5 = bf16[128,1024]{1,0:T(8,128)(2,1)} fusion(f32[128,1024]{1,0:T(8,128)S(1)} %shard_map.70, f32[2,128,1024]{2,1,0:T(8,128)S(1)} %copy-done.11, bf16[128,1024]{1,0:T(8,128)(2,1)S(1)} %collective-permute-done.10, f32[2,128,1024]{2,1,0:T(8,128)S(1)} %copy-done.5, pred[128]{0:T(512)(128)(4,1)S(1)} %iota_compare_fusion), kind=kLoop, calls=%fused_computation.7 | loop fusion | flops 786432 | bytes 2097280 | tf_op jit(solution)/shard_map/convert_element_type | solution.py:313
  (27 shorter events, 0.3 us)
Async XLA Ops:
  0.1 1.2 %copy-start.2 = (bf16[512,1024]{1,0:T(8,128)(2,1)S(1)}, bf16[512,1024]{1,0:T(8,128)(2,1)}, u32[]{:S(2)}) copy-start(bf16[512,1024]{1,0:T(8,128)(2,1)} %own_ref.1) | copy-start | bytes 3145732
  1.9 17.3 %collective-permute-start = (bf16[256,1024]{1,0:T(8,128)(2,1)S(1)}, bf16[256,1024]{1,0:T(8,128)(2,1)S(1)}, u32[]{:S(2)}, u32[]{:S(2)}) collective-permute-start(bf16[256,1024]{1,0:T(8,128)(2,1)S(1)} %shard_map.65), channel_id=1, source_target_pairs={{0,4},{1,5},{2,6},{3,7},{4,8},{5,9},{6,10},{7,11},{8,12},{9,13},{1... | collective-permute-start | bytes 1572872 | tf_op jit(solution)/shard_map/ppermute | solution.py:279
  5.0 1.6 %copy-start = (bf16[128,8192]{1,0:T(8,128)(2,1)S(1)}, bf16[128,8192]{1,0:T(8,128)(2,1)}, u32[]{:S(2)}) copy-start(bf16[128,8192]{1,0:T(8,128)(2,1)} %tokens_ref.3) | copy-start | bytes 6291460
  8.3 0.8 %copy-start.6 = (bf16[128,2048]{1,0:T(8,128)(2,1)}, bf16[128,2048]{1,0:T(8,128)(2,1)S(1)}, u32[]{:S(2)}) copy-start(bf16[128,2048]{1,0:T(8,128)(2,1)S(1)} %get-tuple-element.21.s0) | copy-start | bytes 1572868
  9.1 4.0 %copy-start.3 = (bf16[512,1024]{1,0:T(8,128)(2,1)S(1)}, bf16[512,1024]{1,0:T(8,128)(2,1)}, u32[]{:S(2)}) copy-start(bf16[512,1024]{1,0:T(8,128)(2,1)} %own_ref.1) | copy-start | bytes 3145732
  12.9 6.3 %collective-permute-start.1 = (bf16[128,2048]{1,0:T(8,128)(2,1)S(1)}, bf16[128,2048]{1,0:T(8,128)(2,1)S(1)}, u32[]{:S(2)}, u32[]{:S(2)}) collective-permute-start(bf16[128,2048]{1,0:T(8,128)(2,1)S(1)} %get-tuple-element.23), channel_id=1, source_target_pairs={{0,1},{1,0},{2,3},{3,2},{4,5},{5,4},{6,7},{7,6},{8,9},{9,8},{10,11... | collective-permute-start | bytes 1572872 | tf_op jit(solution)/shard_map/ppermute | solution.py:285
  13.6 16.9 %collective-permute-start.3 = (bf16[256,1024]{1,0:T(8,128)(2,1)S(1)}, bf16[256,1024]{1,0:T(8,128)(2,1)}, u32[]{:S(2)}, u32[]{:S(2)}) collective-permute-start(bf16[256,1024]{1,0:T(8,128)(2,1)S(1)} %shard_map.67), channel_id=1, source_target_pairs={{0,4},{1,5},{2,6},{3,7},{4,8},{5,9},{6,10},{7,11},{8,12},{9,13},{1... | collective-permute-start | bytes 1572872 | tf_op jit(solution)/shard_map/ppermute | solution.py:279
  19.2 0.8 %copy-start.8 = (bf16[128,2048]{1,0:T(8,128)(2,1)}, bf16[128,2048]{1,0:T(8,128)(2,1)S(1)}, u32[]{:S(2)}) copy-start(bf16[128,2048]{1,0:T(8,128)(2,1)S(1)} %collective-permute-done.1.s1) | copy-start | bytes 1572868
  20.0 21.5 %collective-permute-start.5 = (bf16[256,1024]{1,0:T(8,128)(2,1)S(1)}, bf16[256,1024]{1,0:T(8,128)(2,1)}, u32[]{:S(2)}, u32[]{:S(2)}) collective-permute-start(bf16[256,1024]{1,0:T(8,128)(2,1)S(1)} %collective-permute-done.refs_0_), channel_id=1, source_target_pairs={{0,4},{1,5},{2,6},{3,7},{4,8},{5,9},{6,10},{7,11},{8,12},{9,13},{1... | collective-permute-start | bytes 1572872 | tf_op jit(solution)/shard_map/ppermute | solution.py:279
  20.0 23.3 %collective-permute-start.2 = (bf16[128,2048]{1,0:T(8,128)(2,1)}, bf16[128,2048]{1,0:T(8,128)(2,1)}, u32[]{:S(2)}, u32[]{:S(2)}) collective-permute-start(bf16[128,2048]{1,0:T(8,128)(2,1)} %get-tuple-element.25), channel_id=1, source_target_pairs={{0,2},{1,3},{2,0},{3,1},{4,6},{5,7},{6,4},{7,5},{8,10},{9,11},{10,... | collective-permute-start | bytes 1572872 | tf_op jit(solution)/shard_map/ppermute | solution.py:285
  21.5 26.1 %collective-permute-start.6 = (bf16[256,1024]{1,0:T(8,128)(2,1)S(1)}, bf16[256,1024]{1,0:T(8,128)(2,1)}, u32[]{:S(2)}, u32[]{:S(2)}) collective-permute-start(bf16[256,1024]{1,0:T(8,128)(2,1)S(1)} %collective-permute-done.refs_0_), channel_id=1, source_target_pairs={{0,16},{16,0},{1,17},{17,1},{2,18},{18,2},{3,19},{19,3},{4,20},{20... | collective-permute-start | bytes 1572872 | tf_op jit(solution)/shard_map/ppermute | solution.py:282
  30.6 17.0 %collective-permute-start.4 = (bf16[128,2048]{1,0:T(8,128)(2,1)}, bf16[128,2048]{1,0:T(8,128)(2,1)}, u32[]{:S(2)}, u32[]{:S(2)}) collective-permute-start(bf16[128,2048]{1,0:T(8,128)(2,1)} %get-tuple-element.27), channel_id=1, source_target_pairs={{0,3},{1,2},{2,1},{3,0},{4,7},{5,6},{6,5},{7,4},{8,11},{9,10},{10,... | collective-permute-start | bytes 1572872 | tf_op jit(solution)/shard_map/ppermute | solution.py:285
  31.2 18.6 %collective-permute-start.7 = (bf16[256,1024]{1,0:T(8,128)(2,1)}, bf16[256,1024]{1,0:T(8,128)(2,1)}, u32[]{:S(2)}, u32[]{:S(2)}) collective-permute-start(bf16[256,1024]{1,0:T(8,128)(2,1)} %collective-permute-done.3.refs_1_), channel_id=1, source_target_pairs={{0,16},{16,0},{1,17},{17,1},{2,18},{18,2},{3,19},{19,3},{4,20},{20... | collective-permute-start | bytes 1572872 | tf_op jit(solution)/shard_map/ppermute | solution.py:282
  32.5 32.0 %all-to-all-start = ((bf16[16,288,128]{2,1,0:T(8,128)(2,1)}), bf16[16,288,128]{2,1,0:T(8,128)(2,1)S(1)}, u32[]{:S(2)}, u32[]{:S(2)}) async-start(bf16[16,288,128]{2,1,0:T(8,128)(2,1)} %shard_map.66), calls=%async_computation | async-start | bytes 2359296 | tf_op jit(solution)/shard_map/all_to_all | solution.py:303
  41.5 17.7 %collective-permute-start.8 = (bf16[256,1024]{1,0:T(8,128)(2,1)}, bf16[256,1024]{1,0:T(8,128)(2,1)S(1)}, u32[]{:S(2)}, u32[]{:S(2)}) collective-permute-start(bf16[256,1024]{1,0:T(8,128)(2,1)} %collective-permute-done.5.mine_ref), channel_id=1, source_target_pairs={{0,16},{16,0},{1,17},{17,1},{2,18},{18,2},{3,19},{19,3},{4,20},{20... | collective-permute-start | bytes 1572872 | tf_op jit(solution)/shard_map/ppermute | solution.py:282
  49.8 1.0 %copy-start.7 = (bf16[128,2048]{1,0:T(8,128)(2,1)S(1)}, bf16[128,2048]{1,0:T(8,128)(2,1)}, u32[]{:S(2)}) copy-start(bf16[128,2048]{1,0:T(8,128)(2,1)} %copy-done.6) | copy-start | bytes 1572868
  50.8 1.0 %copy-start.9 = (bf16[128,2048]{1,0:T(8,128)(2,1)S(1)}, bf16[128,2048]{1,0:T(8,128)(2,1)}, u32[]{:S(2)}) copy-start(bf16[128,2048]{1,0:T(8,128)(2,1)} %copy-done.8) | copy-start | bytes 1572868
  59.2 5.2 %copy-start.1 = (bf16[128,8192]{1,0:T(8,128)(2,1)S(1)}, bf16[128,8192]{1,0:T(8,128)(2,1)}, u32[]{:S(2)}) copy-start(bf16[128,8192]{1,0:T(8,128)(2,1)} %tokens_ref.3) | copy-start | bytes 6291460
  59.7 4.8 %copy-start.4 = (f32[2,128,1024]{2,1,0:T(8,128)}, f32[2,128,1024]{2,1,0:T(8,128)S(1)}, u32[]{:S(2)}) copy-start(f32[2,128,1024]{2,1,0:T(8,128)S(1)} %get-tuple-element.34) | copy-start | bytes 3145732
  59.7 2.7 %collective-permute-start.9 = (f32[2,128,1024]{2,1,0:T(8,128)S(1)}, f32[2,128,1024]{2,1,0:T(8,128)S(1)}, u32[]{:S(2)}, u32[]{:S(2)}) collective-permute-start(f32[2,128,1024]{2,1,0:T(8,128)S(1)} %get-tuple-element.35), channel_id=1, source_target_pairs={{0,1},{1,0},{2,3},{3,2},{4,5},{5,4},{6,7},{7,6},{8,9},{9,8},{10,11... | collective-permute-start | bytes 3145736 | tf_op jit(solution)/shard_map/ppermute | solution.py:285
  62.4 2.0 %copy-start.10 = (f32[2,128,1024]{2,1,0:T(8,128)}, f32[2,128,1024]{2,1,0:T(8,128)S(1)}, u32[]{:S(2)}) copy-start(f32[2,128,1024]{2,1,0:T(8,128)S(1)} %collective-permute-done.9) | copy-start | bytes 3145732
  63.3 8.6 %collective-permute-start.10 = (bf16[128,1024]{1,0:T(8,128)(2,1)}, bf16[128,1024]{1,0:T(8,128)(2,1)S(1)}, u32[]{:S(2)}, u32[]{:S(2)}) collective-permute-start(bf16[128,1024]{1,0:T(8,128)(2,1)} %fusion.6), channel_id=1, source_target_pairs={{0,2},{1,3},{2,0},{3,1},{4,6},{5,7},{6,4},{7,5},{8,10},{9,11},{10,... | collective-permute-start | bytes 786440 | tf_op jit(solution)/shard_map/ppermute | solution.py:285
  64.5 7.3 %copy-start.5 = (f32[2,128,1024]{2,1,0:T(8,128)S(1)}, f32[2,128,1024]{2,1,0:T(8,128)}, u32[]{:S(2)}) copy-start(f32[2,128,1024]{2,1,0:T(8,128)} %copy-done.4) | copy-start | bytes 3145732
  64.5 7.3 %copy-start.11 = (f32[2,128,1024]{2,1,0:T(8,128)S(1)}, f32[2,128,1024]{2,1,0:T(8,128)}, u32[]{:S(2)}) copy-start(f32[2,128,1024]{2,1,0:T(8,128)} %copy-done.10) | copy-start | bytes 3145732

commit v5 on v4

--- a/solution.py
+++ b/solution.py
@@ -9,6 +9,15 @@
 
 BLOCK = 128
 SQUARE = 4
+WORK = {
+    "half": 0.0,
+    "share": 4.0,
+    "packet": 0.0,
+    "near": 16.0,
+    "far": 0.1,
+    "join": 2.0,
+    "change": 2.0,
+}
 LANES = 128
 ADAPTER_SCALE = 0.5
 VMEM_BYTES = 16 * 2**20
@@ -27,7 +36,8 @@
     return lax.optimization_barrier(values)
 
 
-def cost(flops, touched):
+def cost(step, touched):
+    flops = int(WORK[step] * 1e9)
     return pl.CostEstimate(flops=flops, bytes_accessed=touched, transcendentals=0)
 
 
@@ -54,7 +64,7 @@
         out_specs=[VMEM] * SQUARE,
         out_shape=[share] * SQUARE,
         compiler_params=params(),
-        cost_estimate=cost(0, 4 * rows * features),
+        cost_estimate=cost("share", 4 * rows * features),
     )(where, tokens)
 
 
@@ -116,7 +126,7 @@
             pltpu.SemaphoreType.DMA((3, blocks)),
         ],
         compiler_params=params(TABLE_VMEM_BYTES),
-        cost_estimate=cost(0, 4 * blocks * tall * LANES),
+        cost_estimate=cost("packet", 4 * blocks * tall * LANES),
     )(adapter_of_block, down, up)
 
 
@@ -154,7 +164,7 @@
             pltpu.VMEM((rank, columns), tokens.dtype),
         ],
         compiler_params=params(),
-        cost_estimate=cost(2 * rows * rank * (features + columns), 4 * rows * features),
+        cost_estimate=cost("change", 4 * rows * features),
     )(tokens, packets)
 
 
@@ -172,7 +182,7 @@
         out_specs=VMEM,
         out_shape=jax.ShapeDtypeStruct((depth // 2, columns), whole.dtype),
         compiler_params=params(),
-        cost_estimate=cost(0, 2 * depth * columns),
+        cost_estimate=cost("half", 2 * depth * columns),
     )(where, whole)
 
 
@@ -225,7 +235,7 @@
         ],
         scratch_shapes=[pltpu.VMEM((depth, columns), own.dtype)],
         compiler_params=params(),
-        cost_estimate=cost(2 * rows * depth * columns * (1 + len(pieces) // 2), 8 * rows * columns),
+        cost_estimate=cost("near", 8 * rows * columns),
     )(where, *shares, own, mine, *pieces)
 
 
@@ -249,8 +259,28 @@
         out_specs=[VMEM] * 2,
         out_shape=[result] * 2,
         compiler_params=params(),
-        cost_estimate=cost(8 * rows * left.shape[1] * columns, 32 * rows * columns),
+        cost_estimate=cost("far", 32 * rows * columns),
     )(total, left, other)
+
+
+def join_kernel(keep_ref, incoming_ref, there_ref, here_ref):
+    there_ref[...] = (keep_ref[1] + incoming_ref[1]).astype(there_ref.dtype)
+    here_ref[...] = keep_ref[0] + incoming_ref[0]
+
+
+def join_of(keep, incoming):
+    rows, columns = keep.shape[1:]
+    return pl.pallas_call(
+        join_kernel,
+        in_specs=[VMEM] * 2,
+        out_specs=[VMEM] * 2,
+        out_shape=[
+            jax.ShapeDtypeStruct((rows, columns), jnp.bfloat16),
+            jax.ShapeDtypeStruct((rows, columns), jnp.float32),
+        ],
+        compiler_params=params(),
+        cost_estimate=cost("join", 22 * rows * columns),
+    )(keep, incoming)
 
 
 def per_device(
@@ -288,25 +318,25 @@
     shares = shares_of(where, tokens, ring, depth)
     packets = packets_of(adapter_of_block, adapter_down_weight, adapter_up_weight)
 
-    swapped, packets = after(shares[1], packets)
-    swapped, crossed, slanted = within(swapped, 1), within(shares[2], 2), shares[3]
+    swapped, crossed, slanted = shares[1:]
+    swapped, packets = after(swapped, packets)
+    swapped, crossed = within(swapped, 1), within(crossed, 2)
     pieces = []
     for hop in range(ring // 2 - 1):
         held = [along(piece) for piece in held]
         if hop == 0:
             held[0], swapped = after(held[0], swapped)
-            held[1], slanted = after(held[1], slanted)
-            held[1], packets = after(held[1], packets)
+            held[1], slanted, packets = after(held[1], slanted, packets)
         pieces += held + [across(piece) for piece in held]
-    mine = along(held[0])
+    mine, crossed = after(along(held[0]), crossed)
     shares = [shares[0], swapped, crossed, within(slanted, 3)]
     packets = lax.all_to_all(packets, "dp", 0, 0, tiled=True)
 
     total, left = near_of(where, shares, value_weight_matrix, mine, pieces)
     outgoing, keep = far_of(total, left, across(mine))
     incoming = within(outgoing, 1)
-    there = (keep[1] + incoming[1]).astype(jnp.bfloat16)
-    base = keep[0] + incoming[0] + within(there, 2).astype(jnp.float32)
+    there, here = join_of(keep, incoming)
+    base = here + within(there, 2).astype(jnp.float32)
 
     change = change_of(tokens, packets, rank, depth, width)
     live_rows = jnp.arange(BLOCK, dtype=jnp.int32)[None, :] < block_live_length[:, None]

time: 73.5 us -> 71.2 us (0.969)
  waiting for transfers between devices: 28.7 us -> 27.6 us
  local copies, waits for them, and re-layouts: 6.51 us -> 5.46 us
  starting transfers between devices: 22.8 us -> 23.7 us
  other arithmetic: 1.75 us -> 0.88 us
    ppermute x5, waiting for transfers between devices: 13.3 us -> 9.77 us  [within(): return lax.ppermute(x, 'dp', [(p, p ^ step) for p in range(peer_count)])]
    ppermute x3, waiting for transfers between devices: 9.8 us -> 12.3 us  [along(): return lax.ppermute(x, ('groups', 'dp'), onward)]
    ppermute x3, waiting for transfers between devices: 5.6 us -> 3.58 us  [across(): return lax.ppermute(x, 'groups', [(g, g ^ 1) for g in range(group_count)])]
    all_to_all x1, waiting for transfers between devices: 0.01 us -> 1.94 us  [per_device(): packets = lax.all_to_all(packets, 'dp', 0, 0, tiled=True)]
    ppermute x5, starting transfers between devices: 2.81 us -> 4.21 us  [within(): return lax.ppermute(x, 'dp', [(p, p ^ step) for p in range(peer_count)])]
    unnamed x24 -> x12, local copies, waits for them, and re-layouts: 6.51 us -> 5.46 us
    ppermute x3, starting transfers between devices: 8.99 us -> 8.1 us  [across(): return lax.ppermute(x, 'groups', [(g, g ^ 1) for g in range(group_count)])]
    convert_element_type x1 -> x0, other arithmetic: 0.86 us -> none  [per_device(): there = (keep[1] + incoming[1]).astype(jnp.bfloat16)]
  transfers between devices with their start and end apart: 12 -> 12, of which waited for: 8 -> 8; matrix products, arithmetic and copies ran while one was open for 1% -> 0% of each run, Pallas kernels for 16% -> 17%
where the time goes in v5:
time: 71.2 us; the launch traced here: 70.8 us
  waiting for transfers between devices  27.6 us (39%)
  starting transfers between devices  23.7 us (33%)
  Pallas kernels  12.4 us (17%)
  local copies, waits for them, and re-layouts  5.46 us (8%)
  other arithmetic  0.88 us (1%)
  between operations  0.76 us (1%)
    ppermute x3, waiting for transfers between devices, along(): return lax.ppermute(x, ('groups', 'dp'), onward)  12.3 us
    ppermute x5, waiting for transfers between devices, within(): return lax.ppermute(x, 'dp', [(p, p ^ step) for p in range(peer_count)])  9.77 us
    ppermute x3, starting transfers between devices, across(): return lax.ppermute(x, 'groups', [(g, g ^ 1) for g in range(group_count)])  8.1 us
    all_to_all x1, starting transfers between devices, per_device(): packets = lax.all_to_all(packets, 'dp', 0, 0, tiled=True)  6.72 us
    unnamed x12, local copies, waits for them, and re-layouts  5.46 us
    ppermute x3, starting transfers between devices, along(): return lax.ppermute(x, ('groups', 'dp'), onward)  4.71 us
    ppermute x5, starting transfers between devices, within(): return lax.ppermute(x, 'dp', [(p, p ^ step) for p in range(peer_count)])  4.21 us
    pallas_call x1, Pallas kernels, packets_of(): pl.pallas_call(packet_kernel, in_specs=[SMEM, HBM, HBM], out_specs=HBM, o...  4.02 us
  transfers between devices with their start and end apart: 12, of which 8 were waited for; matrix products, arithmetic and copies ran while one was open for 0% of the time, Pallas kernels for 17%

profile of v5, /device:TPU:0, one launch (start us, length us, event | category | flops | bytes accessed | tf_op | source)
XLA Modules:
  0.0 70.8 jit_solution(16084958532897416391)
XLA Ops:
  0.0 0.1 pad_add_fusion.where_ref
  0.1 1.2 %copy-done = bf16[512,1024]{1,0:T(8,128)(2,1)S(1)} copy-done((bf16[512,1024]{1,0:T(8,128)(2,1)S(1)}, bf16[512,1024]{1,0:T(8,128)(2,1)}, u32[]{:S(2)}) %copy-start) | copy-done | bytes 1048600
  1.3 0.6 shard_map.65
  1.9 3.1 %collective-permute-start = (bf16[256,1024]{1,0:T(8,128)(2,1)S(1)}, bf16[256,1024]{1,0:T(8,128)(2,1)S(1)}, u32[]{:S(2)}, u32[]{:S(2)}) collective-permute-start(bf16[256,1024]{1,0:T(8,128)(2,1)S(1)} %shard_map.65), channel_id=1, source_target_pairs={{0,4},{1,5},{2,6},{3,7},{4,8},{5,9},{6,10},{7,11},{8,12},{9,13},{1... | collective-permute-start | bytes 1572872 | tf_op jit(solution)/shard_map/ppermute | solution.py:309
  5.0 1.6 %copy-done.2 = bf16[128,8192]{1,0:T(8,128)(2,1)S(1)} copy-done((bf16[128,8192]{1,0:T(8,128)(2,1)S(1)}, bf16[128,8192]{1,0:T(8,128)(2,1)}, u32[]{:S(2)}) %copy-start.2) | copy-done | bytes 2097176
  6.6 1.7 %shard_map.64 = (bf16[128,2048]{1,0:T(8,128)(2,1)S(1)}, bf16[128,2048]{1,0:T(8,128)(2,1)S(1)}, bf16[128,2048]{1,0:T(8,128)(2,1)}, bf16[128,2048]{1,0:T(8,128)(2,1)}) custom-call(s32[3]{0:T(128)S(1)} %pad_add_fusion.where_ref, bf16[128,8192]{1,0:T(8,128)(2,1)S(1)} %copy-done.2), custom_call_target="tpu_custom_call" | custom-call | flops 4000000000 | bytes 4194304 | tf_op jit(solution)/shard_map/pallas_call | solution.py:61
  8.3 4.0 %shard_map.66 = bf16[16,288,128]{2,1,0:T(8,128)(2,1)} custom-call(s32[16]{0:T(128)} %chosen_ref.1, bf16[64,64,512]{2,1,0:T(8,128)(2,1)} %down_ref.1, bf16[64,64,64]{2,1,0:T(8,128)(2,1)} %up_ref.1), custom_call_target="tpu_custom_call" | custom-call | bytes 2359296 | tf_op jit(solution)/shard_map/pallas_call | solution.py:117
  12.3 0.1 collective-permute-start.1
  12.4 0.6 shard_map.67
  13.0 1.6 %collective-permute-start.4 = (bf16[256,1024]{1,0:T(8,128)(2,1)S(1)}, bf16[256,1024]{1,0:T(8,128)(2,1)}, u32[]{:S(2)}, u32[]{:S(2)}) collective-permute-start(bf16[256,1024]{1,0:T(8,128)(2,1)S(1)} %shard_map.67), channel_id=1, source_target_pairs={{0,4},{1,5},{2,6},{3,7},{4,8},{5,9},{6,10},{7,11},{8,12},{9,13},{1... | collective-permute-start | bytes 1572872 | tf_op jit(solution)/shard_map/ppermute | solution.py:309
  14.6 1.5 %collective-permute-start.3 = (bf16[128,2048]{1,0:T(8,128)(2,1)}, bf16[128,2048]{1,0:T(8,128)(2,1)}, u32[]{:S(2)}, u32[]{:S(2)}) collective-permute-start(bf16[128,2048]{1,0:T(8,128)(2,1)} %get-tuple-element.29), channel_id=1, source_target_pairs={{0,2},{1,3},{2,0},{3,1},{4,6},{5,7},{6,4},{7,5},{8,10},{9,11},{10,... | collective-permute-start | bytes 1572872 | tf_op jit(solution)/shard_map/ppermute | solution.py:315
  16.1 3.6 %collective-permute-done.refs_0_ = bf16[256,1024]{1,0:T(8,128)(2,1)S(1)} collective-permute-done((bf16[256,1024]{1,0:T(8,128)(2,1)S(1)}, bf16[256,1024]{1,0:T(8,128)(2,1)S(1)}, u32[]{:S(2)}, u32[]{:S(2)}) %collective-permute-start) | collective-permute-done | bytes 524320 | tf_op jit(solution)/shard_map/ppermute | solution.py:309
  19.8 5.3 %collective-permute-start.6 = (bf16[256,1024]{1,0:T(8,128)(2,1)S(1)}, bf16[256,1024]{1,0:T(8,128)(2,1)}, u32[]{:S(2)}, u32[]{:S(2)}) collective-permute-start(bf16[256,1024]{1,0:T(8,128)(2,1)S(1)} %collective-permute-done.refs_0_), channel_id=1, source_target_pairs={{0,16},{16,0},{1,17},{17,1},{2,18},{18,2},{3,19},{19,3},{4,20},{20... | collective-permute-start | bytes 1572872 | tf_op jit(solution)/shard_map/ppermute | solution.py:312
  25.1 6.0 %collective-permute-done.4.refs_1_ = bf16[256,1024]{1,0:T(8,128)(2,1)} collective-permute-done((bf16[256,1024]{1,0:T(8,128)(2,1)S(1)}, bf16[256,1024]{1,0:T(8,128)(2,1)}, u32[]{:S(2)}, u32[]{:S(2)}) %collective-permute-start.4) | collective-permute-done | bytes 524320 | tf_op jit(solution)/shard_map/ppermute | solution.py:309
  31.1 1.0 %collective-permute-start.7 = (bf16[256,1024]{1,0:T(8,128)(2,1)}, bf16[256,1024]{1,0:T(8,128)(2,1)}, u32[]{:S(2)}, u32[]{:S(2)}) collective-permute-start(bf16[256,1024]{1,0:T(8,128)(2,1)} %collective-permute-done.4.refs_1_), channel_id=1, source_target_pairs={{0,16},{16,0},{1,17},{17,1},{2,18},{18,2},{3,19},{19,3},{4,20},{20... | collective-permute-start | bytes 1572872 | tf_op jit(solution)/shard_map/ppermute | solution.py:312
  32.1 6.7 %all-to-all-start = ((bf16[16,288,128]{2,1,0:T(8,128)(2,1)}), bf16[16,288,128]{2,1,0:T(8,128)(2,1)S(1)}, u32[]{:S(2)}, u32[]{:S(2)}) async-start(bf16[16,288,128]{2,1,0:T(8,128)(2,1)} %shard_map.66), calls=%async_computation | async-start | bytes 2359296 | tf_op jit(solution)/shard_map/all_to_all | solution.py:333
  38.8 2.7 %collective-permute-done.2.mine_ref = bf16[256,1024]{1,0:T(8,128)(2,1)} collective-permute-done((bf16[256,1024]{1,0:T(8,128)(2,1)S(1)}, bf16[256,1024]{1,0:T(8,128)(2,1)}, u32[]{:S(2)}, u32[]{:S(2)}) %collective-permute-start.2) | collective-permute-done | bytes 524320 | tf_op jit(solution)/shard_map/ppermute | solution.py:309
  41.5 1.8 %collective-permute-start.8 = (bf16[256,1024]{1,0:T(8,128)(2,1)}, bf16[256,1024]{1,0:T(8,128)(2,1)S(1)}, u32[]{:S(2)}, u32[]{:S(2)}) collective-permute-start(bf16[256,1024]{1,0:T(8,128)(2,1)} %collective-permute-done.2.mine_ref), channel_id=1, source_target_pairs={{0,16},{16,0},{1,17},{17,1},{2,18},{18,2},{3,19},{19,3},{4,20},{20... | collective-permute-start | bytes 1572872 | tf_op jit(solution)/shard_map/ppermute | solution.py:312
  43.3 4.7 %collective-permute-done.5.s3 = bf16[128,2048]{1,0:T(8,128)(2,1)} collective-permute-done((bf16[128,2048]{1,0:T(8,128)(2,1)}, bf16[128,2048]{1,0:T(8,128)(2,1)}, u32[]{:S(2)}, u32[]{:S(2)}) %collective-permute-start.5) | collective-permute-done | bytes 524320 | tf_op jit(solution)/shard_map/ppermute | solution.py:315
  48.0 1.0 %copy-done.5 = bf16[128,2048]{1,0:T(8,128)(2,1)S(1)} copy-done((bf16[128,2048]{1,0:T(8,128)(2,1)S(1)}, bf16[128,2048]{1,0:T(8,128)(2,1)}, u32[]{:S(2)}) %copy-start.5) | copy-done | bytes 524312
  49.1 3.9 %shard_map.68 = (f32[512,1024]{1,0:T(8,128)S(1)}, bf16[512,256]{1,0:T(8,128)(2,1)S(1)}) custom-call(s32[3]{0:T(128)S(1)} %pad_add_fusion.where_ref, bf16[128,2048]{1,0:T(8,128)(2,1)S(1)} %copy-done.5, bf16[128,2048]{1,0:T(8,128)(2,1)S(1)} %collective-permute-done.1.s1, bf16[128,2048]{1,0:T(8,128)(2,1)} %collective-permute-done.3.s2, ...), custom_call_target="tpu_custom_call" | custom-call | flops 16000000000 | bytes 4194304 | tf_op jit(solution)/shard_map/pallas_call | solution.py:228
  53.0 3.6 %collective-permute-done.8.other_ref = bf16[256,1024]{1,0:T(8,128)(2,1)S(1)} collective-permute-done((bf16[256,1024]{1,0:T(8,128)(2,1)}, bf16[256,1024]{1,0:T(8,128)(2,1)S(1)}, u32[]{:S(2)}, u32[]{:S(2)}) %collective-permute-start.8) | collective-permute-done | bytes 524320 | tf_op jit(solution)/shard_map/ppermute | solution.py:312
  56.6 0.4 shard_map.69
  57.0 0.6 collective-permute-start.9
  58.3 1.6 %collective-permute-done.9.incoming_ref = f32[2,128,1024]{2,1,0:T(8,128)S(1)} collective-permute-done((f32[2,128,1024]{2,1,0:T(8,128)S(1)}, f32[2,128,1024]{2,1,0:T(8,128)S(1)}, u32[]{:S(2)}, u32[]{:S(2)}) %collective-permute-start.9) | collective-permute-done | bytes 1048608 | tf_op jit(solution)/shard_map/ppermute | solution.py:315
  60.0 0.1 shard_map.70
  60.1 2.0 %collective-permute-start.10 = (bf16[128,1024]{1,0:T(8,128)(2,1)S(1)}, bf16[128,1024]{1,0:T(8,128)(2,1)S(1)}, u32[]{:S(2)}, u32[]{:S(2)}) collective-permute-start(bf16[128,1024]{1,0:T(8,128)(2,1)S(1)} %get-tuple-element.41), channel_id=1, source_target_pairs={{0,2},{1,3},{2,0},{3,1},{4,6},{5,7},{6,4},{7,5},{8,10},{9,11},{10,... | collective-permute-start | bytes 786440 | tf_op jit(solution)/shard_map/ppermute | solution.py:315
  62.1 1.9 %all-to-all-done.packet_ref = bf16[16,288,128]{2,1,0:T(8,128)(2,1)S(1)} async-done(((bf16[16,288,128]{2,1,0:T(8,128)(2,1)}), bf16[16,288,128]{2,1,0:T(8,128)(2,1)S(1)}, u32[]{:S(2)}, u32[]{:S(2)}) %all-to-all-start) | async-done | bytes 1179680 | tf_op jit(solution)/shard_map/all_to_all | solution.py:333
  64.0 1.6 %copy-done.3 = bf16[128,8192]{1,0:T(8,128)(2,1)S(1)} copy-done((bf16[128,8192]{1,0:T(8,128)(2,1)S(1)}, bf16[128,8192]{1,0:T(8,128)(2,1)}, u32[]{:S(2)}) %copy-start.3) | copy-done | bytes 2097176
  65.6 1.0 %shard_map.71 = f32[128,1024]{1,0:T(8,128)S(1)} custom-call(bf16[128,8192]{1,0:T(8,128)(2,1)S(1)} %copy-done.3, bf16[16,288,128]{2,1,0:T(8,128)(2,1)S(1)} %all-to-all-done.packet_ref), custom_call_target="tpu_custom_call" | custom-call | flops 2000000000 | bytes 4194304 | tf_op jit(solution)/shard_map/pallas_call | solution.py:157
  66.6 3.4 %collective-permute-done.10 = bf16[128,1024]{1,0:T(8,128)(2,1)S(1)} collective-permute-done((bf16[128,1024]{1,0:T(8,128)(2,1)S(1)}, bf16[128,1024]{1,0:T(8,128)(2,1)S(1)}, u32[]{:S(2)}, u32[]{:S(2)}) %collective-permute-start.10) | collective-permute-done | bytes 262176 | tf_op jit(solution)/shard_map/ppermute | solution.py:315
  70.0 0.8 %select_convert_fusion = bf16[128,1024]{1,0:T(8,128)(2,1)} fusion(f32[128,1024]{1,0:T(8,128)S(1)} %shard_map.71, f32[128,1024]{1,0:T(8,128)S(1)} %get-tuple-element.40, bf16[128,1024]{1,0:T(8,128)(2,1)S(1)} %collective-permute-done.10, pred[128]{0:T(512)(128)(4,1)S(1)} %iota_compare_fusion), kind=kLoop, calls=%fused_computation | loop fusion | flops 655360 | bytes 1572992 | tf_op jit(solution)/shard_map/convert_element_type | solution.py:343
  (15 shorter events, 0.0 us)
Async XLA Ops:
  0.1 1.2 %copy-start = (bf16[512,1024]{1,0:T(8,128)(2,1)S(1)}, bf16[512,1024]{1,0:T(8,128)(2,1)}, u32[]{:S(2)}) copy-start(bf16[512,1024]{1,0:T(8,128)(2,1)} %own_ref.1) | copy-start | bytes 3145732
  1.9 17.9 %collective-permute-start = (bf16[256,1024]{1,0:T(8,128)(2,1)S(1)}, bf16[256,1024]{1,0:T(8,128)(2,1)S(1)}, u32[]{:S(2)}, u32[]{:S(2)}) collective-permute-start(bf16[256,1024]{1,0:T(8,128)(2,1)S(1)} %shard_map.65), channel_id=1, source_target_pairs={{0,4},{1,5},{2,6},{3,7},{4,8},{5,9},{6,10},{7,11},{8,12},{9,13},{1... | collective-permute-start | bytes 1572872 | tf_op jit(solution)/shard_map/ppermute | solution.py:309
  5.0 1.6 %copy-start.2 = (bf16[128,8192]{1,0:T(8,128)(2,1)S(1)}, bf16[128,8192]{1,0:T(8,128)(2,1)}, u32[]{:S(2)}) copy-start(bf16[128,8192]{1,0:T(8,128)(2,1)} %tokens_ref.3) | copy-start | bytes 6291460
  8.3 4.0 %copy-start.4 = (bf16[128,2048]{1,0:T(8,128)(2,1)}, bf16[128,2048]{1,0:T(8,128)(2,1)S(1)}, u32[]{:S(2)}) copy-start(bf16[128,2048]{1,0:T(8,128)(2,1)S(1)} %get-tuple-element.24.s0) | copy-start | bytes 1572868
  8.3 4.1 %copy-start.1 = (bf16[512,1024]{1,0:T(8,128)(2,1)S(1)}, bf16[512,1024]{1,0:T(8,128)(2,1)}, u32[]{:S(2)}) copy-start(bf16[512,1024]{1,0:T(8,128)(2,1)} %own_ref.1) | copy-start | bytes 3145732
  12.3 7.4 %collective-permute-start.1 = (bf16[128,2048]{1,0:T(8,128)(2,1)S(1)}, bf16[128,2048]{1,0:T(8,128)(2,1)S(1)}, u32[]{:S(2)}, u32[]{:S(2)}) collective-permute-start(bf16[128,2048]{1,0:T(8,128)(2,1)S(1)} %get-tuple-element.26), channel_id=1, source_target_pairs={{0,1},{1,0},{2,3},{3,2},{4,5},{5,4},{6,7},{7,6},{8,9},{9,8},{10,11... | collective-permute-start | bytes 1572872 | tf_op jit(solution)/shard_map/ppermute | solution.py:315
  13.0 18.1 %collective-permute-start.4 = (bf16[256,1024]{1,0:T(8,128)(2,1)S(1)}, bf16[256,1024]{1,0:T(8,128)(2,1)}, u32[]{:S(2)}, u32[]{:S(2)}) collective-permute-start(bf16[256,1024]{1,0:T(8,128)(2,1)S(1)} %shard_map.67), channel_id=1, source_target_pairs={{0,4},{1,5},{2,6},{3,7},{4,8},{5,9},{6,10},{7,11},{8,12},{9,13},{1... | collective-permute-start | bytes 1572872 | tf_op jit(solution)/shard_map/ppermute | solution.py:309
  14.6 24.2 %collective-permute-start.3 = (bf16[128,2048]{1,0:T(8,128)(2,1)}, bf16[128,2048]{1,0:T(8,128)(2,1)}, u32[]{:S(2)}, u32[]{:S(2)}) collective-permute-start(bf16[128,2048]{1,0:T(8,128)(2,1)} %get-tuple-element.29), channel_id=1, source_target_pairs={{0,2},{1,3},{2,0},{3,1},{4,6},{5,7},{6,4},{7,5},{8,10},{9,11},{10,... | collective-permute-start | bytes 1572872 | tf_op jit(solution)/shard_map/ppermute | solution.py:315
  19.7 21.7 %collective-permute-start.2 = (bf16[256,1024]{1,0:T(8,128)(2,1)S(1)}, bf16[256,1024]{1,0:T(8,128)(2,1)}, u32[]{:S(2)}, u32[]{:S(2)}) collective-permute-start(bf16[256,1024]{1,0:T(8,128)(2,1)S(1)} %collective-permute-done.refs_0_), channel_id=1, source_target_pairs={{0,4},{1,5},{2,6},{3,7},{4,8},{5,9},{6,10},{7,11},{8,12},{9,13},{1... | collective-permute-start | bytes 1572872 | tf_op jit(solution)/shard_map/ppermute | solution.py:309
  19.8 28.3 %collective-permute-start.6 = (bf16[256,1024]{1,0:T(8,128)(2,1)S(1)}, bf16[256,1024]{1,0:T(8,128)(2,1)}, u32[]{:S(2)}, u32[]{:S(2)}) collective-permute-start(bf16[256,1024]{1,0:T(8,128)(2,1)S(1)} %collective-permute-done.refs_0_), channel_id=1, source_target_pairs={{0,16},{16,0},{1,17},{17,1},{2,18},{18,2},{3,19},{19,3},{4,20},{20... | collective-permute-start | bytes 1572872 | tf_op jit(solution)/shard_map/ppermute | solution.py:312
  31.1 16.9 %collective-permute-start.5 = (bf16[128,2048]{1,0:T(8,128)(2,1)}, bf16[128,2048]{1,0:T(8,128)(2,1)}, u32[]{:S(2)}, u32[]{:S(2)}) collective-permute-start(bf16[128,2048]{1,0:T(8,128)(2,1)} %get-tuple-element.33), channel_id=1, source_target_pairs={{0,3},{1,2},{2,1},{3,0},{4,7},{5,6},{6,5},{7,4},{8,11},{9,10},{10,... | collective-permute-start | bytes 1572872 | tf_op jit(solution)/shard_map/ppermute | solution.py:315
  31.1 16.9 %collective-permute-start.7 = (bf16[256,1024]{1,0:T(8,128)(2,1)}, bf16[256,1024]{1,0:T(8,128)(2,1)}, u32[]{:S(2)}, u32[]{:S(2)}) collective-permute-start(bf16[256,1024]{1,0:T(8,128)(2,1)} %collective-permute-done.4.refs_1_), channel_id=1, source_target_pairs={{0,16},{16,0},{1,17},{17,1},{2,18},{18,2},{3,19},{19,3},{4,20},{20... | collective-permute-start | bytes 1572872 | tf_op jit(solution)/shard_map/ppermute | solution.py:312
  32.1 31.9 %all-to-all-start = ((bf16[16,288,128]{2,1,0:T(8,128)(2,1)}), bf16[16,288,128]{2,1,0:T(8,128)(2,1)S(1)}, u32[]{:S(2)}, u32[]{:S(2)}) async-start(bf16[16,288,128]{2,1,0:T(8,128)(2,1)} %shard_map.66), calls=%async_computation | async-start | bytes 2359296 | tf_op jit(solution)/shard_map/all_to_all | solution.py:333
  41.5 15.1 %collective-permute-start.8 = (bf16[256,1024]{1,0:T(8,128)(2,1)}, bf16[256,1024]{1,0:T(8,128)(2,1)S(1)}, u32[]{:S(2)}, u32[]{:S(2)}) collective-permute-start(bf16[256,1024]{1,0:T(8,128)(2,1)} %collective-permute-done.2.mine_ref), channel_id=1, source_target_pairs={{0,16},{16,0},{1,17},{17,1},{2,18},{18,2},{3,19},{19,3},{4,20},{20... | collective-permute-start | bytes 1572872 | tf_op jit(solution)/shard_map/ppermute | solution.py:312
  48.0 1.0 %copy-start.5 = (bf16[128,2048]{1,0:T(8,128)(2,1)S(1)}, bf16[128,2048]{1,0:T(8,128)(2,1)}, u32[]{:S(2)}) copy-start(bf16[128,2048]{1,0:T(8,128)(2,1)} %copy-done.4) | copy-start | bytes 1572868
  57.0 2.9 %collective-permute-start.9 = (f32[2,128,1024]{2,1,0:T(8,128)S(1)}, f32[2,128,1024]{2,1,0:T(8,128)S(1)}, u32[]{:S(2)}, u32[]{:S(2)}) collective-permute-start(f32[2,128,1024]{2,1,0:T(8,128)S(1)} %get-tuple-element.39), channel_id=1, source_target_pairs={{0,1},{1,0},{2,3},{3,2},{4,5},{5,4},{6,7},{7,6},{8,9},{9,8},{10,11... | collective-permute-start | bytes 3145736 | tf_op jit(solution)/shard_map/ppermute | solution.py:315
  60.1 9.9 %collective-permute-start.10 = (bf16[128,1024]{1,0:T(8,128)(2,1)S(1)}, bf16[128,1024]{1,0:T(8,128)(2,1)S(1)}, u32[]{:S(2)}, u32[]{:S(2)}) collective-permute-start(bf16[128,1024]{1,0:T(8,128)(2,1)S(1)} %get-tuple-element.41), channel_id=1, source_target_pairs={{0,2},{1,3},{2,0},{3,1},{4,6},{5,7},{6,4},{7,5},{8,10},{9,11},{10,... | collective-permute-start | bytes 786440 | tf_op jit(solution)/shard_map/ppermute | solution.py:315
  64.0 1.6 %copy-start.3 = (bf16[128,8192]{1,0:T(8,128)(2,1)S(1)}, bf16[128,8192]{1,0:T(8,128)(2,1)}, u32[]{:S(2)}) copy-start(bf16[128,8192]{1,0:T(8,128)(2,1)} %tokens_ref.3) | copy-start | bytes 6291460

commit v6 on v5

--- a/solution.py
+++ b/solution.py
@@ -239,48 +239,43 @@
     )(where, *shares, own, mine, *pieces)
 
 
-def far_kernel(total_ref, left_ref, other_ref, out_ref, keep_ref):
-    rows = out_ref.shape[1]
+def far_kernel(total_ref, left_ref, other_ref, here_ref, mate_ref, there_ref, past_ref):
+    rows = here_ref.shape[0]
     total = total_ref[...] + jnp.dot(
         left_ref[...], other_ref[...], preferred_element_type=jnp.float32
     )
-    keep_ref[0] = total[:rows]
-    out_ref[0] = total[rows : 2 * rows]
-    keep_ref[1] = total[2 * rows : 3 * rows]
-    out_ref[1] = total[3 * rows :]
+    here_ref[...] = total[:rows]
+    mate_ref[...] = total[rows : 2 * rows]
+    there_ref[...] = total[2 * rows : 3 * rows]
+    past_ref[...] = total[3 * rows :]
 
 
 def far_of(total, left, other):
     rows, columns = total.shape[0] // SQUARE, other.shape[1]
-    result = jax.ShapeDtypeStruct((2, rows, columns), jnp.float32)
+    result = jax.ShapeDtypeStruct((rows, columns), jnp.float32)
     return pl.pallas_call(
         far_kernel,
         in_specs=[VMEM] * 3,
-        out_specs=[VMEM] * 2,
-        out_shape=[result] * 2,
+        out_specs=[VMEM] * SQUARE,
+        out_shape=[result] * SQUARE,
         compiler_params=params(),
         cost_estimate=cost("far", 32 * rows * columns),
     )(total, left, other)
 
 
-def join_kernel(keep_ref, incoming_ref, there_ref, here_ref):
-    there_ref[...] = (keep_ref[1] + incoming_ref[1]).astype(there_ref.dtype)
-    here_ref[...] = keep_ref[0] + incoming_ref[0]
-
-
-def join_of(keep, incoming):
-    rows, columns = keep.shape[1:]
+def join_kernel(there_ref, past_ref, joined_ref):
+    joined_ref[...] = (there_ref[...] + past_ref[...]).astype(joined_ref.dtype)
+
+
+def join_of(there, past):
     return pl.pallas_call(
         join_kernel,
         in_specs=[VMEM] * 2,
-        out_specs=[VMEM] * 2,
-        out_shape=[
-            jax.ShapeDtypeStruct((rows, columns), jnp.bfloat16),
-            jax.ShapeDtypeStruct((rows, columns), jnp.float32),
-        ],
-        compiler_params=params(),
-        cost_estimate=cost("join", 22 * rows * columns),
-    )(keep, incoming)
+        out_specs=VMEM,
+        out_shape=jax.ShapeDtypeStruct(there.shape, jnp.bfloat16),
+        compiler_params=params(),
+        cost_estimate=cost("join", 10 * there.size),
+    )(there, past)
 
 
 def per_device(
@@ -333,10 +328,9 @@
     packets = lax.all_to_all(packets, "dp", 0, 0, tiled=True)
 
     total, left = near_of(where, shares, value_weight_matrix, mine, pieces)
-    outgoing, keep = far_of(total, left, across(mine))
-    incoming = within(outgoing, 1)
-    there, here = join_of(keep, incoming)
-    base = here + within(there, 2).astype(jnp.float32)
+    here, mate, there, past = far_of(total, left, across(mine))
+    joined = within(join_of(there, within(past, 1)), 2)
+    base = here + within(mate, 1) + joined.astype(jnp.float32)
 
     change = change_of(tokens, packets, rank, depth, width)
     live_rows = jnp.arange(BLOCK, dtype=jnp.int32)[None, :] < block_live_length[:, None]

time: 71.2 us -> 71.3 us (level)
    ppermute x5 -> x6, waiting for transfers between devices: 9.77 us -> 8.79 us  [within(): return lax.ppermute(x, 'dp', [(p, p ^ step) for p in range(peer_count)])]
    all_to_all x1, waiting for transfers between devices: 1.94 us -> 2.75 us  [per_device(): packets = lax.all_to_all(packets, 'dp', 0, 0, tiled=True)]
    ppermute x5 -> x6, starting transfers between devices: 4.21 us -> 4.32 us  [within(): return lax.ppermute(x, 'dp', [(p, p ^ step) for p in range(peer_count)])]
  transfers between devices with their start and end apart: 12 -> 13, of which waited for: 8 -> 8; matrix products, arithmetic and copies ran while one was open for 0% -> 0% of each run, Pallas kernels for 17% -> 16%
where the time goes in v6:
time: 71.3 us; the launch traced here: 70.9 us
  waiting for transfers between devices  27.6 us (39%)
  starting transfers between devices  23.8 us (33%)
  Pallas kernels  12.2 us (17%)
  local copies, waits for them, and re-layouts  5.46 us (8%)
  other arithmetic  0.93 us (1%)
  between operations  0.77 us (1%)
    ppermute x3, waiting for transfers between devices, along(): return lax.ppermute(x, ('groups', 'dp'), onward)  12.4 us
    ppermute x6, waiting for transfers between devices, within(): return lax.ppermute(x, 'dp', [(p, p ^ step) for p in range(peer_count)])  8.79 us
    ppermute x3, starting transfers between devices, across(): return lax.ppermute(x, 'groups', [(g, g ^ 1) for g in range(group_count)])  8.1 us
    all_to_all x1, starting transfers between devices, per_device(): packets = lax.all_to_all(packets, 'dp', 0, 0, tiled=True)  6.72 us
    unnamed x12, local copies, waits for them, and re-layouts  5.46 us
    ppermute x3, starting transfers between devices, along(): return lax.ppermute(x, ('groups', 'dp'), onward)  4.71 us
    ppermute x6, starting transfers between devices, within(): return lax.ppermute(x, 'dp', [(p, p ^ step) for p in range(peer_count)])  4.32 us
    pallas_call x1, Pallas kernels, near_of(): pl.pallas_call(near_kernel, in_specs=[SMEM] + [VMEM] * (SQUARE + 2 + len(...  3.94 us
  transfers between devices with their start and end apart: 13, of which 8 were waited for; matrix products, arithmetic and copies ran while one was open for 0% of the time, Pallas kernels for 16%

profile of v6, /device:TPU:0, one launch (start us, length us, event | category | flops | bytes accessed | tf_op | source)
XLA Modules:
  0.0 70.9 jit_solution(16458162918217457378)
XLA Ops:
  0.0 0.1 pad_add_fusion.where_ref
  0.1 1.2 %copy-done = bf16[512,1024]{1,0:T(8,128)(2,1)S(1)} copy-done((bf16[512,1024]{1,0:T(8,128)(2,1)S(1)}, bf16[512,1024]{1,0:T(8,128)(2,1)}, u32[]{:S(2)}) %copy-start) | copy-done | bytes 1048600
  1.3 0.6 shard_map.65
  1.9 3.1 %collective-permute-start = (bf16[256,1024]{1,0:T(8,128)(2,1)S(1)}, bf16[256,1024]{1,0:T(8,128)(2,1)S(1)}, u32[]{:S(2)}, u32[]{:S(2)}) collective-permute-start(bf16[256,1024]{1,0:T(8,128)(2,1)S(1)} %shard_map.65), channel_id=1, source_target_pairs={{0,4},{1,5},{2,6},{3,7},{4,8},{5,9},{6,10},{7,11},{8,12},{9,13},{1... | collective-permute-start | bytes 1572872 | tf_op jit(solution)/shard_map/ppermute | solution.py:304
  5.0 1.6 %copy-done.2 = bf16[128,8192]{1,0:T(8,128)(2,1)S(1)} copy-done((bf16[128,8192]{1,0:T(8,128)(2,1)S(1)}, bf16[128,8192]{1,0:T(8,128)(2,1)}, u32[]{:S(2)}) %copy-start.2) | copy-done | bytes 2097176
  6.6 1.7 %shard_map.64 = (bf16[128,2048]{1,0:T(8,128)(2,1)S(1)}, bf16[128,2048]{1,0:T(8,128)(2,1)S(1)}, bf16[128,2048]{1,0:T(8,128)(2,1)}, bf16[128,2048]{1,0:T(8,128)(2,1)}) custom-call(s32[3]{0:T(128)S(1)} %pad_add_fusion.where_ref, bf16[128,8192]{1,0:T(8,128)(2,1)S(1)} %copy-done.2), custom_call_target="tpu_custom_call" | custom-call | flops 4000000000 | bytes 4194304 | tf_op jit(solution)/shard_map/pallas_call | solution.py:61
  8.3 3.9 %shard_map.66 = bf16[16,288,128]{2,1,0:T(8,128)(2,1)} custom-call(s32[16]{0:T(128)} %chosen_ref.1, bf16[64,64,512]{2,1,0:T(8,128)(2,1)} %down_ref.1, bf16[64,64,64]{2,1,0:T(8,128)(2,1)} %up_ref.1), custom_call_target="tpu_custom_call" | custom-call | bytes 2359296 | tf_op jit(solution)/shard_map/pallas_call | solution.py:117
  12.2 0.1 collective-permute-start.1
  12.3 0.6 shard_map.67
  12.9 1.6 %collective-permute-start.4 = (bf16[256,1024]{1,0:T(8,128)(2,1)S(1)}, bf16[256,1024]{1,0:T(8,128)(2,1)}, u32[]{:S(2)}, u32[]{:S(2)}) collective-permute-start(bf16[256,1024]{1,0:T(8,128)(2,1)S(1)} %shard_map.67), channel_id=1, source_target_pairs={{0,4},{1,5},{2,6},{3,7},{4,8},{5,9},{6,10},{7,11},{8,12},{9,13},{1... | collective-permute-start | bytes 1572872 | tf_op jit(solution)/shard_map/ppermute | solution.py:304
  14.5 1.5 %collective-permute-start.3 = (bf16[128,2048]{1,0:T(8,128)(2,1)}, bf16[128,2048]{1,0:T(8,128)(2,1)}, u32[]{:S(2)}, u32[]{:S(2)}) collective-permute-start(bf16[128,2048]{1,0:T(8,128)(2,1)} %get-tuple-element.29), channel_id=1, source_target_pairs={{0,2},{1,3},{2,0},{3,1},{4,6},{5,7},{6,4},{7,5},{8,10},{9,11},{10,... | collective-permute-start | bytes 1572872 | tf_op jit(solution)/shard_map/ppermute | solution.py:310
  16.0 3.7 %collective-permute-done.refs_0_ = bf16[256,1024]{1,0:T(8,128)(2,1)S(1)} collective-permute-done((bf16[256,1024]{1,0:T(8,128)(2,1)S(1)}, bf16[256,1024]{1,0:T(8,128)(2,1)S(1)}, u32[]{:S(2)}, u32[]{:S(2)}) %collective-permute-start) | collective-permute-done | bytes 524320 | tf_op jit(solution)/shard_map/ppermute | solution.py:304
  19.8 5.3 %collective-permute-start.6 = (bf16[256,1024]{1,0:T(8,128)(2,1)S(1)}, bf16[256,1024]{1,0:T(8,128)(2,1)}, u32[]{:S(2)}, u32[]{:S(2)}) collective-permute-start(bf16[256,1024]{1,0:T(8,128)(2,1)S(1)} %collective-permute-done.refs_0_), channel_id=1, source_target_pairs={{0,16},{16,0},{1,17},{17,1},{2,18},{18,2},{3,19},{19,3},{4,20},{20... | collective-permute-start | bytes 1572872 | tf_op jit(solution)/shard_map/ppermute | solution.py:307
  25.1 6.0 %collective-permute-done.4.refs_1_ = bf16[256,1024]{1,0:T(8,128)(2,1)} collective-permute-done((bf16[256,1024]{1,0:T(8,128)(2,1)S(1)}, bf16[256,1024]{1,0:T(8,128)(2,1)}, u32[]{:S(2)}, u32[]{:S(2)}) %collective-permute-start.4) | collective-permute-done | bytes 524320 | tf_op jit(solution)/shard_map/ppermute | solution.py:304
  31.1 1.0 %collective-permute-start.7 = (bf16[256,1024]{1,0:T(8,128)(2,1)}, bf16[256,1024]{1,0:T(8,128)(2,1)}, u32[]{:S(2)}, u32[]{:S(2)}) collective-permute-start(bf16[256,1024]{1,0:T(8,128)(2,1)} %collective-permute-done.4.refs_1_), channel_id=1, source_target_pairs={{0,16},{16,0},{1,17},{17,1},{2,18},{18,2},{3,19},{19,3},{4,20},{20... | collective-permute-start | bytes 1572872 | tf_op jit(solution)/shard_map/ppermute | solution.py:307
  32.1 6.7 %all-to-all-start = ((bf16[16,288,128]{2,1,0:T(8,128)(2,1)}), bf16[16,288,128]{2,1,0:T(8,128)(2,1)S(1)}, u32[]{:S(2)}, u32[]{:S(2)}) async-start(bf16[16,288,128]{2,1,0:T(8,128)(2,1)} %shard_map.66), calls=%async_computation | async-start | bytes 2359296 | tf_op jit(solution)/shard_map/all_to_all | solution.py:328
  38.8 2.7 %collective-permute-done.2.mine_ref = bf16[256,1024]{1,0:T(8,128)(2,1)} collective-permute-done((bf16[256,1024]{1,0:T(8,128)(2,1)S(1)}, bf16[256,1024]{1,0:T(8,128)(2,1)}, u32[]{:S(2)}, u32[]{:S(2)}) %collective-permute-start.2) | collective-permute-done | bytes 524320 | tf_op jit(solution)/shard_map/ppermute | solution.py:304
  41.5 1.8 %collective-permute-start.8 = (bf16[256,1024]{1,0:T(8,128)(2,1)}, bf16[256,1024]{1,0:T(8,128)(2,1)S(1)}, u32[]{:S(2)}, u32[]{:S(2)}) collective-permute-start(bf16[256,1024]{1,0:T(8,128)(2,1)} %collective-permute-done.2.mine_ref), channel_id=1, source_target_pairs={{0,16},{16,0},{1,17},{17,1},{2,18},{18,2},{3,19},{19,3},{4,20},{20... | collective-permute-start | bytes 1572872 | tf_op jit(solution)/shard_map/ppermute | solution.py:307
  43.3 4.6 %collective-permute-done.5.s3 = bf16[128,2048]{1,0:T(8,128)(2,1)} collective-permute-done((bf16[128,2048]{1,0:T(8,128)(2,1)}, bf16[128,2048]{1,0:T(8,128)(2,1)}, u32[]{:S(2)}, u32[]{:S(2)}) %collective-permute-start.5) | collective-permute-done | bytes 524320 | tf_op jit(solution)/shard_map/ppermute | solution.py:310
  47.9 1.0 %copy-done.5 = bf16[128,2048]{1,0:T(8,128)(2,1)S(1)} copy-done((bf16[128,2048]{1,0:T(8,128)(2,1)S(1)}, bf16[128,2048]{1,0:T(8,128)(2,1)}, u32[]{:S(2)}) %copy-start.5) | copy-done | bytes 524312
  48.9 3.9 %shard_map.68 = (f32[512,1024]{1,0:T(8,128)S(1)}, bf16[512,256]{1,0:T(8,128)(2,1)S(1)}) custom-call(s32[3]{0:T(128)S(1)} %pad_add_fusion.where_ref, bf16[128,2048]{1,0:T(8,128)(2,1)S(1)} %copy-done.5, bf16[128,2048]{1,0:T(8,128)(2,1)S(1)} %collective-permute-done.1.s1, bf16[128,2048]{1,0:T(8,128)(2,1)} %collective-permute-done.3.s2, ...), custom_call_target="tpu_custom_call" | custom-call | flops 16000000000 | bytes 4194304 | tf_op jit(solution)/shard_map/pallas_call | solution.py:228
  52.9 3.7 %collective-permute-done.8.other_ref = bf16[256,1024]{1,0:T(8,128)(2,1)S(1)} collective-permute-done((bf16[256,1024]{1,0:T(8,128)(2,1)}, bf16[256,1024]{1,0:T(8,128)(2,1)S(1)}, u32[]{:S(2)}, u32[]{:S(2)}) %collective-permute-start.8) | collective-permute-done | bytes 524320 | tf_op jit(solution)/shard_map/ppermute | solution.py:307
  56.6 0.4 shard_map.69
  57.0 0.7 collective-permute-start.10
  57.7 0.1 collective-permute-start.9
  58.4 0.8 %collective-permute-done.10.past_ref = f32[128,1024]{1,0:T(8,128)S(1)} collective-permute-done((f32[128,1024]{1,0:T(8,128)S(1)}, f32[128,1024]{1,0:T(8,128)S(1)}, u32[]{:S(2)}, u32[]{:S(2)}) %collective-permute-start.10) | collective-permute-done | bytes 524320 | tf_op jit(solution)/shard_map/ppermute | solution.py:310
  59.3 2.0 %collective-permute-start.11 = (bf16[128,1024]{1,0:T(8,128)(2,1)S(1)}, bf16[128,1024]{1,0:T(8,128)(2,1)S(1)}, u32[]{:S(2)}, u32[]{:S(2)}) collective-permute-start(bf16[128,1024]{1,0:T(8,128)(2,1)S(1)} %shard_map.70), channel_id=1, source_target_pairs={{0,2},{1,3},{2,0},{3,1},{4,6},{5,7},{6,4},{7,5},{8,10},{9,11},{10,... | collective-permute-start | bytes 786440 | tf_op jit(solution)/shard_map/ppermute | solution.py:310
  61.3 2.8 %all-to-all-done.packet_ref = bf16[16,288,128]{2,1,0:T(8,128)(2,1)S(1)} async-done(((bf16[16,288,128]{2,1,0:T(8,128)(2,1)}), bf16[16,288,128]{2,1,0:T(8,128)(2,1)S(1)}, u32[]{:S(2)}, u32[]{:S(2)}) %all-to-all-start) | async-done | bytes 1179680 | tf_op jit(solution)/shard_map/all_to_all | solution.py:328
  64.0 1.6 %copy-done.3 = bf16[128,8192]{1,0:T(8,128)(2,1)S(1)} copy-done((bf16[128,8192]{1,0:T(8,128)(2,1)S(1)}, bf16[128,8192]{1,0:T(8,128)(2,1)}, u32[]{:S(2)}) %copy-start.3) | copy-done | bytes 2097176
  65.6 1.0 %shard_map.71 = f32[128,1024]{1,0:T(8,128)S(1)} custom-call(bf16[128,8192]{1,0:T(8,128)(2,1)S(1)} %copy-done.3, bf16[16,288,128]{2,1,0:T(8,128)(2,1)S(1)} %all-to-all-done.packet_ref), custom_call_target="tpu_custom_call" | custom-call | flops 2000000000 | bytes 4194304 | tf_op jit(solution)/shard_map/pallas_call | solution.py:157
  66.6 3.4 %collective-permute-done.11 = bf16[128,1024]{1,0:T(8,128)(2,1)S(1)} collective-permute-done((bf16[128,1024]{1,0:T(8,128)(2,1)S(1)}, bf16[128,1024]{1,0:T(8,128)(2,1)S(1)}, u32[]{:S(2)}, u32[]{:S(2)}) %collective-permute-start.11) | collective-permute-done | bytes 262176 | tf_op jit(solution)/shard_map/ppermute | solution.py:310
  70.0 0.8 %select_convert_fusion = bf16[128,1024]{1,0:T(8,128)(2,1)} fusion(f32[128,1024]{1,0:T(8,128)S(1)} %shard_map.71, bf16[128,1024]{1,0:T(8,128)(2,1)S(1)} %collective-permute-done.11, f32[128,1024]{1,0:T(8,128)S(1)} %get-tuple-element.38, f32[128,1024]{1,0:T(8,128)S(1)} %collective-permute-done.9, pred[128]{0:T(512)(128)(4,1)S(1)} %iota_compare_fusion), kind=kLoop, calls=%fused_computation | loop fusion | flops 786432 | bytes 2097280 | tf_op jit(solution)/shard_map/convert_element_type | solution.py:337
  (17 shorter events, 0.1 us)
Async XLA Ops:
  0.1 1.2 %copy-start = (bf16[512,1024]{1,0:T(8,128)(2,1)S(1)}, bf16[512,1024]{1,0:T(8,128)(2,1)}, u32[]{:S(2)}) copy-start(bf16[512,1024]{1,0:T(8,128)(2,1)} %own_ref.1) | copy-start | bytes 3145732
  1.9 17.9 %collective-permute-start = (bf16[256,1024]{1,0:T(8,128)(2,1)S(1)}, bf16[256,1024]{1,0:T(8,128)(2,1)S(1)}, u32[]{:S(2)}, u32[]{:S(2)}) collective-permute-start(bf16[256,1024]{1,0:T(8,128)(2,1)S(1)} %shard_map.65), channel_id=1, source_target_pairs={{0,4},{1,5},{2,6},{3,7},{4,8},{5,9},{6,10},{7,11},{8,12},{9,13},{1... | collective-permute-start | bytes 1572872 | tf_op jit(solution)/shard_map/ppermute | solution.py:304
  5.0 1.6 %copy-start.2 = (bf16[128,8192]{1,0:T(8,128)(2,1)S(1)}, bf16[128,8192]{1,0:T(8,128)(2,1)}, u32[]{:S(2)}) copy-start(bf16[128,8192]{1,0:T(8,128)(2,1)} %tokens_ref.3) | copy-start | bytes 6291460
  8.3 3.9 %copy-start.4 = (bf16[128,2048]{1,0:T(8,128)(2,1)}, bf16[128,2048]{1,0:T(8,128)(2,1)S(1)}, u32[]{:S(2)}) copy-start(bf16[128,2048]{1,0:T(8,128)(2,1)S(1)} %get-tuple-element.24.s0) | copy-start | bytes 1572868
  8.3 4.0 %copy-start.1 = (bf16[512,1024]{1,0:T(8,128)(2,1)S(1)}, bf16[512,1024]{1,0:T(8,128)(2,1)}, u32[]{:S(2)}) copy-start(bf16[512,1024]{1,0:T(8,128)(2,1)} %own_ref.1) | copy-start | bytes 3145732
  12.2 7.5 %collective-permute-start.1 = (bf16[128,2048]{1,0:T(8,128)(2,1)S(1)}, bf16[128,2048]{1,0:T(8,128)(2,1)S(1)}, u32[]{:S(2)}, u32[]{:S(2)}) collective-permute-start(bf16[128,2048]{1,0:T(8,128)(2,1)S(1)} %get-tuple-element.26), channel_id=1, source_target_pairs={{0,1},{1,0},{2,3},{3,2},{4,5},{5,4},{6,7},{7,6},{8,9},{9,8},{10,11... | collective-permute-start | bytes 1572872 | tf_op jit(solution)/shard_map/ppermute | solution.py:310
  12.9 18.2 %collective-permute-start.4 = (bf16[256,1024]{1,0:T(8,128)(2,1)S(1)}, bf16[256,1024]{1,0:T(8,128)(2,1)}, u32[]{:S(2)}, u32[]{:S(2)}) collective-permute-start(bf16[256,1024]{1,0:T(8,128)(2,1)S(1)} %shard_map.67), channel_id=1, source_target_pairs={{0,4},{1,5},{2,6},{3,7},{4,8},{5,9},{6,10},{7,11},{8,12},{9,13},{1... | collective-permute-start | bytes 1572872 | tf_op jit(solution)/shard_map/ppermute | solution.py:304
  14.5 24.3 %collective-permute-start.3 = (bf16[128,2048]{1,0:T(8,128)(2,1)}, bf16[128,2048]{1,0:T(8,128)(2,1)}, u32[]{:S(2)}, u32[]{:S(2)}) collective-permute-start(bf16[128,2048]{1,0:T(8,128)(2,1)} %get-tuple-element.29), channel_id=1, source_target_pairs={{0,2},{1,3},{2,0},{3,1},{4,6},{5,7},{6,4},{7,5},{8,10},{9,11},{10,... | collective-permute-start | bytes 1572872 | tf_op jit(solution)/shard_map/ppermute | solution.py:310
  19.7 21.7 %collective-permute-start.2 = (bf16[256,1024]{1,0:T(8,128)(2,1)S(1)}, bf16[256,1024]{1,0:T(8,128)(2,1)}, u32[]{:S(2)}, u32[]{:S(2)}) collective-permute-start(bf16[256,1024]{1,0:T(8,128)(2,1)S(1)} %collective-permute-done.refs_0_), channel_id=1, source_target_pairs={{0,4},{1,5},{2,6},{3,7},{4,8},{5,9},{6,10},{7,11},{8,12},{9,13},{1... | collective-permute-start | bytes 1572872 | tf_op jit(solution)/shard_map/ppermute | solution.py:304
  19.8 28.1 %collective-permute-start.6 = (bf16[256,1024]{1,0:T(8,128)(2,1)S(1)}, bf16[256,1024]{1,0:T(8,128)(2,1)}, u32[]{:S(2)}, u32[]{:S(2)}) collective-permute-start(bf16[256,1024]{1,0:T(8,128)(2,1)S(1)} %collective-permute-done.refs_0_), channel_id=1, source_target_pairs={{0,16},{16,0},{1,17},{17,1},{2,18},{18,2},{3,19},{19,3},{4,20},{20... | collective-permute-start | bytes 1572872 | tf_op jit(solution)/shard_map/ppermute | solution.py:307
  31.1 16.8 %collective-permute-start.5 = (bf16[128,2048]{1,0:T(8,128)(2,1)}, bf16[128,2048]{1,0:T(8,128)(2,1)}, u32[]{:S(2)}, u32[]{:S(2)}) collective-permute-start(bf16[128,2048]{1,0:T(8,128)(2,1)} %get-tuple-element.33), channel_id=1, source_target_pairs={{0,3},{1,2},{2,1},{3,0},{4,7},{5,6},{6,5},{7,4},{8,11},{9,10},{10,... | collective-permute-start | bytes 1572872 | tf_op jit(solution)/shard_map/ppermute | solution.py:310
  31.1 16.8 %collective-permute-start.7 = (bf16[256,1024]{1,0:T(8,128)(2,1)}, bf16[256,1024]{1,0:T(8,128)(2,1)}, u32[]{:S(2)}, u32[]{:S(2)}) collective-permute-start(bf16[256,1024]{1,0:T(8,128)(2,1)} %collective-permute-done.4.refs_1_), channel_id=1, source_target_pairs={{0,16},{16,0},{1,17},{17,1},{2,18},{18,2},{3,19},{19,3},{4,20},{20... | collective-permute-start | bytes 1572872 | tf_op jit(solution)/shard_map/ppermute | solution.py:307
  32.1 32.0 %all-to-all-start = ((bf16[16,288,128]{2,1,0:T(8,128)(2,1)}), bf16[16,288,128]{2,1,0:T(8,128)(2,1)S(1)}, u32[]{:S(2)}, u32[]{:S(2)}) async-start(bf16[16,288,128]{2,1,0:T(8,128)(2,1)} %shard_map.66), calls=%async_computation | async-start | bytes 2359296 | tf_op jit(solution)/shard_map/all_to_all | solution.py:328
  41.5 15.1 %collective-permute-start.8 = (bf16[256,1024]{1,0:T(8,128)(2,1)}, bf16[256,1024]{1,0:T(8,128)(2,1)S(1)}, u32[]{:S(2)}, u32[]{:S(2)}) collective-permute-start(bf16[256,1024]{1,0:T(8,128)(2,1)} %collective-permute-done.2.mine_ref), channel_id=1, source_target_pairs={{0,16},{16,0},{1,17},{17,1},{2,18},{18,2},{3,19},{19,3},{4,20},{20... | collective-permute-start | bytes 1572872 | tf_op jit(solution)/shard_map/ppermute | solution.py:307
  47.9 1.0 %copy-start.5 = (bf16[128,2048]{1,0:T(8,128)(2,1)S(1)}, bf16[128,2048]{1,0:T(8,128)(2,1)}, u32[]{:S(2)}) copy-start(bf16[128,2048]{1,0:T(8,128)(2,1)} %copy-done.4) | copy-start | bytes 1572868
  57.0 2.2 %collective-permute-start.10 = (f32[128,1024]{1,0:T(8,128)S(1)}, f32[128,1024]{1,0:T(8,128)S(1)}, u32[]{:S(2)}, u32[]{:S(2)}) collective-permute-start(f32[128,1024]{1,0:T(8,128)S(1)} %get-tuple-element.41), channel_id=1, source_target_pairs={{0,1},{1,0},{2,3},{3,2},{4,5},{5,4},{6,7},{7,6},{8,9},{9,8},{10,11... | collective-permute-start | bytes 1572872 | tf_op jit(solution)/shard_map/ppermute | solution.py:310
  57.7 9.0 %collective-permute-start.9 = (f32[128,1024]{1,0:T(8,128)S(1)}, f32[128,1024]{1,0:T(8,128)S(1)}, u32[]{:S(2)}, u32[]{:S(2)}) collective-permute-start(f32[128,1024]{1,0:T(8,128)S(1)} %get-tuple-element.39), channel_id=1, source_target_pairs={{0,1},{1,0},{2,3},{3,2},{4,5},{5,4},{6,7},{7,6},{8,9},{9,8},{10,11... | collective-permute-start | bytes 1572872 | tf_op jit(solution)/shard_map/ppermute | solution.py:310
  59.3 10.8 %collective-permute-start.11 = (bf16[128,1024]{1,0:T(8,128)(2,1)S(1)}, bf16[128,1024]{1,0:T(8,128)(2,1)S(1)}, u32[]{:S(2)}, u32[]{:S(2)}) collective-permute-start(bf16[128,1024]{1,0:T(8,128)(2,1)S(1)} %shard_map.70), channel_id=1, source_target_pairs={{0,2},{1,3},{2,0},{3,1},{4,6},{5,7},{6,4},{7,5},{8,10},{9,11},{10,... | collective-permute-start | bytes 786440 | tf_op jit(solution)/shard_map/ppermute | solution.py:310
  64.0 1.6 %copy-start.3 = (bf16[128,8192]{1,0:T(8,128)(2,1)S(1)}, bf16[128,8192]{1,0:T(8,128)(2,1)}, u32[]{:S(2)}) copy-start(bf16[128,8192]{1,0:T(8,128)(2,1)} %tokens_ref.3) | copy-start | bytes 6291460

commit v7 on v5

--- a/solution.py
+++ b/solution.py
@@ -14,8 +14,8 @@
     "share": 4.0,
     "packet": 0.0,
     "near": 16.0,
-    "far": 0.1,
-    "join": 2.0,
+    "far": 2.0,
+    "join": 8.0,
     "change": 2.0,
 }
 LANES = 128
@@ -319,7 +319,7 @@
     packets = packets_of(adapter_of_block, adapter_down_weight, adapter_up_weight)
 
     swapped, crossed, slanted = shares[1:]
-    swapped, packets = after(swapped, packets)
+    crossed, packets = after(crossed, packets)
     swapped, crossed = within(swapped, 1), within(crossed, 2)
     pieces = []
     for hop in range(ring // 2 - 1):
@@ -328,7 +328,9 @@
             held[0], swapped = after(held[0], swapped)
             held[1], slanted, packets = after(held[1], slanted, packets)
         pieces += held + [across(piece) for piece in held]
-    mine, crossed = after(along(held[0]), crossed)
+    mine = along(held[0])
+    if pieces:
+        mine, pieces[-2] = after(mine, pieces[-2])
     shares = [shares[0], swapped, crossed, within(slanted, 3)]
     packets = lax.all_to_all(packets, "dp", 0, 0, tiled=True)
 

time: 71.2 us -> 71.2 us (level)
  transfers between devices with their start and end apart: 12 -> 12, of which waited for: 8 -> 8; matrix products, arithmetic and copies ran while one was open for 0% -> 0% of each run, Pallas kernels for 17% -> 16%
where the time goes in v7:
time: 71.2 us; the launch traced here: 70.8 us
  waiting for transfers between devices  27.8 us (39%)
  starting transfers between devices  23.8 us (33%)
  Pallas kernels  12.1 us (17%)
  local copies, waits for them, and re-layouts  5.46 us (8%)
  other arithmetic  0.88 us (1%)
  between operations  0.74 us (1%)
    ppermute x3, waiting for transfers between devices, along(): return lax.ppermute(x, ('groups', 'dp'), onward)  12.6 us
    ppermute x5, waiting for transfers between devices, within(): return lax.ppermute(x, 'dp', [(p, p ^ step) for p in range(peer_count)])  9.63 us
    ppermute x3, starting transfers between devices, across(): return lax.ppermute(x, 'groups', [(g, g ^ 1) for g in range(group_count)])  8.07 us
    all_to_all x1, starting transfers between devices, per_device(): packets = lax.all_to_all(packets, 'dp', 0, 0, tiled=True)  6.72 us
    unnamed x12, local copies, waits for them, and re-layouts  5.46 us
    ppermute x3, starting transfers between devices, along(): return lax.ppermute(x, ('groups', 'dp'), onward)  4.74 us
    ppermute x5, starting transfers between devices, within(): return lax.ppermute(x, 'dp', [(p, p ^ step) for p in range(peer_count)])  4.23 us
    pallas_call x1, Pallas kernels, near_of(): pl.pallas_call(near_kernel, in_specs=[SMEM] + [VMEM] * (SQUARE + 2 + len(...  3.95 us
  transfers between devices with their start and end apart: 12, of which 8 were waited for; matrix products, arithmetic and copies ran while one was open for 0% of the time, Pallas kernels for 16%

profile of v7, /device:TPU:0, one launch (start us, length us, event | category | flops | bytes accessed | tf_op | source)
XLA Modules:
  0.0 70.8 jit_solution(1501211475150516211)
XLA Ops:
  0.0 0.1 pad_add_fusion.where_ref
  0.1 1.2 %copy-done = bf16[512,1024]{1,0:T(8,128)(2,1)S(1)} copy-done((bf16[512,1024]{1,0:T(8,128)(2,1)S(1)}, bf16[512,1024]{1,0:T(8,128)(2,1)}, u32[]{:S(2)}) %copy-start) | copy-done | bytes 1048600
  1.3 0.6 shard_map.65
  1.9 3.1 %collective-permute-start = (bf16[256,1024]{1,0:T(8,128)(2,1)S(1)}, bf16[256,1024]{1,0:T(8,128)(2,1)S(1)}, u32[]{:S(2)}, u32[]{:S(2)}) collective-permute-start(bf16[256,1024]{1,0:T(8,128)(2,1)S(1)} %shard_map.65), channel_id=1, source_target_pairs={{0,4},{1,5},{2,6},{3,7},{4,8},{5,9},{6,10},{7,11},{8,12},{9,13},{1... | collective-permute-start | bytes 1572872 | tf_op jit(solution)/shard_map/ppermute | solution.py:309
  5.0 1.6 %copy-done.2 = bf16[128,8192]{1,0:T(8,128)(2,1)S(1)} copy-done((bf16[128,8192]{1,0:T(8,128)(2,1)S(1)}, bf16[128,8192]{1,0:T(8,128)(2,1)}, u32[]{:S(2)}) %copy-start.2) | copy-done | bytes 2097176
  6.6 1.7 %shard_map.64 = (bf16[128,2048]{1,0:T(8,128)(2,1)S(1)}, bf16[128,2048]{1,0:T(8,128)(2,1)S(1)}, bf16[128,2048]{1,0:T(8,128)(2,1)}, bf16[128,2048]{1,0:T(8,128)(2,1)}) custom-call(s32[3]{0:T(128)S(1)} %pad_add_fusion.where_ref, bf16[128,8192]{1,0:T(8,128)(2,1)S(1)} %copy-done.2), custom_call_target="tpu_custom_call" | custom-call | flops 4000000000 | bytes 4194304 | tf_op jit(solution)/shard_map/pallas_call | solution.py:61
  8.3 0.6 shard_map.67
  8.9 1.6 %collective-permute-start.3 = (bf16[256,1024]{1,0:T(8,128)(2,1)S(1)}, bf16[256,1024]{1,0:T(8,128)(2,1)}, u32[]{:S(2)}, u32[]{:S(2)}) collective-permute-start(bf16[256,1024]{1,0:T(8,128)(2,1)S(1)} %shard_map.67), channel_id=1, source_target_pairs={{0,4},{1,5},{2,6},{3,7},{4,8},{5,9},{6,10},{7,11},{8,12},{9,13},{1... | collective-permute-start | bytes 1572872 | tf_op jit(solution)/shard_map/ppermute | solution.py:309
  10.5 3.8 %shard_map.66 = bf16[16,288,128]{2,1,0:T(8,128)(2,1)} custom-call(s32[16]{0:T(128)} %chosen_ref.1, bf16[64,64,512]{2,1,0:T(8,128)(2,1)} %down_ref.1, bf16[64,64,64]{2,1,0:T(8,128)(2,1)} %up_ref.1), custom_call_target="tpu_custom_call" | custom-call | bytes 2359296 | tf_op jit(solution)/shard_map/pallas_call | solution.py:117
  14.3 1.6 %collective-permute-start.2 = (bf16[128,2048]{1,0:T(8,128)(2,1)}, bf16[128,2048]{1,0:T(8,128)(2,1)}, u32[]{:S(2)}, u32[]{:S(2)}) collective-permute-start(bf16[128,2048]{1,0:T(8,128)(2,1)} %get-tuple-element.28), channel_id=1, source_target_pairs={{0,2},{1,3},{2,0},{3,1},{4,6},{5,7},{6,4},{7,5},{8,10},{9,11},{10,... | collective-permute-start | bytes 1572872 | tf_op jit(solution)/shard_map/ppermute | solution.py:315
  15.9 3.9 %collective-permute-done.refs_0_ = bf16[256,1024]{1,0:T(8,128)(2,1)S(1)} collective-permute-done((bf16[256,1024]{1,0:T(8,128)(2,1)S(1)}, bf16[256,1024]{1,0:T(8,128)(2,1)S(1)}, u32[]{:S(2)}, u32[]{:S(2)}) %collective-permute-start) | collective-permute-done | bytes 524320 | tf_op jit(solution)/shard_map/ppermute | solution.py:309
  19.8 0.0 collective-permute-start.5
  19.8 5.3 %collective-permute-start.6 = (bf16[256,1024]{1,0:T(8,128)(2,1)S(1)}, bf16[256,1024]{1,0:T(8,128)(2,1)}, u32[]{:S(2)}, u32[]{:S(2)}) collective-permute-start(bf16[256,1024]{1,0:T(8,128)(2,1)S(1)} %collective-permute-done.refs_0_), channel_id=1, source_target_pairs={{0,16},{16,0},{1,17},{17,1},{2,18},{18,2},{3,19},{19,3},{4,20},{20... | collective-permute-start | bytes 1572872 | tf_op jit(solution)/shard_map/ppermute | solution.py:312
  25.1 6.0 %collective-permute-done.3.refs_1_ = bf16[256,1024]{1,0:T(8,128)(2,1)} collective-permute-done((bf16[256,1024]{1,0:T(8,128)(2,1)S(1)}, bf16[256,1024]{1,0:T(8,128)(2,1)}, u32[]{:S(2)}, u32[]{:S(2)}) %collective-permute-start.3) | collective-permute-done | bytes 524320 | tf_op jit(solution)/shard_map/ppermute | solution.py:309
  31.1 1.0 %collective-permute-start.7 = (bf16[256,1024]{1,0:T(8,128)(2,1)}, bf16[256,1024]{1,0:T(8,128)(2,1)}, u32[]{:S(2)}, u32[]{:S(2)}) collective-permute-start(bf16[256,1024]{1,0:T(8,128)(2,1)} %collective-permute-done.3.refs_1_), channel_id=1, source_target_pairs={{0,16},{16,0},{1,17},{17,1},{2,18},{18,2},{3,19},{19,3},{4,20},{20... | collective-permute-start | bytes 1572872 | tf_op jit(solution)/shard_map/ppermute | solution.py:312
  32.1 6.7 %all-to-all-start = ((bf16[16,288,128]{2,1,0:T(8,128)(2,1)}), bf16[16,288,128]{2,1,0:T(8,128)(2,1)S(1)}, u32[]{:S(2)}, u32[]{:S(2)}) async-start(bf16[16,288,128]{2,1,0:T(8,128)(2,1)} %shard_map.66), calls=%async_computation | async-start | bytes 2359296 | tf_op jit(solution)/shard_map/all_to_all | solution.py:335
  38.8 2.7 %collective-permute-done.5.mine_ref = bf16[256,1024]{1,0:T(8,128)(2,1)} collective-permute-done((bf16[256,1024]{1,0:T(8,128)(2,1)S(1)}, bf16[256,1024]{1,0:T(8,128)(2,1)}, u32[]{:S(2)}, u32[]{:S(2)}) %collective-permute-start.5) | collective-permute-done | bytes 524320 | tf_op jit(solution)/shard_map/ppermute | solution.py:309
  41.5 1.8 %collective-permute-start.8 = (bf16[256,1024]{1,0:T(8,128)(2,1)}, bf16[256,1024]{1,0:T(8,128)(2,1)S(1)}, u32[]{:S(2)}, u32[]{:S(2)}) collective-permute-start(bf16[256,1024]{1,0:T(8,128)(2,1)} %collective-permute-done.5.mine_ref), channel_id=1, source_target_pairs={{0,16},{16,0},{1,17},{17,1},{2,18},{18,2},{3,19},{19,3},{4,20},{20... | collective-permute-start | bytes 1572872 | tf_op jit(solution)/shard_map/ppermute | solution.py:312
  43.3 4.6 %collective-permute-done.4.s3 = bf16[128,2048]{1,0:T(8,128)(2,1)} collective-permute-done((bf16[128,2048]{1,0:T(8,128)(2,1)}, bf16[128,2048]{1,0:T(8,128)(2,1)}, u32[]{:S(2)}, u32[]{:S(2)}) %collective-permute-start.4) | collective-permute-done | bytes 524320 | tf_op jit(solution)/shard_map/ppermute | solution.py:315
  47.9 1.0 %copy-done.5 = bf16[128,2048]{1,0:T(8,128)(2,1)S(1)} copy-done((bf16[128,2048]{1,0:T(8,128)(2,1)S(1)}, bf16[128,2048]{1,0:T(8,128)(2,1)}, u32[]{:S(2)}) %copy-start.5) | copy-done | bytes 524312
  48.9 3.9 %shard_map.68 = (f32[512,1024]{1,0:T(8,128)S(1)}, bf16[512,256]{1,0:T(8,128)(2,1)S(1)}) custom-call(s32[3]{0:T(128)S(1)} %pad_add_fusion.where_ref, bf16[128,2048]{1,0:T(8,128)(2,1)S(1)} %copy-done.5, bf16[128,2048]{1,0:T(8,128)(2,1)S(1)} %collective-permute-done.1.s1, bf16[128,2048]{1,0:T(8,128)(2,1)} %collective-permute-done.2.s2, ...), custom_call_target="tpu_custom_call" | custom-call | flops 16000000000 | bytes 4194304 | tf_op jit(solution)/shard_map/pallas_call | solution.py:228
  52.9 3.7 %collective-permute-done.8.other_ref = bf16[256,1024]{1,0:T(8,128)(2,1)S(1)} collective-permute-done((bf16[256,1024]{1,0:T(8,128)(2,1)}, bf16[256,1024]{1,0:T(8,128)(2,1)S(1)}, u32[]{:S(2)}, u32[]{:S(2)}) %collective-permute-start.8) | collective-permute-done | bytes 524320 | tf_op jit(solution)/shard_map/ppermute | solution.py:312
  56.6 0.4 shard_map.69
  57.0 0.6 collective-permute-start.9
  58.3 1.6 %collective-permute-done.9.incoming_ref = f32[2,128,1024]{2,1,0:T(8,128)S(1)} collective-permute-done((f32[2,128,1024]{2,1,0:T(8,128)S(1)}, f32[2,128,1024]{2,1,0:T(8,128)S(1)}, u32[]{:S(2)}, u32[]{:S(2)}) %collective-permute-start.9) | collective-permute-done | bytes 1048608 | tf_op jit(solution)/shard_map/ppermute | solution.py:315
  60.0 0.1 shard_map.70
  60.1 2.0 %collective-permute-start.10 = (bf16[128,1024]{1,0:T(8,128)(2,1)S(1)}, bf16[128,1024]{1,0:T(8,128)(2,1)S(1)}, u32[]{:S(2)}, u32[]{:S(2)}) collective-permute-start(bf16[128,1024]{1,0:T(8,128)(2,1)S(1)} %get-tuple-element.41), channel_id=1, source_target_pairs={{0,2},{1,3},{2,0},{3,1},{4,6},{5,7},{6,4},{7,5},{8,10},{9,11},{10,... | collective-permute-start | bytes 786440 | tf_op jit(solution)/shard_map/ppermute | solution.py:315
  62.1 1.9 %all-to-all-done.packet_ref = bf16[16,288,128]{2,1,0:T(8,128)(2,1)S(1)} async-done(((bf16[16,288,128]{2,1,0:T(8,128)(2,1)}), bf16[16,288,128]{2,1,0:T(8,128)(2,1)S(1)}, u32[]{:S(2)}, u32[]{:S(2)}) %all-to-all-start) | async-done | bytes 1179680 | tf_op jit(solution)/shard_map/all_to_all | solution.py:335
  64.0 1.6 %copy-done.3 = bf16[128,8192]{1,0:T(8,128)(2,1)S(1)} copy-done((bf16[128,8192]{1,0:T(8,128)(2,1)S(1)}, bf16[128,8192]{1,0:T(8,128)(2,1)}, u32[]{:S(2)}) %copy-start.3) | copy-done | bytes 2097176
  65.6 1.0 %shard_map.71 = f32[128,1024]{1,0:T(8,128)S(1)} custom-call(bf16[128,8192]{1,0:T(8,128)(2,1)S(1)} %copy-done.3, bf16[16,288,128]{2,1,0:T(8,128)(2,1)S(1)} %all-to-all-done.packet_ref), custom_call_target="tpu_custom_call" | custom-call | flops 2000000000 | bytes 4194304 | tf_op jit(solution)/shard_map/pallas_call | solution.py:157
  66.6 3.4 %collective-permute-done.10 = bf16[128,1024]{1,0:T(8,128)(2,1)S(1)} collective-permute-done((bf16[128,1024]{1,0:T(8,128)(2,1)S(1)}, bf16[128,1024]{1,0:T(8,128)(2,1)S(1)}, u32[]{:S(2)}, u32[]{:S(2)}) %collective-permute-start.10) | collective-permute-done | bytes 262176 | tf_op jit(solution)/shard_map/ppermute | solution.py:315
  70.0 0.8 %select_convert_fusion = bf16[128,1024]{1,0:T(8,128)(2,1)} fusion(f32[128,1024]{1,0:T(8,128)S(1)} %shard_map.71, f32[128,1024]{1,0:T(8,128)S(1)} %get-tuple-element.40, bf16[128,1024]{1,0:T(8,128)(2,1)S(1)} %collective-permute-done.10, pred[128]{0:T(512)(128)(4,1)S(1)} %iota_compare_fusion), kind=kLoop, calls=%fused_computation | loop fusion | flops 655360 | bytes 1572992 | tf_op jit(solution)/shard_map/convert_element_type | solution.py:345
  (15 shorter events, 0.0 us)
Async XLA Ops:
  0.1 1.2 %copy-start = (bf16[512,1024]{1,0:T(8,128)(2,1)S(1)}, bf16[512,1024]{1,0:T(8,128)(2,1)}, u32[]{:S(2)}) copy-start(bf16[512,1024]{1,0:T(8,128)(2,1)} %own_ref.1) | copy-start | bytes 3145732
  1.9 6.4 %copy-start.1 = (bf16[512,1024]{1,0:T(8,128)(2,1)S(1)}, bf16[512,1024]{1,0:T(8,128)(2,1)}, u32[]{:S(2)}) copy-start(bf16[512,1024]{1,0:T(8,128)(2,1)} %own_ref.1) | copy-start | bytes 3145732
  1.9 17.9 %collective-permute-start = (bf16[256,1024]{1,0:T(8,128)(2,1)S(1)}, bf16[256,1024]{1,0:T(8,128)(2,1)S(1)}, u32[]{:S(2)}, u32[]{:S(2)}) collective-permute-start(bf16[256,1024]{1,0:T(8,128)(2,1)S(1)} %shard_map.65), channel_id=1, source_target_pairs={{0,4},{1,5},{2,6},{3,7},{4,8},{5,9},{6,10},{7,11},{8,12},{9,13},{1... | collective-permute-start | bytes 1572872 | tf_op jit(solution)/shard_map/ppermute | solution.py:309
  5.0 1.6 %copy-start.2 = (bf16[128,8192]{1,0:T(8,128)(2,1)S(1)}, bf16[128,8192]{1,0:T(8,128)(2,1)}, u32[]{:S(2)}) copy-start(bf16[128,8192]{1,0:T(8,128)(2,1)} %tokens_ref.3) | copy-start | bytes 6291460
  8.3 6.0 %copy-start.4 = (bf16[128,2048]{1,0:T(8,128)(2,1)}, bf16[128,2048]{1,0:T(8,128)(2,1)S(1)}, u32[]{:S(2)}) copy-start(bf16[128,2048]{1,0:T(8,128)(2,1)S(1)} %get-tuple-element.24.s0) | copy-start | bytes 1572868
  8.3 11.5 %collective-permute-start.1 = (bf16[128,2048]{1,0:T(8,128)(2,1)S(1)}, bf16[128,2048]{1,0:T(8,128)(2,1)S(1)}, u32[]{:S(2)}, u32[]{:S(2)}) collective-permute-start(bf16[128,2048]{1,0:T(8,128)(2,1)S(1)} %get-tuple-element.25), channel_id=1, source_target_pairs={{0,1},{1,0},{2,3},{3,2},{4,5},{5,4},{6,7},{7,6},{8,9},{9,8},{10,11... | collective-permute-start | bytes 1572872 | tf_op jit(solution)/shard_map/ppermute | solution.py:315
  8.9 22.2 %collective-permute-start.3 = (bf16[256,1024]{1,0:T(8,128)(2,1)S(1)}, bf16[256,1024]{1,0:T(8,128)(2,1)}, u32[]{:S(2)}, u32[]{:S(2)}) collective-permute-start(bf16[256,1024]{1,0:T(8,128)(2,1)S(1)} %shard_map.67), channel_id=1, source_target_pairs={{0,4},{1,5},{2,6},{3,7},{4,8},{5,9},{6,10},{7,11},{8,12},{9,13},{1... | collective-permute-start | bytes 1572872 | tf_op jit(solution)/shard_map/ppermute | solution.py:309
  14.3 29.0 %collective-permute-start.2 = (bf16[128,2048]{1,0:T(8,128)(2,1)}, bf16[128,2048]{1,0:T(8,128)(2,1)}, u32[]{:S(2)}, u32[]{:S(2)}) collective-permute-start(bf16[128,2048]{1,0:T(8,128)(2,1)} %get-tuple-element.28), channel_id=1, source_target_pairs={{0,2},{1,3},{2,0},{3,1},{4,6},{5,7},{6,4},{7,5},{8,10},{9,11},{10,... | collective-permute-start | bytes 1572872 | tf_op jit(solution)/shard_map/ppermute | solution.py:315
  19.8 21.7 %collective-permute-start.5 = (bf16[256,1024]{1,0:T(8,128)(2,1)S(1)}, bf16[256,1024]{1,0:T(8,128)(2,1)}, u32[]{:S(2)}, u32[]{:S(2)}) collective-permute-start(bf16[256,1024]{1,0:T(8,128)(2,1)S(1)} %collective-permute-done.refs_0_), channel_id=1, source_target_pairs={{0,4},{1,5},{2,6},{3,7},{4,8},{5,9},{6,10},{7,11},{8,12},{9,13},{1... | collective-permute-start | bytes 1572872 | tf_op jit(solution)/shard_map/ppermute | solution.py:309
  19.8 21.7 %collective-permute-start.6 = (bf16[256,1024]{1,0:T(8,128)(2,1)S(1)}, bf16[256,1024]{1,0:T(8,128)(2,1)}, u32[]{:S(2)}, u32[]{:S(2)}) collective-permute-start(bf16[256,1024]{1,0:T(8,128)(2,1)S(1)} %collective-permute-done.refs_0_), channel_id=1, source_target_pairs={{0,16},{16,0},{1,17},{17,1},{2,18},{18,2},{3,19},{19,3},{4,20},{20... | collective-permute-start | bytes 1572872 | tf_op jit(solution)/shard_map/ppermute | solution.py:312
  31.1 16.8 %collective-permute-start.4 = (bf16[128,2048]{1,0:T(8,128)(2,1)}, bf16[128,2048]{1,0:T(8,128)(2,1)}, u32[]{:S(2)}, u32[]{:S(2)}) collective-permute-start(bf16[128,2048]{1,0:T(8,128)(2,1)} %get-tuple-element.31), channel_id=1, source_target_pairs={{0,3},{1,2},{2,1},{3,0},{4,7},{5,6},{6,5},{7,4},{8,11},{9,10},{10,... | collective-permute-start | bytes 1572872 | tf_op jit(solution)/shard_map/ppermute | solution.py:315
  31.1 16.8 %collective-permute-start.7 = (bf16[256,1024]{1,0:T(8,128)(2,1)}, bf16[256,1024]{1,0:T(8,128)(2,1)}, u32[]{:S(2)}, u32[]{:S(2)}) collective-permute-start(bf16[256,1024]{1,0:T(8,128)(2,1)} %collective-permute-done.3.refs_1_), channel_id=1, source_target_pairs={{0,16},{16,0},{1,17},{17,1},{2,18},{18,2},{3,19},{19,3},{4,20},{20... | collective-permute-start | bytes 1572872 | tf_op jit(solution)/shard_map/ppermute | solution.py:312
  32.1 31.9 %all-to-all-start = ((bf16[16,288,128]{2,1,0:T(8,128)(2,1)}), bf16[16,288,128]{2,1,0:T(8,128)(2,1)S(1)}, u32[]{:S(2)}, u32[]{:S(2)}) async-start(bf16[16,288,128]{2,1,0:T(8,128)(2,1)} %shard_map.66), calls=%async_computation | async-start | bytes 2359296 | tf_op jit(solution)/shard_map/all_to_all | solution.py:335
  41.5 15.1 %collective-permute-start.8 = (bf16[256,1024]{1,0:T(8,128)(2,1)}, bf16[256,1024]{1,0:T(8,128)(2,1)S(1)}, u32[]{:S(2)}, u32[]{:S(2)}) collective-permute-start(bf16[256,1024]{1,0:T(8,128)(2,1)} %collective-permute-done.5.mine_ref), channel_id=1, source_target_pairs={{0,16},{16,0},{1,17},{17,1},{2,18},{18,2},{3,19},{19,3},{4,20},{20... | collective-permute-start | bytes 1572872 | tf_op jit(solution)/shard_map/ppermute | solution.py:312
  47.9 1.0 %copy-start.5 = (bf16[128,2048]{1,0:T(8,128)(2,1)S(1)}, bf16[128,2048]{1,0:T(8,128)(2,1)}, u32[]{:S(2)}) copy-start(bf16[128,2048]{1,0:T(8,128)(2,1)} %copy-done.4) | copy-start | bytes 1572868
  57.0 2.9 %collective-permute-start.9 = (f32[2,128,1024]{2,1,0:T(8,128)S(1)}, f32[2,128,1024]{2,1,0:T(8,128)S(1)}, u32[]{:S(2)}, u32[]{:S(2)}) collective-permute-start(f32[2,128,1024]{2,1,0:T(8,128)S(1)} %get-tuple-element.39), channel_id=1, source_target_pairs={{0,1},{1,0},{2,3},{3,2},{4,5},{5,4},{6,7},{7,6},{8,9},{9,8},{10,11... | collective-permute-start | bytes 3145736 | tf_op jit(solution)/shard_map/ppermute | solution.py:315
  60.1 9.9 %collective-permute-start.10 = (bf16[128,1024]{1,0:T(8,128)(2,1)S(1)}, bf16[128,1024]{1,0:T(8,128)(2,1)S(1)}, u32[]{:S(2)}, u32[]{:S(2)}) collective-permute-start(bf16[128,1024]{1,0:T(8,128)(2,1)S(1)} %get-tuple-element.41), channel_id=1, source_target_pairs={{0,2},{1,3},{2,0},{3,1},{4,6},{5,7},{6,4},{7,5},{8,10},{9,11},{10,... | collective-permute-start | bytes 786440 | tf_op jit(solution)/shard_map/ppermute | solution.py:315
  64.0 1.6 %copy-start.3 = (bf16[128,8192]{1,0:T(8,128)(2,1)S(1)}, bf16[128,8192]{1,0:T(8,128)(2,1)}, u32[]{:S(2)}) copy-start(bf16[128,8192]{1,0:T(8,128)(2,1)} %tokens_ref.3) | copy-start | bytes 6291460

commit v8 on v7

--- a/solution.py
+++ b/solution.py
@@ -41,17 +41,20 @@
     return pl.CostEstimate(flops=flops, bytes_accessed=touched, transcendentals=0)
 
 
-def share_kernel(ring, depth, where_ref, tokens_ref, *share_refs):
+def starts_of(where_ref, ring, depth, mate):
     place, member, side = where_ref[0], where_ref[1], where_ref[2]
     step = 2 * side - 1
     order = [0]
     for hop in range(1, ring // 2):
         order += [step * hop, -step * hop]
     order.append(ring // 2)
-    for turn, ahead in enumerate(order):
-        source = lax.rem(place + ahead + ring, ring)
-        for mate, share_ref in enumerate(share_refs):
-            start = pl.multiple_of((source * SQUARE + (member ^ mate)) * depth, depth)
+    sources = [lax.rem(place + ahead + ring, ring) for ahead in order]
+    return [pl.multiple_of((s * SQUARE + (member ^ mate)) * depth, depth) for s in sources]
+
+
+def share_kernel(ring, depth, where_ref, tokens_ref, *share_refs):
+    for mate, share_ref in enumerate(share_refs):
+        for turn, start in enumerate(starts_of(where_ref, ring, depth, mate + 1)):
             share_ref[:, turn * depth : (turn + 1) * depth] = tokens_ref[:, pl.ds(start, depth)]
 
 
@@ -61,8 +64,8 @@
     return pl.pallas_call(
         functools.partial(share_kernel, ring, depth),
         in_specs=[SMEM, VMEM],
-        out_specs=[VMEM] * SQUARE,
-        out_shape=[share] * SQUARE,
+        out_specs=[VMEM] * (SQUARE - 1),
+        out_shape=[share] * (SQUARE - 1),
         compiler_params=params(),
         cost_estimate=cost("share", 4 * rows * features),
     )(where, tokens)
@@ -186,10 +189,10 @@
     )(where, whole)
 
 
-def stacked(share_refs, turn, depth):
-    return jnp.concatenate(
-        [share[:, turn * depth : (turn + 1) * depth] for share in share_refs], axis=0
-    )
+def stacked(tokens_ref, start, share_refs, turn, depth):
+    own = tokens_ref[:, pl.ds(start, depth)]
+    others = [share[:, turn * depth : (turn + 1) * depth] for share in share_refs]
+    return jnp.concatenate([own] + others, axis=0)
 
 
 def place_half(weight, side, half_ref):
@@ -197,14 +200,15 @@
     weight[pl.ds(pl.multiple_of(side * half, half), half), :] = half_ref[...]
 
 
-def near_kernel(where_ref, s0, s1, s2, s3, own_ref, mine_ref, *refs):
+def near_kernel(where_ref, tokens_ref, s1, s2, s3, own_ref, mine_ref, *refs):
     pieces, (total_ref, left_ref, weight) = refs[:-3], refs[-3:]
     depth = weight.shape[0]
     half = depth // 2
-    shares = (s0, s1, s2, s3)
+    shares = (s1, s2, s3)
     side = where_ref[2]
+    starts = starts_of(where_ref, s1.shape[1] // depth, depth, 0)
     total_ref[...] = jnp.dot(
-        stacked(shares, 0, depth), own_ref[...], preferred_element_type=jnp.float32
+        stacked(tokens_ref, starts[0], shares, 0, depth), own_ref[...], preferred_element_type=jnp.float32
     )
     turns = len(pieces) // 2
     for turn in range(turns):
@@ -212,9 +216,9 @@
         place_half(weight, first, pieces[2 * turn])
         place_half(weight, 1 - first, pieces[2 * turn + 1])
         total_ref[...] += jnp.dot(
-            stacked(shares, turn + 1, depth), weight[...], preferred_element_type=jnp.float32
+            stacked(tokens_ref, starts[turn + 1], shares, turn + 1, depth), weight[...], preferred_element_type=jnp.float32
         )
-    far = stacked(shares, turns + 1, depth)
+    far = stacked(tokens_ref, starts[-1], shares, turns + 1, depth)
     low, high = far[:, :half], far[:, half:]
     total_ref[...] += jnp.dot(
         jnp.where(side == 0, low, high), mine_ref[...], preferred_element_type=jnp.float32
@@ -222,9 +226,9 @@
     left_ref[...] = jnp.where(side == 0, high, low)
 
 
-def near_of(where, shares, own, mine, pieces):
+def near_of(where, tokens, shares, own, mine, pieces):
     depth, columns = own.shape
-    rows = shares[0].shape[0] * SQUARE
+    rows = tokens.shape[0] * SQUARE
     return pl.pallas_call(
         near_kernel,
         in_specs=[SMEM] + [VMEM] * (SQUARE + 2 + len(pieces)),
@@ -236,7 +240,7 @@
         scratch_shapes=[pltpu.VMEM((depth, columns), own.dtype)],
         compiler_params=params(),
         cost_estimate=cost("near", 8 * rows * columns),
-    )(where, *shares, own, mine, *pieces)
+    )(where, tokens, *shares, own, mine, *pieces)
 
 
 def far_kernel(total_ref, left_ref, other_ref, out_ref, keep_ref):
@@ -318,7 +322,7 @@
     shares = shares_of(where, tokens, ring, depth)
     packets = packets_of(adapter_of_block, adapter_down_weight, adapter_up_weight)
 
-    swapped, crossed, slanted = shares[1:]
+    swapped, crossed, slanted = shares
     crossed, packets = after(crossed, packets)
     swapped, crossed = within(swapped, 1), within(crossed, 2)
     pieces = []
@@ -331,10 +335,10 @@
     mine = along(held[0])
     if pieces:
         mine, pieces[-2] = after(mine, pieces[-2])
-    shares = [shares[0], swapped, crossed, within(slanted, 3)]
+    shares = [swapped, crossed, within(slanted, 3)]
     packets = lax.all_to_all(packets, "dp", 0, 0, tiled=True)
 
-    total, left = near_of(where, shares, value_weight_matrix, mine, pieces)
+    total, left = near_of(where, tokens, shares, value_weight_matrix, mine, pieces)
     outgoing, keep = far_of(total, left, across(mine))
     incoming = within(outgoing, 1)
     there, here = join_of(keep, incoming)

time: 71.2 us -> 71.2 us (level)
    unnamed x12 -> x10, local copies, waits for them, and re-layouts: 5.46 us -> 6.01 us
where the time goes in v8:
time: 71.2 us; the launch traced here: 70.8 us
  waiting for transfers between devices  27.2 us (38%)
  starting transfers between devices  23.8 us (33%)
  Pallas kernels  12.2 us (17%)
  local copies, waits for them, and re-layouts  6.01 us (8%)
  other arithmetic  0.88 us (1%)
  between operations  0.73 us (1%)
    ppermute x3, waiting for transfers between devices, along(): return lax.ppermute(x, ('groups', 'dp'), onward)  12.5 us
    ppermute x5, waiting for transfers between devices, within(): return lax.ppermute(x, 'dp', [(p, p ^ step) for p in range(peer_count)])  9.63 us
    ppermute x3, starting transfers between devices, across(): return lax.ppermute(x, 'groups', [(g, g ^ 1) for g in range(group_count)])  8.07 us
    all_to_all x1, starting transfers between devices, per_device(): packets = lax.all_to_all(packets, 'dp', 0, 0, tiled=True)  6.72 us
    unnamed x10, local copies, waits for them, and re-layouts  6.01 us
    ppermute x3, starting transfers between devices, along(): return lax.ppermute(x, ('groups', 'dp'), onward)  4.74 us
    ppermute x5, starting transfers between devices, within(): return lax.ppermute(x, 'dp', [(p, p ^ step) for p in range(peer_count)])  4.24 us
    pallas_call x1, Pallas kernels, near_of(): pl.pallas_call(near_kernel, in_specs=[SMEM] + [VMEM] * (SQUARE + 2 + len(...  3.95 us
  transfers between devices with their start and end apart: 12, of which 8 were waited for; matrix products, arithmetic and copies ran while one was open for 0% of the time, Pallas kernels for 16%

profile of v8, /device:TPU:0, one launch (start us, length us, event | category | flops | bytes accessed | tf_op | source)
XLA Modules:
  0.0 70.8 jit_solution(662053873588464472)
XLA Ops:
  0.0 0.1 pad_add_fusion.where_ref
  0.1 1.2 %copy-done = bf16[512,1024]{1,0:T(8,128)(2,1)S(1)} copy-done((bf16[512,1024]{1,0:T(8,128)(2,1)S(1)}, bf16[512,1024]{1,0:T(8,128)(2,1)}, u32[]{:S(2)}) %copy-start) | copy-done | bytes 1048600
  1.3 0.6 shard_map.64
  1.9 3.1 %collective-permute-start = (bf16[256,1024]{1,0:T(8,128)(2,1)S(1)}, bf16[256,1024]{1,0:T(8,128)(2,1)S(1)}, u32[]{:S(2)}, u32[]{:S(2)}) collective-permute-start(bf16[256,1024]{1,0:T(8,128)(2,1)S(1)} %shard_map.64), channel_id=1, source_target_pairs={{0,4},{1,5},{2,6},{3,7},{4,8},{5,9},{6,10},{7,11},{8,12},{9,13},{1... | collective-permute-start | bytes 1572872 | tf_op jit(solution)/shard_map/ppermute | solution.py:313
  5.0 1.6 %copy-done.2 = bf16[128,8192]{1,0:T(8,128)(2,1)S(1)} copy-done((bf16[128,8192]{1,0:T(8,128)(2,1)S(1)}, bf16[128,8192]{1,0:T(8,128)(2,1)}, u32[]{:S(2)}) %copy-start.2) | copy-done | bytes 2097176
  6.6 1.7 %shard_map.65 = (bf16[128,2048]{1,0:T(8,128)(2,1)S(1)}, bf16[128,2048]{1,0:T(8,128)(2,1)}, bf16[128,2048]{1,0:T(8,128)(2,1)}) custom-call(s32[3]{0:T(128)S(1)} %pad_add_fusion.where_ref, bf16[128,8192]{1,0:T(8,128)(2,1)S(1)} %copy-done.2), custom_call_target="tpu_custom_call" | custom-call | flops 4000000000 | bytes 4194304 | tf_op jit(solution)/shard_map/pallas_call | solution.py:64
  8.2 0.6 shard_map.67
  8.8 1.6 %collective-permute-start.3 = (bf16[256,1024]{1,0:T(8,128)(2,1)S(1)}, bf16[256,1024]{1,0:T(8,128)(2,1)}, u32[]{:S(2)}, u32[]{:S(2)}) collective-permute-start(bf16[256,1024]{1,0:T(8,128)(2,1)S(1)} %shard_map.67), channel_id=1, source_target_pairs={{0,4},{1,5},{2,6},{3,7},{4,8},{5,9},{6,10},{7,11},{8,12},{9,13},{1... | collective-permute-start | bytes 1572872 | tf_op jit(solution)/shard_map/ppermute | solution.py:313
  10.5 3.9 %shard_map.66 = bf16[16,288,128]{2,1,0:T(8,128)(2,1)} custom-call(s32[16]{0:T(128)} %chosen_ref.1, bf16[64,64,512]{2,1,0:T(8,128)(2,1)} %down_ref.1, bf16[64,64,64]{2,1,0:T(8,128)(2,1)} %up_ref.1), custom_call_target="tpu_custom_call" | custom-call | bytes 2359296 | tf_op jit(solution)/shard_map/pallas_call | solution.py:120
  14.3 1.6 %collective-permute-start.2 = (bf16[128,2048]{1,0:T(8,128)(2,1)}, bf16[128,2048]{1,0:T(8,128)(2,1)}, u32[]{:S(2)}, u32[]{:S(2)}) collective-permute-start(bf16[128,2048]{1,0:T(8,128)(2,1)} %get-tuple-element.26), channel_id=1, source_target_pairs={{0,2},{1,3},{2,0},{3,1},{4,6},{5,7},{6,4},{7,5},{8,10},{9,11},{10,... | collective-permute-start | bytes 1572872 | tf_op jit(solution)/shard_map/ppermute | solution.py:319
  15.9 3.8 %collective-permute-done.refs_0_ = bf16[256,1024]{1,0:T(8,128)(2,1)S(1)} collective-permute-done((bf16[256,1024]{1,0:T(8,128)(2,1)S(1)}, bf16[256,1024]{1,0:T(8,128)(2,1)S(1)}, u32[]{:S(2)}, u32[]{:S(2)}) %collective-permute-start) | collective-permute-done | bytes 524320 | tf_op jit(solution)/shard_map/ppermute | solution.py:313
  19.8 0.0 collective-permute-start.5
  19.8 5.3 %collective-permute-start.6 = (bf16[256,1024]{1,0:T(8,128)(2,1)S(1)}, bf16[256,1024]{1,0:T(8,128)(2,1)}, u32[]{:S(2)}, u32[]{:S(2)}) collective-permute-start(bf16[256,1024]{1,0:T(8,128)(2,1)S(1)} %collective-permute-done.refs_0_), channel_id=1, source_target_pairs={{0,16},{16,0},{1,17},{17,1},{2,18},{18,2},{3,19},{19,3},{4,20},{20... | collective-permute-start | bytes 1572872 | tf_op jit(solution)/shard_map/ppermute | solution.py:316
  25.1 6.0 %collective-permute-done.3.refs_1_ = bf16[256,1024]{1,0:T(8,128)(2,1)} collective-permute-done((bf16[256,1024]{1,0:T(8,128)(2,1)S(1)}, bf16[256,1024]{1,0:T(8,128)(2,1)}, u32[]{:S(2)}, u32[]{:S(2)}) %collective-permute-start.3) | collective-permute-done | bytes 524320 | tf_op jit(solution)/shard_map/ppermute | solution.py:313
  31.1 1.0 %collective-permute-start.7 = (bf16[256,1024]{1,0:T(8,128)(2,1)}, bf16[256,1024]{1,0:T(8,128)(2,1)}, u32[]{:S(2)}, u32[]{:S(2)}) collective-permute-start(bf16[256,1024]{1,0:T(8,128)(2,1)} %collective-permute-done.3.refs_1_), channel_id=1, source_target_pairs={{0,16},{16,0},{1,17},{17,1},{2,18},{18,2},{3,19},{19,3},{4,20},{20... | collective-permute-start | bytes 1572872 | tf_op jit(solution)/shard_map/ppermute | solution.py:316
  32.1 6.7 %all-to-all-start = ((bf16[16,288,128]{2,1,0:T(8,128)(2,1)}), bf16[16,288,128]{2,1,0:T(8,128)(2,1)S(1)}, u32[]{:S(2)}, u32[]{:S(2)}) async-start(bf16[16,288,128]{2,1,0:T(8,128)(2,1)} %shard_map.66), calls=%async_computation | async-start | bytes 2359296 | tf_op jit(solution)/shard_map/all_to_all | solution.py:339
  38.8 2.7 %collective-permute-done.5.mine_ref = bf16[256,1024]{1,0:T(8,128)(2,1)} collective-permute-done((bf16[256,1024]{1,0:T(8,128)(2,1)S(1)}, bf16[256,1024]{1,0:T(8,128)(2,1)}, u32[]{:S(2)}, u32[]{:S(2)}) %collective-permute-start.5) | collective-permute-done | bytes 524320 | tf_op jit(solution)/shard_map/ppermute | solution.py:313
  41.5 1.8 %collective-permute-start.8 = (bf16[256,1024]{1,0:T(8,128)(2,1)}, bf16[256,1024]{1,0:T(8,128)(2,1)S(1)}, u32[]{:S(2)}, u32[]{:S(2)}) collective-permute-start(bf16[256,1024]{1,0:T(8,128)(2,1)} %collective-permute-done.5.mine_ref), channel_id=1, source_target_pairs={{0,16},{16,0},{1,17},{17,1},{2,18},{18,2},{3,19},{19,3},{4,20},{20... | collective-permute-start | bytes 1572872 | tf_op jit(solution)/shard_map/ppermute | solution.py:316
  43.3 4.6 %collective-permute-done.4.s3 = bf16[128,2048]{1,0:T(8,128)(2,1)} collective-permute-done((bf16[128,2048]{1,0:T(8,128)(2,1)}, bf16[128,2048]{1,0:T(8,128)(2,1)}, u32[]{:S(2)}, u32[]{:S(2)}) %collective-permute-start.4) | collective-permute-done | bytes 524320 | tf_op jit(solution)/shard_map/ppermute | solution.py:319
  47.9 1.6 %copy-done.3 = bf16[128,8192]{1,0:T(8,128)(2,1)S(1)} copy-done((bf16[128,8192]{1,0:T(8,128)(2,1)S(1)}, bf16[128,8192]{1,0:T(8,128)(2,1)}, u32[]{:S(2)}) %copy-start.3) | copy-done | bytes 2097176
  49.5 4.0 %shard_map.68 = (f32[512,1024]{1,0:T(8,128)S(1)}, bf16[512,256]{1,0:T(8,128)(2,1)S(1)}) custom-call(s32[3]{0:T(128)S(1)} %pad_add_fusion.where_ref, bf16[128,8192]{1,0:T(8,128)(2,1)S(1)} %copy-done.3, bf16[128,2048]{1,0:T(8,128)(2,1)S(1)} %collective-permute-done.1.s1, bf16[128,2048]{1,0:T(8,128)(2,1)} %collective-permute-done.2.s2, ...), custom_call_target="tpu_custom_call" | custom-call | flops 16000000000 | bytes 4194304 | tf_op jit(solution)/shard_map/pallas_call | solution.py:232
  53.5 3.1 %collective-permute-done.8.other_ref = bf16[256,1024]{1,0:T(8,128)(2,1)S(1)} collective-permute-done((bf16[256,1024]{1,0:T(8,128)(2,1)}, bf16[256,1024]{1,0:T(8,128)(2,1)S(1)}, u32[]{:S(2)}, u32[]{:S(2)}) %collective-permute-start.8) | collective-permute-done | bytes 524320 | tf_op jit(solution)/shard_map/ppermute | solution.py:316
  56.6 0.4 shard_map.69
  57.0 0.6 collective-permute-start.9
  58.3 1.6 %collective-permute-done.9.incoming_ref = f32[2,128,1024]{2,1,0:T(8,128)S(1)} collective-permute-done((f32[2,128,1024]{2,1,0:T(8,128)S(1)}, f32[2,128,1024]{2,1,0:T(8,128)S(1)}, u32[]{:S(2)}, u32[]{:S(2)}) %collective-permute-start.9) | collective-permute-done | bytes 1048608 | tf_op jit(solution)/shard_map/ppermute | solution.py:319
  60.0 0.1 shard_map.70
  60.1 2.0 %collective-permute-start.10 = (bf16[128,1024]{1,0:T(8,128)(2,1)S(1)}, bf16[128,1024]{1,0:T(8,128)(2,1)S(1)}, u32[]{:S(2)}, u32[]{:S(2)}) collective-permute-start(bf16[128,1024]{1,0:T(8,128)(2,1)S(1)} %get-tuple-element.39), channel_id=1, source_target_pairs={{0,2},{1,3},{2,0},{3,1},{4,6},{5,7},{6,4},{7,5},{8,10},{9,11},{10,... | collective-permute-start | bytes 786440 | tf_op jit(solution)/shard_map/ppermute | solution.py:319
  62.1 1.9 %all-to-all-done.packet_ref = bf16[16,288,128]{2,1,0:T(8,128)(2,1)S(1)} async-done(((bf16[16,288,128]{2,1,0:T(8,128)(2,1)}), bf16[16,288,128]{2,1,0:T(8,128)(2,1)S(1)}, u32[]{:S(2)}, u32[]{:S(2)}) %all-to-all-start) | async-done | bytes 1179680 | tf_op jit(solution)/shard_map/all_to_all | solution.py:339
  64.0 1.6 %copy-done.4 = bf16[128,8192]{1,0:T(8,128)(2,1)S(1)} copy-done((bf16[128,8192]{1,0:T(8,128)(2,1)S(1)}, bf16[128,8192]{1,0:T(8,128)(2,1)}, u32[]{:S(2)}) %copy-start.4) | copy-done | bytes 2097176
  65.6 1.0 %shard_map.71 = f32[128,1024]{1,0:T(8,128)S(1)} custom-call(bf16[128,8192]{1,0:T(8,128)(2,1)S(1)} %copy-done.4, bf16[16,288,128]{2,1,0:T(8,128)(2,1)S(1)} %all-to-all-done.packet_ref), custom_call_target="tpu_custom_call" | custom-call | flops 2000000000 | bytes 4194304 | tf_op jit(solution)/shard_map/pallas_call | solution.py:160
  66.6 3.4 %collective-permute-done.10 = bf16[128,1024]{1,0:T(8,128)(2,1)S(1)} collective-permute-done((bf16[128,1024]{1,0:T(8,128)(2,1)S(1)}, bf16[128,1024]{1,0:T(8,128)(2,1)S(1)}, u32[]{:S(2)}, u32[]{:S(2)}) %collective-permute-start.10) | collective-permute-done | bytes 262176 | tf_op jit(solution)/shard_map/ppermute | solution.py:319
  70.0 0.8 %select_convert_fusion = bf16[128,1024]{1,0:T(8,128)(2,1)} fusion(f32[128,1024]{1,0:T(8,128)S(1)} %shard_map.71, f32[128,1024]{1,0:T(8,128)S(1)} %get-tuple-element.38, bf16[128,1024]{1,0:T(8,128)(2,1)S(1)} %collective-permute-done.10, pred[128]{0:T(512)(128)(4,1)S(1)} %iota_compare_fusion), kind=kLoop, calls=%fused_computation | loop fusion | flops 655360 | bytes 1572992 | tf_op jit(solution)/shard_map/convert_element_type | solution.py:349
  (13 shorter events, 0.0 us)
Async XLA Ops:
  0.1 1.2 %copy-start = (bf16[512,1024]{1,0:T(8,128)(2,1)S(1)}, bf16[512,1024]{1,0:T(8,128)(2,1)}, u32[]{:S(2)}) copy-start(bf16[512,1024]{1,0:T(8,128)(2,1)} %own_ref.1) | copy-start | bytes 3145732
  1.9 6.4 %copy-start.1 = (bf16[512,1024]{1,0:T(8,128)(2,1)S(1)}, bf16[512,1024]{1,0:T(8,128)(2,1)}, u32[]{:S(2)}) copy-start(bf16[512,1024]{1,0:T(8,128)(2,1)} %own_ref.1) | copy-start | bytes 3145732
  1.9 17.9 %collective-permute-start = (bf16[256,1024]{1,0:T(8,128)(2,1)S(1)}, bf16[256,1024]{1,0:T(8,128)(2,1)S(1)}, u32[]{:S(2)}, u32[]{:S(2)}) collective-permute-start(bf16[256,1024]{1,0:T(8,128)(2,1)S(1)} %shard_map.64), channel_id=1, source_target_pairs={{0,4},{1,5},{2,6},{3,7},{4,8},{5,9},{6,10},{7,11},{8,12},{9,13},{1... | collective-permute-start | bytes 1572872 | tf_op jit(solution)/shard_map/ppermute | solution.py:313
  5.0 1.6 %copy-start.2 = (bf16[128,8192]{1,0:T(8,128)(2,1)S(1)}, bf16[128,8192]{1,0:T(8,128)(2,1)}, u32[]{:S(2)}) copy-start(bf16[128,8192]{1,0:T(8,128)(2,1)} %tokens_ref.5) | copy-start | bytes 6291460
  8.2 11.5 %collective-permute-start.1 = (bf16[128,2048]{1,0:T(8,128)(2,1)S(1)}, bf16[128,2048]{1,0:T(8,128)(2,1)S(1)}, u32[]{:S(2)}, u32[]{:S(2)}) collective-permute-start(bf16[128,2048]{1,0:T(8,128)(2,1)S(1)} %get-tuple-element.23), channel_id=1, source_target_pairs={{0,1},{1,0},{2,3},{3,2},{4,5},{5,4},{6,7},{7,6},{8,9},{9,8},{10,11... | collective-permute-start | bytes 1572872 | tf_op jit(solution)/shard_map/ppermute | solution.py:319
  8.8 22.3 %collective-permute-start.3 = (bf16[256,1024]{1,0:T(8,128)(2,1)S(1)}, bf16[256,1024]{1,0:T(8,128)(2,1)}, u32[]{:S(2)}, u32[]{:S(2)}) collective-permute-start(bf16[256,1024]{1,0:T(8,128)(2,1)S(1)} %shard_map.67), channel_id=1, source_target_pairs={{0,4},{1,5},{2,6},{3,7},{4,8},{5,9},{6,10},{7,11},{8,12},{9,13},{1... | collective-permute-start | bytes 1572872 | tf_op jit(solution)/shard_map/ppermute | solution.py:313
  14.3 29.0 %collective-permute-start.2 = (bf16[128,2048]{1,0:T(8,128)(2,1)}, bf16[128,2048]{1,0:T(8,128)(2,1)}, u32[]{:S(2)}, u32[]{:S(2)}) collective-permute-start(bf16[128,2048]{1,0:T(8,128)(2,1)} %get-tuple-element.26), channel_id=1, source_target_pairs={{0,2},{1,3},{2,0},{3,1},{4,6},{5,7},{6,4},{7,5},{8,10},{9,11},{10,... | collective-permute-start | bytes 1572872 | tf_op jit(solution)/shard_map/ppermute | solution.py:319
  19.8 21.7 %collective-permute-start.5 = (bf16[256,1024]{1,0:T(8,128)(2,1)S(1)}, bf16[256,1024]{1,0:T(8,128)(2,1)}, u32[]{:S(2)}, u32[]{:S(2)}) collective-permute-start(bf16[256,1024]{1,0:T(8,128)(2,1)S(1)} %collective-permute-done.refs_0_), channel_id=1, source_target_pairs={{0,4},{1,5},{2,6},{3,7},{4,8},{5,9},{6,10},{7,11},{8,12},{9,13},{1... | collective-permute-start | bytes 1572872 | tf_op jit(solution)/shard_map/ppermute | solution.py:313
  19.8 21.7 %collective-permute-start.6 = (bf16[256,1024]{1,0:T(8,128)(2,1)S(1)}, bf16[256,1024]{1,0:T(8,128)(2,1)}, u32[]{:S(2)}, u32[]{:S(2)}) collective-permute-start(bf16[256,1024]{1,0:T(8,128)(2,1)S(1)} %collective-permute-done.refs_0_), channel_id=1, source_target_pairs={{0,16},{16,0},{1,17},{17,1},{2,18},{18,2},{3,19},{19,3},{4,20},{20... | collective-permute-start | bytes 1572872 | tf_op jit(solution)/shard_map/ppermute | solution.py:316
  31.1 16.8 %collective-permute-start.4 = (bf16[128,2048]{1,0:T(8,128)(2,1)}, bf16[128,2048]{1,0:T(8,128)(2,1)}, u32[]{:S(2)}, u32[]{:S(2)}) collective-permute-start(bf16[128,2048]{1,0:T(8,128)(2,1)} %get-tuple-element.29), channel_id=1, source_target_pairs={{0,3},{1,2},{2,1},{3,0},{4,7},{5,6},{6,5},{7,4},{8,11},{9,10},{10,... | collective-permute-start | bytes 1572872 | tf_op jit(solution)/shard_map/ppermute | solution.py:319
  31.1 16.8 %collective-permute-start.7 = (bf16[256,1024]{1,0:T(8,128)(2,1)}, bf16[256,1024]{1,0:T(8,128)(2,1)}, u32[]{:S(2)}, u32[]{:S(2)}) collective-permute-start(bf16[256,1024]{1,0:T(8,128)(2,1)} %collective-permute-done.3.refs_1_), channel_id=1, source_target_pairs={{0,16},{16,0},{1,17},{17,1},{2,18},{18,2},{3,19},{19,3},{4,20},{20... | collective-permute-start | bytes 1572872 | tf_op jit(solution)/shard_map/ppermute | solution.py:316
  32.1 31.9 %all-to-all-start = ((bf16[16,288,128]{2,1,0:T(8,128)(2,1)}), bf16[16,288,128]{2,1,0:T(8,128)(2,1)S(1)}, u32[]{:S(2)}, u32[]{:S(2)}) async-start(bf16[16,288,128]{2,1,0:T(8,128)(2,1)} %shard_map.66), calls=%async_computation | async-start | bytes 2359296 | tf_op jit(solution)/shard_map/all_to_all | solution.py:339
  41.5 15.1 %collective-permute-start.8 = (bf16[256,1024]{1,0:T(8,128)(2,1)}, bf16[256,1024]{1,0:T(8,128)(2,1)S(1)}, u32[]{:S(2)}, u32[]{:S(2)}) collective-permute-start(bf16[256,1024]{1,0:T(8,128)(2,1)} %collective-permute-done.5.mine_ref), channel_id=1, source_target_pairs={{0,16},{16,0},{1,17},{17,1},{2,18},{18,2},{3,19},{19,3},{4,20},{20... | collective-permute-start | bytes 1572872 | tf_op jit(solution)/shard_map/ppermute | solution.py:316
  47.9 1.6 %copy-start.3 = (bf16[128,8192]{1,0:T(8,128)(2,1)S(1)}, bf16[128,8192]{1,0:T(8,128)(2,1)}, u32[]{:S(2)}) copy-start(bf16[128,8192]{1,0:T(8,128)(2,1)} %tokens_ref.5) | copy-start | bytes 6291460
  57.0 2.9 %collective-permute-start.9 = (f32[2,128,1024]{2,1,0:T(8,128)S(1)}, f32[2,128,1024]{2,1,0:T(8,128)S(1)}, u32[]{:S(2)}, u32[]{:S(2)}) collective-permute-start(f32[2,128,1024]{2,1,0:T(8,128)S(1)} %get-tuple-element.37), channel_id=1, source_target_pairs={{0,1},{1,0},{2,3},{3,2},{4,5},{5,4},{6,7},{7,6},{8,9},{9,8},{10,11... | collective-permute-start | bytes 3145736 | tf_op jit(solution)/shard_map/ppermute | solution.py:319
  60.1 9.9 %collective-permute-start.10 = (bf16[128,1024]{1,0:T(8,128)(2,1)S(1)}, bf16[128,1024]{1,0:T(8,128)(2,1)S(1)}, u32[]{:S(2)}, u32[]{:S(2)}) collective-permute-start(bf16[128,1024]{1,0:T(8,128)(2,1)S(1)} %get-tuple-element.39), channel_id=1, source_target_pairs={{0,2},{1,3},{2,0},{3,1},{4,6},{5,7},{6,4},{7,5},{8,10},{9,11},{10,... | collective-permute-start | bytes 786440 | tf_op jit(solution)/shard_map/ppermute | solution.py:319
  64.0 1.6 %copy-start.4 = (bf16[128,8192]{1,0:T(8,128)(2,1)S(1)}, bf16[128,8192]{1,0:T(8,128)(2,1)}, u32[]{:S(2)}) copy-start(bf16[128,8192]{1,0:T(8,128)(2,1)} %tokens_ref.5) | copy-start | bytes 6291460

commit v9 on v7

--- a/solution.py
+++ b/solution.py
@@ -326,7 +326,8 @@
         held = [along(piece) for piece in held]
         if hop == 0:
             held[0], swapped = after(held[0], swapped)
-            held[1], slanted, packets = after(held[1], slanted, packets)
+            held[0], slanted = after(held[0], slanted)
+            held[1], packets = after(held[1], packets)
         pieces += held + [across(piece) for piece in held]
     mine = along(held[0])
     if pieces:

time: 71.2 us -> 71.3 us (level)
  no operation moved by 1% of the time
where the time goes in v9:
time: 71.3 us; the launch traced here: 70.8 us
  waiting for transfers between devices  27.8 us (39%)
  starting transfers between devices  23.8 us (33%)
  Pallas kernels  12.1 us (17%)
  local copies, waits for them, and re-layouts  5.46 us (8%)
  other arithmetic  0.88 us (1%)
  between operations  0.74 us (1%)
    ppermute x3, waiting for transfers between devices, along(): return lax.ppermute(x, ('groups', 'dp'), onward)  12.6 us
    ppermute x5, waiting for transfers between devices, within(): return lax.ppermute(x, 'dp', [(p, p ^ step) for p in range(peer_count)])  9.63 us
    ppermute x3, starting transfers between devices, across(): return lax.ppermute(x, 'groups', [(g, g ^ 1) for g in range(group_count)])  8.07 us
    all_to_all x1, starting transfers between devices, per_device(): packets = lax.all_to_all(packets, 'dp', 0, 0, tiled=True)  6.72 us
    unnamed x12, local copies, waits for them, and re-layouts  5.46 us
    ppermute x3, starting transfers between devices, along(): return lax.ppermute(x, ('groups', 'dp'), onward)  4.74 us
    ppermute x5, starting transfers between devices, within(): return lax.ppermute(x, 'dp', [(p, p ^ step) for p in range(peer_count)])  4.23 us
    pallas_call x1, Pallas kernels, near_of(): pl.pallas_call(near_kernel, in_specs=[SMEM] + [VMEM] * (SQUARE + 2 + len(...  3.95 us
  transfers between devices with their start and end apart: 12, of which 8 were waited for; matrix products, arithmetic and copies ran while one was open for 0% of the time, Pallas kernels for 16%

profile of v9, /device:TPU:0, one launch (start us, length us, event | category | flops | bytes accessed | tf_op | source)
XLA Modules:
  0.0 70.8 jit_solution(16271321283264090848)
XLA Ops:
  0.0 0.1 pad_add_fusion.where_ref
  0.1 1.2 %copy-done = bf16[512,1024]{1,0:T(8,128)(2,1)S(1)} copy-done((bf16[512,1024]{1,0:T(8,128)(2,1)S(1)}, bf16[512,1024]{1,0:T(8,128)(2,1)}, u32[]{:S(2)}) %copy-start) | copy-done | bytes 1048600
  1.3 0.6 shard_map.65
  1.9 3.1 %collective-permute-start = (bf16[256,1024]{1,0:T(8,128)(2,1)S(1)}, bf16[256,1024]{1,0:T(8,128)(2,1)S(1)}, u32[]{:S(2)}, u32[]{:S(2)}) collective-permute-start(bf16[256,1024]{1,0:T(8,128)(2,1)S(1)} %shard_map.65), channel_id=1, source_target_pairs={{0,4},{1,5},{2,6},{3,7},{4,8},{5,9},{6,10},{7,11},{8,12},{9,13},{1... | collective-permute-start | bytes 1572872 | tf_op jit(solution)/shard_map/ppermute | solution.py:309
  5.0 1.6 %copy-done.2 = bf16[128,8192]{1,0:T(8,128)(2,1)S(1)} copy-done((bf16[128,8192]{1,0:T(8,128)(2,1)S(1)}, bf16[128,8192]{1,0:T(8,128)(2,1)}, u32[]{:S(2)}) %copy-start.2) | copy-done | bytes 2097176
  6.6 1.7 %shard_map.64 = (bf16[128,2048]{1,0:T(8,128)(2,1)S(1)}, bf16[128,2048]{1,0:T(8,128)(2,1)S(1)}, bf16[128,2048]{1,0:T(8,128)(2,1)}, bf16[128,2048]{1,0:T(8,128)(2,1)}) custom-call(s32[3]{0:T(128)S(1)} %pad_add_fusion.where_ref, bf16[128,8192]{1,0:T(8,128)(2,1)S(1)} %copy-done.2), custom_call_target="tpu_custom_call" | custom-call | flops 4000000000 | bytes 4194304 | tf_op jit(solution)/shard_map/pallas_call | solution.py:61
  8.3 0.6 shard_map.67
  8.9 1.6 %collective-permute-start.6 = (bf16[256,1024]{1,0:T(8,128)(2,1)S(1)}, bf16[256,1024]{1,0:T(8,128)(2,1)}, u32[]{:S(2)}, u32[]{:S(2)}) collective-permute-start(bf16[256,1024]{1,0:T(8,128)(2,1)S(1)} %shard_map.67), channel_id=1, source_target_pairs={{0,4},{1,5},{2,6},{3,7},{4,8},{5,9},{6,10},{7,11},{8,12},{9,13},{1... | collective-permute-start | bytes 1572872 | tf_op jit(solution)/shard_map/ppermute | solution.py:309
  10.5 3.8 %shard_map.66 = bf16[16,288,128]{2,1,0:T(8,128)(2,1)} custom-call(s32[16]{0:T(128)} %chosen_ref.1, bf16[64,64,512]{2,1,0:T(8,128)(2,1)} %down_ref.1, bf16[64,64,64]{2,1,0:T(8,128)(2,1)} %up_ref.1), custom_call_target="tpu_custom_call" | custom-call | bytes 2359296 | tf_op jit(solution)/shard_map/pallas_call | solution.py:117
  14.3 1.6 %collective-permute-start.2 = (bf16[128,2048]{1,0:T(8,128)(2,1)}, bf16[128,2048]{1,0:T(8,128)(2,1)}, u32[]{:S(2)}, u32[]{:S(2)}) collective-permute-start(bf16[128,2048]{1,0:T(8,128)(2,1)} %get-tuple-element.29), channel_id=1, source_target_pairs={{0,2},{1,3},{2,0},{3,1},{4,6},{5,7},{6,4},{7,5},{8,10},{9,11},{10,... | collective-permute-start | bytes 1572872 | tf_op jit(solution)/shard_map/ppermute | solution.py:315
  15.9 3.9 %collective-permute-done.refs_0_ = bf16[256,1024]{1,0:T(8,128)(2,1)S(1)} collective-permute-done((bf16[256,1024]{1,0:T(8,128)(2,1)S(1)}, bf16[256,1024]{1,0:T(8,128)(2,1)S(1)}, u32[]{:S(2)}, u32[]{:S(2)}) %collective-permute-start) | collective-permute-done | bytes 524320 | tf_op jit(solution)/shard_map/ppermute | solution.py:309
  19.8 0.0 collective-permute-start.4
  19.8 5.3 %collective-permute-start.5 = (bf16[256,1024]{1,0:T(8,128)(2,1)S(1)}, bf16[256,1024]{1,0:T(8,128)(2,1)}, u32[]{:S(2)}, u32[]{:S(2)}) collective-permute-start(bf16[256,1024]{1,0:T(8,128)(2,1)S(1)} %collective-permute-done.refs_0_), channel_id=1, source_target_pairs={{0,16},{16,0},{1,17},{17,1},{2,18},{18,2},{3,19},{19,3},{4,20},{20... | collective-permute-start | bytes 1572872 | tf_op jit(solution)/shard_map/ppermute | solution.py:312
  25.1 6.0 %collective-permute-done.6.refs_1_ = bf16[256,1024]{1,0:T(8,128)(2,1)} collective-permute-done((bf16[256,1024]{1,0:T(8,128)(2,1)S(1)}, bf16[256,1024]{1,0:T(8,128)(2,1)}, u32[]{:S(2)}, u32[]{:S(2)}) %collective-permute-start.6) | collective-permute-done | bytes 524320 | tf_op jit(solution)/shard_map/ppermute | solution.py:309
  31.1 1.0 %collective-permute-start.7 = (bf16[256,1024]{1,0:T(8,128)(2,1)}, bf16[256,1024]{1,0:T(8,128)(2,1)}, u32[]{:S(2)}, u32[]{:S(2)}) collective-permute-start(bf16[256,1024]{1,0:T(8,128)(2,1)} %collective-permute-done.6.refs_1_), channel_id=1, source_target_pairs={{0,16},{16,0},{1,17},{17,1},{2,18},{18,2},{3,19},{19,3},{4,20},{20... | collective-permute-start | bytes 1572872 | tf_op jit(solution)/shard_map/ppermute | solution.py:312
  32.1 6.7 %all-to-all-start = ((bf16[16,288,128]{2,1,0:T(8,128)(2,1)}), bf16[16,288,128]{2,1,0:T(8,128)(2,1)S(1)}, u32[]{:S(2)}, u32[]{:S(2)}) async-start(bf16[16,288,128]{2,1,0:T(8,128)(2,1)} %shard_map.66), calls=%async_computation | async-start | bytes 2359296 | tf_op jit(solution)/shard_map/all_to_all | solution.py:336
  38.8 2.7 %collective-permute-done.4.mine_ref = bf16[256,1024]{1,0:T(8,128)(2,1)} collective-permute-done((bf16[256,1024]{1,0:T(8,128)(2,1)S(1)}, bf16[256,1024]{1,0:T(8,128)(2,1)}, u32[]{:S(2)}, u32[]{:S(2)}) %collective-permute-start.4) | collective-permute-done | bytes 524320 | tf_op jit(solution)/shard_map/ppermute | solution.py:309
  41.5 1.8 %collective-permute-start.8 = (bf16[256,1024]{1,0:T(8,128)(2,1)}, bf16[256,1024]{1,0:T(8,128)(2,1)S(1)}, u32[]{:S(2)}, u32[]{:S(2)}) collective-permute-start(bf16[256,1024]{1,0:T(8,128)(2,1)} %collective-permute-done.4.mine_ref), channel_id=1, source_target_pairs={{0,16},{16,0},{1,17},{17,1},{2,18},{18,2},{3,19},{19,3},{4,20},{20... | collective-permute-start | bytes 1572872 | tf_op jit(solution)/shard_map/ppermute | solution.py:312
  43.3 4.6 %collective-permute-done.3.s3 = bf16[128,2048]{1,0:T(8,128)(2,1)} collective-permute-done((bf16[128,2048]{1,0:T(8,128)(2,1)}, bf16[128,2048]{1,0:T(8,128)(2,1)}, u32[]{:S(2)}, u32[]{:S(2)}) %collective-permute-start.3) | collective-permute-done | bytes 524320 | tf_op jit(solution)/shard_map/ppermute | solution.py:315
  47.9 1.0 %copy-done.5 = bf16[128,2048]{1,0:T(8,128)(2,1)S(1)} copy-done((bf16[128,2048]{1,0:T(8,128)(2,1)S(1)}, bf16[128,2048]{1,0:T(8,128)(2,1)}, u32[]{:S(2)}) %copy-start.5) | copy-done | bytes 524312
  48.9 3.9 %shard_map.68 = (f32[512,1024]{1,0:T(8,128)S(1)}, bf16[512,256]{1,0:T(8,128)(2,1)S(1)}) custom-call(s32[3]{0:T(128)S(1)} %pad_add_fusion.where_ref, bf16[128,2048]{1,0:T(8,128)(2,1)S(1)} %copy-done.5, bf16[128,2048]{1,0:T(8,128)(2,1)S(1)} %collective-permute-done.1.s1, bf16[128,2048]{1,0:T(8,128)(2,1)} %collective-permute-done.2.s2, ...), custom_call_target="tpu_custom_call" | custom-call | flops 16000000000 | bytes 4194304 | tf_op jit(solution)/shard_map/pallas_call | solution.py:228
  52.9 3.7 %collective-permute-done.8.other_ref = bf16[256,1024]{1,0:T(8,128)(2,1)S(1)} collective-permute-done((bf16[256,1024]{1,0:T(8,128)(2,1)}, bf16[256,1024]{1,0:T(8,128)(2,1)S(1)}, u32[]{:S(2)}, u32[]{:S(2)}) %collective-permute-start.8) | collective-permute-done | bytes 524320 | tf_op jit(solution)/shard_map/ppermute | solution.py:312
  56.6 0.4 shard_map.69
  57.0 0.6 collective-permute-start.9
  58.3 1.6 %collective-permute-done.9.incoming_ref = f32[2,128,1024]{2,1,0:T(8,128)S(1)} collective-permute-done((f32[2,128,1024]{2,1,0:T(8,128)S(1)}, f32[2,128,1024]{2,1,0:T(8,128)S(1)}, u32[]{:S(2)}, u32[]{:S(2)}) %collective-permute-start.9) | collective-permute-done | bytes 1048608 | tf_op jit(solution)/shard_map/ppermute | solution.py:315
  60.0 0.1 shard_map.70
  60.1 2.0 %collective-permute-start.10 = (bf16[128,1024]{1,0:T(8,128)(2,1)S(1)}, bf16[128,1024]{1,0:T(8,128)(2,1)S(1)}, u32[]{:S(2)}, u32[]{:S(2)}) collective-permute-start(bf16[128,1024]{1,0:T(8,128)(2,1)S(1)} %get-tuple-element.43), channel_id=1, source_target_pairs={{0,2},{1,3},{2,0},{3,1},{4,6},{5,7},{6,4},{7,5},{8,10},{9,11},{10,... | collective-permute-start | bytes 786440 | tf_op jit(solution)/shard_map/ppermute | solution.py:315
  62.1 1.9 %all-to-all-done.packet_ref = bf16[16,288,128]{2,1,0:T(8,128)(2,1)S(1)} async-done(((bf16[16,288,128]{2,1,0:T(8,128)(2,1)}), bf16[16,288,128]{2,1,0:T(8,128)(2,1)S(1)}, u32[]{:S(2)}, u32[]{:S(2)}) %all-to-all-start) | async-done | bytes 1179680 | tf_op jit(solution)/shard_map/all_to_all | solution.py:336
  64.0 1.6 %copy-done.3 = bf16[128,8192]{1,0:T(8,128)(2,1)S(1)} copy-done((bf16[128,8192]{1,0:T(8,128)(2,1)S(1)}, bf16[128,8192]{1,0:T(8,128)(2,1)}, u32[]{:S(2)}) %copy-start.3) | copy-done | bytes 2097176
  65.6 1.0 %shard_map.71 = f32[128,1024]{1,0:T(8,128)S(1)} custom-call(bf16[128,8192]{1,0:T(8,128)(2,1)S(1)} %copy-done.3, bf16[16,288,128]{2,1,0:T(8,128)(2,1)S(1)} %all-to-all-done.packet_ref), custom_call_target="tpu_custom_call" | custom-call | flops 2000000000 | bytes 4194304 | tf_op jit(solution)/shard_map/pallas_call | solution.py:157
  66.6 3.4 %collective-permute-done.10 = bf16[128,1024]{1,0:T(8,128)(2,1)S(1)} collective-permute-done((bf16[128,1024]{1,0:T(8,128)(2,1)S(1)}, bf16[128,1024]{1,0:T(8,128)(2,1)S(1)}, u32[]{:S(2)}, u32[]{:S(2)}) %collective-permute-start.10) | collective-permute-done | bytes 262176 | tf_op jit(solution)/shard_map/ppermute | solution.py:315
  70.0 0.8 %select_convert_fusion = bf16[128,1024]{1,0:T(8,128)(2,1)} fusion(f32[128,1024]{1,0:T(8,128)S(1)} %shard_map.71, f32[128,1024]{1,0:T(8,128)S(1)} %get-tuple-element.42, bf16[128,1024]{1,0:T(8,128)(2,1)S(1)} %collective-permute-done.10, pred[128]{0:T(512)(128)(4,1)S(1)} %iota_compare_fusion), kind=kLoop, calls=%fused_computation | loop fusion | flops 655360 | bytes 1572992 | tf_op jit(solution)/shard_map/convert_element_type | solution.py:346
  (15 shorter events, 0.0 us)
Async XLA Ops:
  0.1 1.2 %copy-start = (bf16[512,1024]{1,0:T(8,128)(2,1)S(1)}, bf16[512,1024]{1,0:T(8,128)(2,1)}, u32[]{:S(2)}) copy-start(bf16[512,1024]{1,0:T(8,128)(2,1)} %own_ref.1) | copy-start | bytes 3145732
  1.9 6.4 %copy-start.1 = (bf16[512,1024]{1,0:T(8,128)(2,1)S(1)}, bf16[512,1024]{1,0:T(8,128)(2,1)}, u32[]{:S(2)}) copy-start(bf16[512,1024]{1,0:T(8,128)(2,1)} %own_ref.1) | copy-start | bytes 3145732
  1.9 17.9 %collective-permute-start = (bf16[256,1024]{1,0:T(8,128)(2,1)S(1)}, bf16[256,1024]{1,0:T(8,128)(2,1)S(1)}, u32[]{:S(2)}, u32[]{:S(2)}) collective-permute-start(bf16[256,1024]{1,0:T(8,128)(2,1)S(1)} %shard_map.65), channel_id=1, source_target_pairs={{0,4},{1,5},{2,6},{3,7},{4,8},{5,9},{6,10},{7,11},{8,12},{9,13},{1... | collective-permute-start | bytes 1572872 | tf_op jit(solution)/shard_map/ppermute | solution.py:309
  5.0 1.6 %copy-start.2 = (bf16[128,8192]{1,0:T(8,128)(2,1)S(1)}, bf16[128,8192]{1,0:T(8,128)(2,1)}, u32[]{:S(2)}) copy-start(bf16[128,8192]{1,0:T(8,128)(2,1)} %tokens_ref.3) | copy-start | bytes 6291460
  8.3 6.0 %copy-start.4 = (bf16[128,2048]{1,0:T(8,128)(2,1)}, bf16[128,2048]{1,0:T(8,128)(2,1)S(1)}, u32[]{:S(2)}) copy-start(bf16[128,2048]{1,0:T(8,128)(2,1)S(1)} %get-tuple-element.25.s0) | copy-start | bytes 1572868
  8.3 11.5 %collective-permute-start.1 = (bf16[128,2048]{1,0:T(8,128)(2,1)S(1)}, bf16[128,2048]{1,0:T(8,128)(2,1)S(1)}, u32[]{:S(2)}, u32[]{:S(2)}) collective-permute-start(bf16[128,2048]{1,0:T(8,128)(2,1)S(1)} %get-tuple-element.26), channel_id=1, source_target_pairs={{0,1},{1,0},{2,3},{3,2},{4,5},{5,4},{6,7},{7,6},{8,9},{9,8},{10,11... | collective-permute-start | bytes 1572872 | tf_op jit(solution)/shard_map/ppermute | solution.py:315
  8.9 22.2 %collective-permute-start.6 = (bf16[256,1024]{1,0:T(8,128)(2,1)S(1)}, bf16[256,1024]{1,0:T(8,128)(2,1)}, u32[]{:S(2)}, u32[]{:S(2)}) collective-permute-start(bf16[256,1024]{1,0:T(8,128)(2,1)S(1)} %shard_map.67), channel_id=1, source_target_pairs={{0,4},{1,5},{2,6},{3,7},{4,8},{5,9},{6,10},{7,11},{8,12},{9,13},{1... | collective-permute-start | bytes 1572872 | tf_op jit(solution)/shard_map/ppermute | solution.py:309
  14.3 29.0 %collective-permute-start.2 = (bf16[128,2048]{1,0:T(8,128)(2,1)}, bf16[128,2048]{1,0:T(8,128)(2,1)}, u32[]{:S(2)}, u32[]{:S(2)}) collective-permute-start(bf16[128,2048]{1,0:T(8,128)(2,1)} %get-tuple-element.29), channel_id=1, source_target_pairs={{0,2},{1,3},{2,0},{3,1},{4,6},{5,7},{6,4},{7,5},{8,10},{9,11},{10,... | collective-permute-start | bytes 1572872 | tf_op jit(solution)/shard_map/ppermute | solution.py:315
  19.8 21.7 %collective-permute-start.4 = (bf16[256,1024]{1,0:T(8,128)(2,1)S(1)}, bf16[256,1024]{1,0:T(8,128)(2,1)}, u32[]{:S(2)}, u32[]{:S(2)}) collective-permute-start(bf16[256,1024]{1,0:T(8,128)(2,1)S(1)} %collective-permute-done.refs_0_), channel_id=1, source_target_pairs={{0,4},{1,5},{2,6},{3,7},{4,8},{5,9},{6,10},{7,11},{8,12},{9,13},{1... | collective-permute-start | bytes 1572872 | tf_op jit(solution)/shard_map/ppermute | solution.py:309
  19.8 21.7 %collective-permute-start.5 = (bf16[256,1024]{1,0:T(8,128)(2,1)S(1)}, bf16[256,1024]{1,0:T(8,128)(2,1)}, u32[]{:S(2)}, u32[]{:S(2)}) collective-permute-start(bf16[256,1024]{1,0:T(8,128)(2,1)S(1)} %collective-permute-done.refs_0_), channel_id=1, source_target_pairs={{0,16},{16,0},{1,17},{17,1},{2,18},{18,2},{3,19},{19,3},{4,20},{20... | collective-permute-start | bytes 1572872 | tf_op jit(solution)/shard_map/ppermute | solution.py:312
  31.1 16.8 %collective-permute-start.3 = (bf16[128,2048]{1,0:T(8,128)(2,1)}, bf16[128,2048]{1,0:T(8,128)(2,1)}, u32[]{:S(2)}, u32[]{:S(2)}) collective-permute-start(bf16[128,2048]{1,0:T(8,128)(2,1)} %get-tuple-element.32), channel_id=1, source_target_pairs={{0,3},{1,2},{2,1},{3,0},{4,7},{5,6},{6,5},{7,4},{8,11},{9,10},{10,... | collective-permute-start | bytes 1572872 | tf_op jit(solution)/shard_map/ppermute | solution.py:315
  31.1 16.8 %collective-permute-start.7 = (bf16[256,1024]{1,0:T(8,128)(2,1)}, bf16[256,1024]{1,0:T(8,128)(2,1)}, u32[]{:S(2)}, u32[]{:S(2)}) collective-permute-start(bf16[256,1024]{1,0:T(8,128)(2,1)} %collective-permute-done.6.refs_1_), channel_id=1, source_target_pairs={{0,16},{16,0},{1,17},{17,1},{2,18},{18,2},{3,19},{19,3},{4,20},{20... | collective-permute-start | bytes 1572872 | tf_op jit(solution)/shard_map/ppermute | solution.py:312
  32.1 31.9 %all-to-all-start = ((bf16[16,288,128]{2,1,0:T(8,128)(2,1)}), bf16[16,288,128]{2,1,0:T(8,128)(2,1)S(1)}, u32[]{:S(2)}, u32[]{:S(2)}) async-start(bf16[16,288,128]{2,1,0:T(8,128)(2,1)} %shard_map.66), calls=%async_computation | async-start | bytes 2359296 | tf_op jit(solution)/shard_map/all_to_all | solution.py:336
  41.5 15.1 %collective-permute-start.8 = (bf16[256,1024]{1,0:T(8,128)(2,1)}, bf16[256,1024]{1,0:T(8,128)(2,1)S(1)}, u32[]{:S(2)}, u32[]{:S(2)}) collective-permute-start(bf16[256,1024]{1,0:T(8,128)(2,1)} %collective-permute-done.4.mine_ref), channel_id=1, source_target_pairs={{0,16},{16,0},{1,17},{17,1},{2,18},{18,2},{3,19},{19,3},{4,20},{20... | collective-permute-start | bytes 1572872 | tf_op jit(solution)/shard_map/ppermute | solution.py:312
  47.9 1.0 %copy-start.5 = (bf16[128,2048]{1,0:T(8,128)(2,1)S(1)}, bf16[128,2048]{1,0:T(8,128)(2,1)}, u32[]{:S(2)}) copy-start(bf16[128,2048]{1,0:T(8,128)(2,1)} %copy-done.4) | copy-start | bytes 1572868
  57.0 2.9 %collective-permute-start.9 = (f32[2,128,1024]{2,1,0:T(8,128)S(1)}, f32[2,128,1024]{2,1,0:T(8,128)S(1)}, u32[]{:S(2)}, u32[]{:S(2)}) collective-permute-start(f32[2,128,1024]{2,1,0:T(8,128)S(1)} %get-tuple-element.41), channel_id=1, source_target_pairs={{0,1},{1,0},{2,3},{3,2},{4,5},{5,4},{6,7},{7,6},{8,9},{9,8},{10,11... | collective-permute-start | bytes 3145736 | tf_op jit(solution)/shard_map/ppermute | solution.py:315
  60.1 9.9 %collective-permute-start.10 = (bf16[128,1024]{1,0:T(8,128)(2,1)S(1)}, bf16[128,1024]{1,0:T(8,128)(2,1)S(1)}, u32[]{:S(2)}, u32[]{:S(2)}) collective-permute-start(bf16[128,1024]{1,0:T(8,128)(2,1)S(1)} %get-tuple-element.43), channel_id=1, source_target_pairs={{0,2},{1,3},{2,0},{3,1},{4,6},{5,7},{6,4},{7,5},{8,10},{9,11},{10,... | collective-permute-start | bytes 786440 | tf_op jit(solution)/shard_map/ppermute | solution.py:315
  64.0 1.6 %copy-start.3 = (bf16[128,8192]{1,0:T(8,128)(2,1)S(1)}, bf16[128,8192]{1,0:T(8,128)(2,1)}, u32[]{:S(2)}) copy-start(bf16[128,8192]{1,0:T(8,128)(2,1)} %tokens_ref.3) | copy-start | bytes 6291460
